TPU v7x, 32 devices: a whole 2x2x4 slice. The times are simulated.
32 devices in a mesh: dp: 8 (over z, x), span: 2 (over y), tensor: 2 (over core).
Axes of the slice: x: 2, y: 2, z: 4, core: 2. Of those that a mesh axis runs over, the one named last changes fastest.
Arguments:
- queries: bfloat16 [8, 256, 4096], P('dp', 'span', 'tensor'), may hold values from -180 to 180
- key_states: bfloat16 [8, 256, 4096], P('dp', 'span', 'tensor'), may hold values from -6 to 6
- value_states: bfloat16 [8, 256, 4096], P('dp', 'span', 'tensor'), may hold values from -6 to 6
- out_grad: bfloat16 [8, 256, 4096], P('dp', None, 'span'), may hold values from -6 to 6
- out_weight: bfloat16 [4096, 4096], P('tensor', 'span'), may hold values from -0.09375 to 0.09375
- align_ids: int32 [8, 2, 2], P('dp', 'span'), may hold values from 0 to 1, as said below
- align_count: int32 [8, 2], P('dp', 'span'), may hold values from 1 to 2
Outputs:
- query_grad: bfloat16 [8, 256, 4096], P('dp', 'span', 'tensor')
- key_grad: bfloat16 [8, 256, 4096], P('dp', 'span', 'tensor')
- value_grad: bfloat16 [8, 256, 4096], P('dp', 'span', 'tensor')
- weight_grad: float32 [4096, 4096], P('tensor', 'span')
Inputs may be any that keep to these rules, and one draw needn't show every extreme that they name: `align_ids`: each span's ids are distinct; block b is held by index b // 1 of span, span n by index n // 1, and every id of span n names a block whose holder differs from span n's holder by at most one.
All inputs are finite; a program needn't handle non-finite values.
Results may differ from a plain program's by a relative error of at most 0.033.
Values may be sent and summed in bfloat16 or wider, within the bound.
No kernel may reach another device: no remote copies, remote signals or barrier semaphores. Data moves between devices by JAX's collectives and lax.ppermute only.
A program may use at most 128 MiB of HBM per device.

v0:
```python
import math

import jax
import jax.numpy as jnp
from jax import lax
from jax.sharding import PartitionSpec as P

HEAD_DIM = 128
SPAN = 128
BLOCK = 128
ALIGN = 2


def with_halo(block, sides, width):
    for axis, dim in sides:
        count = lax.axis_size(axis)
        forward = [(i, i + 1) for i in range(count - 1)]
        backward = [(target, source) for source, target in forward]
        low = lax.ppermute(
            lax.slice_in_dim(block, block.shape[dim] - width, None, axis=dim), axis, forward
        )
        high = lax.ppermute(lax.slice_in_dim(block, 0, width, axis=dim), axis, backward)
        block = jnp.concatenate([low, block, high], axis=dim)
    return block


def shifted(value, axis, steps):
    count = lax.axis_size(axis)
    initial, last = (max(0, -steps), min(count, count - steps))
    return lax.ppermute(value, axis, [(source, source + steps) for source in range(initial, last)])


def shards(queries, key_states, value_states, out_grad, out_weight, align_ids, align_count):
    f32 = jnp.float32
    b16 = jnp.bfloat16
    scale = 1.0 / math.sqrt(HEAD_DIM)
    local_width = queries.shape[2]
    local_heads = local_width // HEAD_DIM
    target_rows = queries.shape[1]
    source_rows = key_states.shape[1]
    span_number = target_rows // SPAN
    block_number = source_rows // BLOCK
    grad_rows = out_grad[0]
    context_grad = (
        lax.psum_scatter(
            lax.dot_general(
                grad_rows, out_weight, (((1,), (1,)), ((), ())), preferred_element_type=f32
            ).astype(jnp.bfloat16),
            "span",
            scatter_dimension=0,
            tiled=True,
        )
        .astype(jnp.float32)
        .astype(b16)
    )
    stacked = jnp.stack([key_states[0], value_states[0]])
    panel = with_halo(stacked, (("span", 1),), source_rows)
    position = lax.axis_index("span")
    local_ids = align_ids[0] - (position - 1) * block_number
    panel_blocks = panel.reshape(2, 3 * block_number, BLOCK, local_width)
    fetched = panel_blocks[:, local_ids]
    key_near = fetched[0].reshape(span_number, ALIGN * BLOCK, local_heads, HEAD_DIM)
    value_near = fetched[1].reshape(span_number, ALIGN * BLOCK, local_heads, HEAD_DIM)
    query_heads = queries[0].reshape(span_number, SPAN, local_heads, HEAD_DIM)
    live = (jnp.arange(ALIGN * BLOCK) // BLOCK)[None, :] < align_count[0][:, None]
    mask = live[:, None, None, :]
    scores = (
        jnp.einsum("nqhd,nkhd->nhqk", query_heads, key_near, preferred_element_type=f32) * scale
    )
    masked = jnp.where(mask, scores, -1e30)
    top = jnp.max(masked, axis=-1, keepdims=True)
    weights = jnp.where(mask, jnp.exp(masked - top), 0.0)
    prob = weights / jnp.sum(weights, axis=-1, keepdims=True)
    prob_half = prob.astype(b16)
    context = jnp.einsum(
        "nhqk,nkhd->nqhd", prob_half, value_near, preferred_element_type=f32
    ).astype(b16)
    grad_heads = context_grad.reshape(span_number, SPAN, local_heads, HEAD_DIM)
    dprob = jnp.einsum("nqhd,nkhd->nhqk", grad_heads, value_near, preferred_element_type=f32)
    delta = jnp.einsum("nqhd,nqhd->nhq", grad_heads, context, preferred_element_type=f32)[..., None]
    dscore = (prob * (dprob - delta)).astype(b16)
    query_grad = (
        jnp.einsum("nhqk,nkhd->nqhd", dscore, key_near, preferred_element_type=f32) * scale
    ).astype(b16)
    key_term = (
        jnp.einsum("nhqk,nqhd->nkhd", dscore, query_heads, preferred_element_type=f32) * scale
    )
    value_term = jnp.einsum("nhqk,nqhd->nkhd", prob_half, grad_heads, preferred_element_type=f32)
    slot_terms = jnp.stack([key_term, value_term]).reshape(
        2, span_number * ALIGN, BLOCK, local_width
    )
    flat_ids = local_ids.reshape(span_number * ALIGN)
    spread = (
        jnp.zeros((2, 3 * block_number, BLOCK, local_width), f32).at[:, flat_ids].add(slot_terms)
    )
    spread = spread.reshape(2, 3 * source_rows, local_width)
    lower_rim = spread[:, :source_rows].astype(b16)
    upper_rim = spread[:, 2 * source_rows :].astype(b16)
    from_above = shifted(lower_rim, "span", -1)
    from_below = shifted(upper_rim, "span", 1)
    summed = (
        spread[:, source_rows : 2 * source_rows] + from_above.astype(f32) + from_below.astype(f32)
    )
    pair_grad = summed.astype(b16)
    flat_context = context.reshape(target_rows, local_width)
    gathered = lax.all_gather(flat_context, "span", axis=0, tiled=True)
    partial_grad = lax.dot_general(
        gathered, grad_rows, (((0,), (0,)), ((), ())), preferred_element_type=f32
    )
    weight_grad = lax.psum(partial_grad, "dp")
    query_out = query_grad.reshape(1, target_rows, local_width)
    return (query_out, pair_grad[0][None], pair_grad[1][None], weight_grad)


def solution(mesh):
    return jax.shard_map(
        shards,
        mesh=mesh,
        in_specs=(
            P("dp", "span", "tensor"),
            P("dp", "span", "tensor"),
            P("dp", "span", "tensor"),
            P("dp", None, "span"),
            P("tensor", "span"),
            P("dp", "span", None),
            P("dp", "span"),
        ),
        out_specs=(
            P("dp", "span", "tensor"),
            P("dp", "span", "tensor"),
            P("dp", "span", "tensor"),
            P("tensor", "span"),
        ),
        check_vma=False,
    )
```

profile of v0, /device:TPU:8, one launch (start us, length us, event | category | flops | bytes accessed | tf_op | source)
XLA Modules:
  0.0 629.9 jit_solution(5922074715852494510)
XLA Ops:
  9.5 1.3 collective-permute-start.1
  10.8 5.6 collective-permute-start
  16.4 6.8 %convolution_convert_fusion = bf16[256,2048]{1,0:T(8,128)(2,1)} fusion(bf16[2048,2048]{1,0:T(8,128)(2,1)} %param.11, bf16[1,256,2048]{2,1,0:T(8,128)(2,1)S(1)} %copy-done), kind=kOutput, calls=%fused_computation.5 | convolution fusion | flops 2148007936 | bytes 10485760 | tf_op jit(solution)/shard_map/dot_general | solution.py:46
  23.8 2.0 copy.66
  25.8 16.3 %collective-permute-done.1 = bf16[2,128,2048]{2,1,0:T(8,128)(2,1)S(1)} collective-permute-done((bf16[2,128,2048]{2,1,0:T(8,128)(2,1)S(1)}, bf16[2,128,2048]{2,1,0:T(8,128)(2,1)S(1)}, u32[]{:S(2)}, u32[]{:S(2)}) %collective-permute-start.1) | collective-permute-done | bytes 1048608 | tf_op jit(solution)/shard_map/ppermute | solution.py:22
  42.1 4.7 collective-permute-done
  46.8 2.8 pad_maximum_fusion
  49.6 2.6 gather_fusion
  53.6 1.6 copy.42
  55.2 2.5 copy.65
  57.7 1.6 copy.45
  59.8 2.3 fusion.29
  64.3 2.6 copy.61
  66.9 3.4 multiply_reduce_fusion
  70.4 23.8 %all-gather.2.cloned.1.call-done = bf16[256,2048]{0,1:T(8,128)(2,1)} async-done(((bf16[128,2048]{0,1:T(8,128)(2,1)}), bf16[256,2048]{0,1:T(8,128)(2,1)}) %all-gather.2.cloned.1.call-update) | async-done | bytes 1048592 | tf_op jit(solution)/shard_map/all_gather | solution.py:106
  94.2 9.7 %fusion.9 = f32[2048,2048]{1,0:T(8,128)} fusion(bf16[256,2048]{0,1:T(8,128)(2,1)} %all-gather.2.cloned.1.call-done, bf16[1,256,2048]{2,1,0:T(8,128)(2,1)S(1)} %copy-done), kind=kOutput, calls=%fused_computation.21 | convolution fusion | flops 2147483648 | bytes 18874368 | tf_op jit(solution)/shard_map/dot_general | solution.py:107
  104.4 3.5 convolution_bitcast_fusion
  108.0 3.1 copy.64
  111.0 2.7 multiply_convert_fusion
  115.8 3.8 maximum_bitcast_fusion
  119.5 4.4 copy.52
  124.0 3.4 broadcast_in_dim.34
  127.4 8.3 %scatter_fusion = f32[2,3,128,2048]{3,2,1,0:T(8,128)} fusion(f32[2,3,128,2048]{3,2,1,0:T(8,128)} %broadcast_in_dim.34, s32[2]{0:T(128)S(1)} %fusion.21, f32[2,2,128,2048]{3,2,1,0:T(8,128)} %copy.52), kind=kCustom, calls=%fused_computation.1 | custom fusion | flops 1048576 | bytes 12582920 | tf_op jit(solution)/shard_map/scatter-add | solution.py:94
  135.7 3.3 bitcast_convert_fusion.1
  139.1 1.5 fusion.26
  140.6 1.3 collective-permute-start.2
  141.8 6.5 %collective-permute-start.3 = (bf16[2,128,2048]{2,1,0:T(8,128)(2,1)}, bf16[2,128,2048]{2,1,0:T(8,128)(2,1)}, u32[]{:S(2)}, u32[]{:S(2)}) collective-permute-start(bf16[2,128,2048]{2,1,0:T(8,128)(2,1)} %get-tuple-element.17), channel_id=1, source_target_pairs={{0,2},{1,3},{4,6},{5,7},{8,10},{9,11},{12,14},{13,15},{16,18},{17,... | collective-permute-start | bytes 3145736 | tf_op jit(solution)/shard_map/ppermute | solution.py:30
  149.8 18.0 %collective-permute-done.2 = bf16[2,128,2048]{2,1,0:T(8,128)(2,1)} collective-permute-done((bf16[2,128,2048]{2,1,0:T(8,128)(2,1)}, bf16[2,128,2048]{2,1,0:T(8,128)(2,1)}, u32[]{:S(2)}, u32[]{:S(2)}) %collective-permute-start.2) | collective-permute-done | bytes 1048608 | tf_op jit(solution)/shard_map/ppermute | solution.py:30
  167.9 2.2 collective-permute-done.3
  170.0 2.7 fusion.2
  173.8 437.7 %all-reduce.2.cloned.1.call-done = f32[2048,2048]{1,0:T(8,128)} async-done(((f32[2048,2048]{1,0:T(8,128)}), f32[2048,2048]{1,0:T(8,128)}) %all-reduce.2.cloned.1.call-update) | async-done | bytes 16777232 | tf_op jit(solution)/shard_map/psum | solution.py:110
  611.5 11.9 %copy.77 = f32[2048,2048]{1,0:T(8,128)} copy(f32[2048,2048]{1,0:T(8,128)} %all-reduce.2.cloned.1.call-done) | data formatting | bytes 33554432
  (36 shorter events, 11.5 us)
Async XLA Ops:
  7.2 9.2 %copy-start = (bf16[1,256,2048]{2,1,0:T(8,128)(2,1)S(1)}, bf16[1,256,2048]{2,1,0:T(8,128)(2,1)}, u32[]{:S(2)}) copy-start(bf16[1,256,2048]{2,1,0:T(8,128)(2,1)} %param.10) | copy-start | bytes 3145732
  7.2 54.9 %reduce-scatter.2.cloned.1.call-start = ((), (), s32[]{:S(2)}) async-start(), calls=%async_computation.1 | async-start | bytes 1572864 | tf_op jit(solution)/shard_map/reduce_scatter | solution.py:45
  9.5 32.6 %collective-permute-start.1 = (bf16[2,128,2048]{2,1,0:T(8,128)(2,1)S(1)}, bf16[2,128,2048]{2,1,0:T(8,128)(2,1)S(1)}, u32[]{:S(2)}, u32[]{:S(2)}) collective-permute-start(bf16[2,128,2048]{2,1,0:T(8,128)(2,1)S(1)} %constant_dynamic-update-slice_fusion), channel_id=1, source_target_pairs={{2,0},{3,1},{6,4},{7,5},{10,8},{11,9},{14,12},{15,13},{18,16},{19,... | collective-permute-start | bytes 3145736 | tf_op jit(solution)/shard_map/ppermute | solution.py:22
  10.8 36.1 %collective-permute-start = (bf16[2,128,2048]{2,1,0:T(8,128)(2,1)S(1)}, bf16[2,128,2048]{2,1,0:T(8,128)(2,1)}, u32[]{:S(2)}, u32[]{:S(2)}) collective-permute-start(bf16[2,128,2048]{2,1,0:T(8,128)(2,1)S(1)} %constant_dynamic-update-slice_fusion), channel_id=1, source_target_pairs={{0,2},{1,3},{4,6},{5,7},{8,10},{9,11},{12,14},{13,15},{16,18},{17,... | collective-permute-start | bytes 3145736 | tf_op jit(solution)/shard_map/ppermute | solution.py:19
  23.1 2.7 copy-start.5
  23.1 71.0 %all-gather.2.cloned.1.call-start = ((), (), s32[]{:S(2)}) async-start(), calls=%async_computation.2 | async-start | bytes 1572864 | tf_op jit(solution)/shard_map/all_gather | solution.py:106
  55.2 4.1 copy-start.3
  70.3 541.2 %all-reduce.2.cloned.1.call-start = ((), (), s32[]{:S(2)}) async-start(), calls=%async_computation.3 | async-start | bytes 33554432 | tf_op jit(solution)/shard_map/psum | solution.py:110
  104.4 3.6 copy-start.4
  114.2 1.6 copy-start.2
  140.6 27.3 %collective-permute-start.2 = (bf16[2,128,2048]{2,1,0:T(8,128)(2,1)}, bf16[2,128,2048]{2,1,0:T(8,128)(2,1)}, u32[]{:S(2)}, u32[]{:S(2)}) collective-permute-start(bf16[2,128,2048]{2,1,0:T(8,128)(2,1)} %get-tuple-element.16), channel_id=1, source_target_pairs={{2,0},{3,1},{6,4},{7,5},{10,8},{11,9},{14,12},{15,13},{18,16},{19,... | collective-permute-start | bytes 3145736 | tf_op jit(solution)/shard_map/ppermute | solution.py:30
  141.8 28.2 %collective-permute-start.3 = (bf16[2,128,2048]{2,1,0:T(8,128)(2,1)}, bf16[2,128,2048]{2,1,0:T(8,128)(2,1)}, u32[]{:S(2)}, u32[]{:S(2)}) collective-permute-start(bf16[2,128,2048]{2,1,0:T(8,128)(2,1)} %get-tuple-element.17), channel_id=1, source_target_pairs={{0,2},{1,3},{4,6},{5,7},{8,10},{9,11},{12,14},{13,15},{16,18},{17,... | collective-permute-start | bytes 3145736 | tf_op jit(solution)/shard_map/ppermute | solution.py:30
  611.5 11.9 %copy-start.1 = (bf16[1,256,2048]{2,1,0:T(8,128)(2,1)S(1)}, bf16[1,256,2048]{2,1,0:T(8,128)(2,1)}, u32[]{:S(2)}) copy-start(bf16[1,256,2048]{2,1,0:T(8,128)(2,1)} %param.10) | copy-start | bytes 3145732
Sparse Core Ops, SparseCore 0:
  23.3 25.5 reduce-scatter.1
  70.4 23.7 all-gather.1
  104.1 507.3 all-reduce.1
where the time goes:
time: 634 us; the launch traced here: 630 us
  waiting for transfers between devices  503 us (79%)
  local copies, waits for them, and re-layouts  46 us (7%)
  matrix products  27.5 us (4%)
  other arithmetic  24.3 us (4%)
  starting transfers between devices  14.8 us (2%)
  between operations  14.6 us (2%)
    psum x1, waiting for transfers between devices, shards(): weight_grad = lax.psum(partial_grad, 'dp')  438 us
    all_gather x1, waiting for transfers between devices, shards(): gathered = lax.all_gather(flat_context, 'span', axis=0, tiled=True)  23.8 us
    unnamed x20, local copies, waits for them, and re-layouts  22.9 us
    ppermute x2, waiting for transfers between devices, shifted(): lax.ppermute(value, axis, [(source, source + steps) for source in range(i...  20.2 us
    ppermute x1, waiting for transfers between devices, with_halo(): lax.ppermute(lax.slice_in_dim(block, 0, width, axis=dim), axis, backward)  16.3 us
  transfers between devices with their start and end apart: 7, of which 6 were waited for; matrix products, arithmetic and copies ran while one was open for 10% of the time, Pallas kernels for 0%

commit v1 on v0

--- a/solution.py
+++ b/solution.py
@@ -103,11 +103,26 @@
     )
     pair_grad = summed.astype(b16)
     flat_context = context.reshape(target_rows, local_width)
-    gathered = lax.all_gather(flat_context, "span", axis=0, tiled=True)
-    partial_grad = lax.dot_general(
-        gathered, grad_rows, (((0,), (0,)), ((), ())), preferred_element_type=f32
-    )
-    weight_grad = lax.psum(partial_grad, "dp")
+    documents = lax.axis_size("dp")
+    tokens = documents * grad_rows.shape[0]
+    columns = grad_rows.shape[1]
+    if tokens * (local_width + columns) <= 2 * local_width * columns:
+        cores = lax.axis_size("tensor")
+        share = grad_rows.shape[0] // cores
+        own_share = lax.dynamic_slice_in_dim(
+            grad_rows, lax.axis_index("tensor") * share, share, axis=0
+        )
+        all_grad = lax.all_gather(own_share, ("dp", "tensor"), axis=0, tiled=True)
+        all_context = lax.all_gather(flat_context, ("dp", "span"), axis=0, tiled=True)
+        weight_grad = lax.dot_general(
+            all_context, all_grad, (((0,), (0,)), ((), ())), preferred_element_type=f32
+        )
+    else:
+        gathered = lax.all_gather(flat_context, "span", axis=0, tiled=True)
+        partial_grad = lax.dot_general(
+            gathered, grad_rows, (((0,), (0,)), ((), ())), preferred_element_type=f32
+        )
+        weight_grad = lax.psum(partial_grad, "dp")
     query_out = query_grad.reshape(1, target_rows, local_width)
     return (query_out, pair_grad[0][None], pair_grad[1][None], weight_grad)
 

time: 634 us -> 283 us (0.45)
  waiting for transfers between devices: 503 us -> 155 us
  local copies, waits for them, and re-layouts: 46 us -> 32.3 us
  matrix products: 27.5 us -> 40.4 us
    psum x1 -> x0, waiting for transfers between devices: 438 us -> none  [shards(): weight_grad = lax.psum(partial_grad, 'dp')]
    all_gather x1 -> x2, waiting for transfers between devices: 23.8 us -> 90.3 us  [the longest x1 90.3 us: shards(): lax.all_gather(flat_context, ('dp', 'span'), axis=0, tiled=True)]
    ppermute x1, waiting for transfers between devices: 4.73 us -> 29.6 us  [with_halo(): lax.ppermute(lax.slice_in_dim(block, block.shape[dim] - width, None, axis...]
    dot_general x1, matrix products: 9.73 us -> 24.3 us  [shards(): lax.dot_general(all_context, all_grad, (((0,), (0,)), ((), ())), preferre...]
    unnamed x20 -> x29, local copies, waits for them, and re-layouts: 22.9 us -> 9.37 us
    ppermute x1, waiting for transfers between devices: 16.3 us -> 4.18 us  [with_halo(): lax.ppermute(lax.slice_in_dim(block, 0, width, axis=dim), axis, backward)]
    ppermute x2, waiting for transfers between devices: 20.2 us -> 31.2 us  [shifted(): lax.ppermute(value, axis, [(source, source + steps) for source in range(i...]
  transfers between devices with their start and end apart: 7 -> 7, of which waited for: 6 -> 5; matrix products, arithmetic and copies ran while one was open for 10% -> 22% of each run, Pallas kernels for 0% -> 0%
where the time goes in v1:
time: 283 us; the launch traced here: 279 us
  waiting for transfers between devices  155 us (55%)
  matrix products  40.4 us (14%)
  local copies, waits for them, and re-layouts  32.3 us (11%)
  other arithmetic  23.3 us (8%)
  between operations  16.4 us (6%)
  starting transfers between devices  11.8 us (4%)
    all_gather x1, waiting for transfers between devices, shards(): lax.all_gather(flat_context, ('dp', 'span'), axis=0, tiled=True)  90.3 us
    ppermute x2, waiting for transfers between devices, shifted(): lax.ppermute(value, axis, [(source, source + steps) for source in range(i...  31.2 us
    ppermute x1, waiting for transfers between devices, with_halo(): lax.ppermute(lax.slice_in_dim(block, block.shape[dim] - width, None, axis...  29.6 us
    dot_general x1, matrix products, shards(): lax.dot_general(all_context, all_grad, (((0,), (0,)), ((), ())), preferre...  24.3 us
    unnamed x29, local copies, waits for them, and re-layouts  9.37 us
    scatter-add x1, other arithmetic, shards(): jnp.zeros((2, 3 * block_number, BLOCK, local_width), f32).at[:, flat_ids]  8.2 us
    another operation x2, local copies, waits for them, and re-layouts, shards(): jnp.stack([key_term, value_term])  7.44 us
    ppermute x2, starting transfers between devices, shifted(): lax.ppermute(value, axis, [(source, source + steps) for source in range(i...  6.87 us
  transfers between devices with their start and end apart: 7, of which 5 were waited for; matrix products, arithmetic and copies ran while one was open for 22% of the time, Pallas kernels for 0%

profile of v1, /device:TPU:8, one launch (start us, length us, event | category | flops | bytes accessed | tf_op | source)
XLA Modules:
  0.0 279.5 jit_solution(15597228796381000964)
XLA Ops:
  8.1 1.2 copy-done
  9.2 6.8 %convolution_convert_fusion = bf16[256,2048]{1,0:T(8,128)(2,1)} fusion(bf16[2048,2048]{1,0:T(8,128)(2,1)} %param.11, bf16[1,256,2048]{2,1,0:T(8,128)(2,1)S(1)} %copy-done), kind=kOutput, calls=%fused_computation.7 | convolution fusion | flops 2148007936 | bytes 10485760 | tf_op jit(solution)/shard_map/dot_general | solution.py:46
  17.5 3.5 %collective-permute-start = (bf16[2,128,2048]{2,1,0:T(8,128)(2,1)S(1)}, bf16[2,128,2048]{2,1,0:T(8,128)(2,1)S(1)}, u32[]{:S(2)}, u32[]{:S(2)}) collective-permute-start(bf16[2,128,2048]{2,1,0:T(8,128)(2,1)S(1)} %constant_dynamic-update-slice_fusion), channel_id=1, source_target_pairs={{0,2},{1,3},{4,6},{5,7},{8,10},{9,11},{12,14},{13,15},{16,18},{17,... | collective-permute-start | bytes 3145736 | tf_op jit(solution)/shard_map/ppermute | solution.py:19
  21.0 1.3 collective-permute-start.1
  22.3 2.0 copy.66
  24.9 29.6 %collective-permute-done = bf16[2,128,2048]{2,1,0:T(8,128)(2,1)S(1)} collective-permute-done((bf16[2,128,2048]{2,1,0:T(8,128)(2,1)S(1)}, bf16[2,128,2048]{2,1,0:T(8,128)(2,1)S(1)}, u32[]{:S(2)}, u32[]{:S(2)}) %collective-permute-start) | collective-permute-done | bytes 1048608 | tf_op jit(solution)/shard_map/ppermute | solution.py:19
  54.5 4.2 %collective-permute-done.1 = bf16[2,128,2048]{2,1,0:T(8,128)(2,1)S(1)} collective-permute-done((bf16[2,128,2048]{2,1,0:T(8,128)(2,1)S(1)}, bf16[2,128,2048]{2,1,0:T(8,128)(2,1)S(1)}, u32[]{:S(2)}, u32[]{:S(2)}) %collective-permute-start.1) | collective-permute-done | bytes 1048608 | tf_op jit(solution)/shard_map/ppermute | solution.py:22
  58.7 1.8 pad_maximum_fusion
  60.5 2.6 gather_fusion
  65.2 1.5 copy.68
  66.7 1.6 copy.42
  68.8 2.2 fusion.29
  72.3 1.5 copy.61
  73.8 3.5 %multiply_reduce_fusion = (f32[16,128]{1,0:T(8,128)S(1)}, bf16[16,128,128]{2,1,0:T(8,128)(2,1)}) fusion(f32[16,128,128]{1,2,0:T(8,128)} %copy.61, bf16[256,16,128]{0,2,1:T(8,128)(2,1)} %copy.42, f32[16,128,256]{1,2,0:T(8,128)} %get-tuple-element.23, f32[16,128]{1,0:T(8,128)S(1)} %get-tuple-element.22), kind=kOutput, calls=%fused_computation.24 | convolution fusion | flops 136312832 | bytes 4734976 | tf_op jit(solution)/shard_map/nhqk,nkhd->nqhd/dot_general | solution.py:75
  77.4 1.2 copy.49
  78.6 2.7 multiply_convert_fusion
  81.8 1.2 copy.48
  83.5 1.8 convolution_bitcast_fusion
  85.3 3.1 %copy.64 = f32[1,256,16,128]{3,2,1,0:T(8,128)} copy(f32[1,256,16,128]{1,3,2,0:T(8,128)} %convolution_bitcast_fusion) | data formatting | bytes 4194304 | tf_op jit(solution)/shard_map/stack | solution.py:89
  88.3 5.4 %maximum_bitcast_fusion = f32[2,2,128,2048]{3,1,2,0:T(2,128)S(1)} fusion(f32[1,2,128,2048]{3,0,2,1:T(1,128)} %bitcast.94, f32[1,2,128,2048]{3,0,2,1:T(1,128)S(1)} %bitcast.93), kind=kLoop, calls=%fused_computation.5 | loop fusion | flops 1048576 | bytes 8388608 | tf_op jit(solution)/shard_map/stack | solution.py:89
  93.7 4.4 %copy.52 = f32[2,2,128,2048]{3,2,1,0:T(8,128)} copy(f32[2,2,128,2048]{3,1,2,0:T(2,128)S(1)} %maximum_bitcast_fusion) | data formatting | bytes 8388608 | tf_op jit(solution)/shard_map/stack | solution.py:89
  98.1 3.5 %broadcast_in_dim.34 = f32[2,3,128,2048]{3,2,1,0:T(8,128)} broadcast(f32[]{:T(128)} %constant.44.clone.1), dimensions={} | broadcast | bytes 6291460 | tf_op jit(solution)/shard_map/broadcast_in_dim | solution.py:94
  101.6 8.2 %scatter_fusion = f32[2,3,128,2048]{3,2,1,0:T(8,128)} fusion(f32[2,3,128,2048]{3,2,1,0:T(8,128)} %broadcast_in_dim.34, s32[2]{0:T(128)S(1)} %fusion.21, f32[2,2,128,2048]{3,2,1,0:T(8,128)} %copy.52), kind=kCustom, calls=%fused_computation.1 | custom fusion | flops 1048576 | bytes 12582920 | tf_op jit(solution)/shard_map/scatter-add | solution.py:94
  109.8 3.3 %bitcast_convert_fusion.1 = bf16[2,384,2048]{2,1,0:T(8,128)(2,1)S(1)} fusion(f32[2,3,128,2048]{3,2,1,0:T(8,128)} %scatter_fusion), kind=kLoop, calls=%fused_computation.47 | loop fusion | flops 1572864 | bytes 9437184 | tf_op jit(solution)/shard_map/convert.1
  113.0 1.5 fusion.26
  114.5 1.3 collective-permute-start.2
  115.8 5.6 %collective-permute-start.3 = (bf16[2,128,2048]{2,1,0:T(8,128)(2,1)}, bf16[2,128,2048]{2,1,0:T(8,128)(2,1)}, u32[]{:S(2)}, u32[]{:S(2)}) collective-permute-start(bf16[2,128,2048]{2,1,0:T(8,128)(2,1)} %get-tuple-element.17), channel_id=1, source_target_pairs={{0,2},{1,3},{4,6},{5,7},{8,10},{9,11},{12,14},{13,15},{16,18},{17,... | collective-permute-start | bytes 3145736 | tf_op jit(solution)/shard_map/ppermute | solution.py:30
  122.9 29.8 %collective-permute-done.2 = bf16[2,128,2048]{2,1,0:T(8,128)(2,1)S(1)} collective-permute-done((bf16[2,128,2048]{2,1,0:T(8,128)(2,1)}, bf16[2,128,2048]{2,1,0:T(8,128)(2,1)S(1)}, u32[]{:S(2)}, u32[]{:S(2)}) %collective-permute-start.2) | collective-permute-done | bytes 1048608 | tf_op jit(solution)/shard_map/ppermute | solution.py:30
  152.7 1.3 collective-permute-done.3
  154.0 2.3 fusion.4
  157.4 90.3 %all-gather.4.cloned.1.call-done = bf16[2048,2048]{0,1:T(8,128)(2,1)} async-done(((bf16[128,2048]{0,1:T(8,128)(2,1)}), bf16[2048,2048]{0,1:T(8,128)(2,1)}) %all-gather.4.cloned.1.call-update) | async-done | bytes 8388624 | tf_op jit(solution)/shard_map/all_gather | solution.py:116
  247.8 24.3 %fusion.1 = f32[2048,2048]{1,0:T(8,128)} fusion(bf16[2048,2048]{0,1:T(8,128)(2,1)} %all-gather.4.cloned.1.call-done, bf16[1,2048,2048]{2,1,0:T(8,128)(2,1)} %all-gather.6.cloned.1.call-done), kind=kOutput, calls=%fused_computation.3 | convolution fusion | flops 17179869184 | bytes 33554432 | tf_op jit(solution)/shard_map/dot_general | solution.py:117
  (46 shorter events, 8.8 us)
Async XLA Ops:
  8.0 1.2 copy-start
  8.0 63.0 %reduce-scatter.2.cloned.1.call-start = ((), (), s32[]{:S(2)}) async-start(), calls=%async_computation.1 | async-start | bytes 1572864 | tf_op jit(solution)/shard_map/reduce_scatter | solution.py:45
  16.0 1.1 copy-start.6
  16.0 1.4 copy-start.7
  16.1 141.4 %all-gather.6.cloned.1.call-start = ((), (), s32[]{:S(2)}) async-start(), calls=%async_computation.3 | async-start | bytes 8912896 | tf_op jit(solution)/shard_map/all_gather | solution.py:115
  17.0 7.9 %copy-start.9 = (s32[1,1,2]{2,1,0:T(1,128)S(1)}, s32[1,1,2]{2,1,0:T(1,128)}, u32[]{:S(2)}) copy-start(s32[1,1,2]{2,1,0:T(1,128)} %param.12) | copy-start | bytes 28
  17.0 230.7 %all-gather.4.cloned.1.call-start = ((), (), s32[]{:S(2)}) async-start(), calls=%async_computation.2 | async-start | bytes 8912896 | tf_op jit(solution)/shard_map/all_gather | solution.py:116
  17.5 37.1 %collective-permute-start = (bf16[2,128,2048]{2,1,0:T(8,128)(2,1)S(1)}, bf16[2,128,2048]{2,1,0:T(8,128)(2,1)S(1)}, u32[]{:S(2)}, u32[]{:S(2)}) collective-permute-start(bf16[2,128,2048]{2,1,0:T(8,128)(2,1)S(1)} %constant_dynamic-update-slice_fusion), channel_id=1, source_target_pairs={{0,2},{1,3},{4,6},{5,7},{8,10},{9,11},{12,14},{13,15},{16,18},{17,... | collective-permute-start | bytes 3145736 | tf_op jit(solution)/shard_map/ppermute | solution.py:19
  21.0 37.7 %collective-permute-start.1 = (bf16[2,128,2048]{2,1,0:T(8,128)(2,1)S(1)}, bf16[2,128,2048]{2,1,0:T(8,128)(2,1)S(1)}, u32[]{:S(2)}, u32[]{:S(2)}) collective-permute-start(bf16[2,128,2048]{2,1,0:T(8,128)(2,1)S(1)} %constant_dynamic-update-slice_fusion), channel_id=1, source_target_pairs={{2,0},{3,1},{6,4},{7,5},{10,8},{11,9},{14,12},{15,13},{18,16},{19,... | collective-permute-start | bytes 3145736 | tf_op jit(solution)/shard_map/ppermute | solution.py:22
  65.2 3.1 %copy-start.2 = (bf16[16,8,16,128]{3,2,1,0:T(8,128)(2,1)S(1)}, bf16[16,8,16,128]{3,2,1,0:T(8,128)(2,1)}, u32[]{:S(2)}) copy-start(bf16[16,8,16,128]{3,2,1,0:T(8,128)(2,1)} %copy.66) | copy-start | bytes 1572868
  73.8 4.8 %copy-start.5 = (bf16[256,16,128]{0,2,1:T(8,128)(2,1)S(1)}, bf16[256,16,128]{0,2,1:T(8,128)(2,1)}, u32[]{:S(2)}) copy-start(bf16[256,16,128]{0,2,1:T(8,128)(2,1)} %copy.42) | copy-start | bytes 3145732
  81.3 1.7 copy-start.3
  81.7 1.3 copy-start.8
  81.7 1.8 copy-start.10
  113.0 8.4 %copy-start.4 = (bf16[16,128,256]{1,2,0:T(8,128)(2,1)S(1)}, bf16[16,128,256]{1,2,0:T(8,128)(2,1)}, u32[]{:S(2)}) copy-start(bf16[16,128,256]{1,2,0:T(8,128)(2,1)} %copy-done.3) | copy-start | bytes 3145732
  114.5 38.2 %collective-permute-start.2 = (bf16[2,128,2048]{2,1,0:T(8,128)(2,1)}, bf16[2,128,2048]{2,1,0:T(8,128)(2,1)S(1)}, u32[]{:S(2)}, u32[]{:S(2)}) collective-permute-start(bf16[2,128,2048]{2,1,0:T(8,128)(2,1)} %get-tuple-element.16), channel_id=1, source_target_pairs={{2,0},{3,1},{6,4},{7,5},{10,8},{11,9},{14,12},{15,13},{18,16},{19,... | collective-permute-start | bytes 3145736 | tf_op jit(solution)/shard_map/ppermute | solution.py:30
  115.8 38.2 %collective-permute-start.3 = (bf16[2,128,2048]{2,1,0:T(8,128)(2,1)}, bf16[2,128,2048]{2,1,0:T(8,128)(2,1)}, u32[]{:S(2)}, u32[]{:S(2)}) collective-permute-start(bf16[2,128,2048]{2,1,0:T(8,128)(2,1)} %get-tuple-element.17), channel_id=1, source_target_pairs={{0,2},{1,3},{4,6},{5,7},{8,10},{9,11},{12,14},{13,15},{16,18},{17,... | collective-permute-start | bytes 3145736 | tf_op jit(solution)/shard_map/ppermute | solution.py:30
  247.8 24.3 %copy-start.1 = (bf16[1,256,2048]{2,1,0:T(8,128)(2,1)S(1)}, bf16[1,256,2048]{2,1,0:T(8,128)(2,1)}, u32[]{:S(2)}) copy-start(bf16[1,256,2048]{2,1,0:T(8,128)(2,1)} %param.10) | copy-start | bytes 3145732
Sparse Core Ops, SparseCore 0:
  16.2 32.5 reduce-scatter.1
Sparse Core Ops, SparseCore 1:
  18.9 75.2 all-gather.5
  97.2 150.5 all-gather.3

commit v2 on v1

--- a/solution.py
+++ b/solution.py
@@ -3,6 +3,8 @@
 import jax
 import jax.numpy as jnp
 from jax import lax
+from jax.experimental import pallas as pl
+from jax.experimental.pallas import tpu as pltpu
 from jax.sharding import PartitionSpec as P
 
 HEAD_DIM = 128
@@ -30,7 +32,214 @@
     return lax.ppermute(value, axis, [(source, source + steps) for source in range(initial, last)])
 
 
+NT = (((1,), (1,)), ((), ()))
+TN = (((0,), (0,)), ((), ()))
+NN = (((1,), (0,)), ((), ()))
+
+
+def dot(a, b, dims):
+    return lax.dot_general(a, b, dims, preferred_element_type=jnp.float32)
+
+
+def ordered(first, own, peer):
+    return jnp.where(
+        first, jnp.concatenate([own, peer], axis=0), jnp.concatenate([peer, own], axis=0)
+    )
+
+
+def forward_kernel(scale, info, q_own, k_own, v_own, q_peer, k_peer, v_peer, prob_ref, context_ref):
+    first = info[0] == 0
+    q = ordered(first, q_own[...], q_peer[0])
+    k = ordered(first, k_own[...], k_peer[0])
+    v = ordered(first, v_own[...], v_peer[0])
+    scores = dot(k, q, NT) * scale
+    lane = lax.broadcasted_iota(jnp.int32, (1, 2 * SPAN), 1) < SPAN
+    bias = [
+        jnp.where(jnp.where(lane, info[1 + b], info[3 + b]) > 0, 0.0, -1e30) for b in range(2)
+    ]
+    scores = jnp.concatenate([scores[:BLOCK] + bias[0], scores[BLOCK:] + bias[1]], axis=0)
+    weights = jnp.exp(scores - jnp.max(scores, axis=0, keepdims=True))
+    prob = weights * (1.0 / jnp.sum(weights, axis=0, keepdims=True))
+    prob_ref[0] = prob
+    context_ref[...] = dot(v, prob.astype(jnp.bfloat16), TN).astype(jnp.bfloat16)
+
+
+def backward_kernel(
+    scale, info, q_own, k_own, v_own, q_peer, k_peer, v_peer, prob_ref, cg_own, cg_peer, kept, sent
+):
+    b16 = jnp.bfloat16
+    first = info[0] == 0
+    q = ordered(first, q_own[...], q_peer[0])
+    k = ordered(first, k_own[...], k_peer[0])
+    v = ordered(first, v_own[...], v_peer[0])
+    cg = (cg_own[...].astype(jnp.float32) + cg_peer[...].astype(jnp.float32)).astype(b16)
+    prob = prob_ref[0]
+    dprob = dot(v, cg, NT)
+    delta = jnp.sum(prob * dprob, axis=0, keepdims=True)
+    dscore = (prob * (dprob - delta)).astype(b16)
+    grads = (
+        (dot(dscore, k, TN) * scale).astype(b16),
+        (dot(dscore, q, NN) * scale).astype(b16),
+        dot(prob.astype(b16), cg, NN).astype(b16),
+    )
+    for i, grad in enumerate(grads):
+        kept[i] = jnp.where(first, grad[:SPAN], grad[SPAN:])
+        sent[i] = jnp.where(first, grad[SPAN:], grad[:SPAN])
+
+
+def weight_kernel(count, *refs):
+    left, right, out = refs[1 : 1 + count], refs[1 + count : 1 + 2 * count], refs[-1]
+    rows = out.shape[0]
+    step = min(256, rows)
+    for r in range(0, rows, step):
+        total = dot(left[0][r : r + step], right[0][...], NN)
+        for a, b in zip(left[1:], right[1:]):
+            total += dot(a[r : r + step], b[...], NN)
+        out[r : r + step] = total
+
+
+def weight_block(place, left, right, held, width):
+    count = len(left)
+    rows, depth = left[0].shape
+    columns = right[0].shape[1]
+    tile = 256
+    tiles = columns // tile
+    in_specs = [pl.BlockSpec((rows, depth), lambda j, p: (0, 0))] * count
+    in_specs += [pl.BlockSpec((depth, tile), lambda j, p: (0, j))] * count
+    operands = [place, *left, *right]
+    aliases = {}
+    if held is not None:
+        in_specs.append(pl.BlockSpec(memory_space=pl.ANY))
+        operands.append(held)
+        aliases = {len(operands) - 1: 0}
+    return pl.pallas_call(
+        lambda *refs: weight_kernel(count, *refs),
+        grid_spec=pltpu.PrefetchScalarGridSpec(
+            num_scalar_prefetch=1,
+            grid=(tiles,),
+            in_specs=in_specs,
+            out_specs=pl.BlockSpec((rows, tile), lambda j, p: (p[0], p[1] * tiles + j)),
+        ),
+        out_shape=jax.ShapeDtypeStruct((width[0], width[1]), jnp.float32),
+        input_output_aliases=aliases,
+        compiler_params=pltpu.CompilerParams(vmem_limit_bytes=40 * 2**20),
+        cost_estimate=pl.CostEstimate(
+            flops=2 * rows * depth * count * columns,
+            bytes_accessed=4 * rows * columns + 2 * count * depth * (rows + columns),
+            transcendentals=0,
+        ),
+    )(*operands)
+
+
+def exchange(value, axis, bits):
+    count = lax.axis_size(axis)
+    return lax.ppermute(value, axis, [(i, i ^ bits) for i in range(count)])
+
+
+def paired(queries, key_states, value_states, out_grad, out_weight, align_ids, align_count):
+    f32 = jnp.float32
+    b16 = jnp.bfloat16
+    scale = 1.0 / math.sqrt(HEAD_DIM)
+    width = queries.shape[2]
+    half = width // 2
+    heads = half // HEAD_DIM
+    rows = queries.shape[1]
+    tokens, columns = out_grad.shape[1:]
+    core_columns = columns // 2
+    y = lax.axis_index("span")
+    t = lax.axis_index("tensor")
+
+    def part(value, which):
+        return lax.dynamic_slice_in_dim(value, which * half, half, axis=1)
+
+    own = (queries[0], key_states[0], value_states[0])
+    peer = exchange(jnp.stack([part(v, 1 - y) for v in own]), "span", 1)
+    slot = jnp.arange(ALIGN)
+    live = jnp.stack(
+        [jnp.any((align_ids[0, 0] == b) & (slot < align_count[0, 0])) for b in range(2)]
+    ).astype(jnp.int32)
+    live_peer = exchange(jnp.broadcast_to(live[:, None], (2, 128)), "span", 1)[:, 0]
+    live = jnp.where(y == 0, jnp.concatenate([live, live_peer]), jnp.concatenate([live_peer, live]))
+    info = jnp.concatenate([jnp.reshape(y, (1,)).astype(jnp.int32), live])
+
+    grad_rows = out_grad[0]
+    grads = [lax.dynamic_slice_in_dim(grad_rows, t * core_columns, core_columns, axis=1)]
+    grads += [exchange(grads[0], "dp", 2 * k) for k in range(1, 4)]
+    grads += [exchange(g, "dp", 1) for g in grads]
+    grads_core = [lax.dynamic_slice_in_dim(grad_rows, (1 - t) * core_columns, core_columns, axis=1)]
+    grads_core += [exchange(g, "tensor", 1) for g in grads[1:]]
+
+    partial = dot(grad_rows, out_weight, NT).astype(b16)
+    partial_peer = exchange(part(partial, 1 - y), "span", 1)
+
+    own_spec = pl.BlockSpec((rows, HEAD_DIM), lambda h, info: (0, info[0] * heads + h))
+    peer_specs = [
+        pl.BlockSpec((1, rows, HEAD_DIM), lambda h, info, i=i: (i, 0, h)) for i in range(3)
+    ]
+    prob_spec = pl.BlockSpec((1, 2 * BLOCK, 2 * SPAN), lambda h, info: (h, 0, 0))
+    prob, context = pl.pallas_call(
+        lambda *refs: forward_kernel(scale, *refs),
+        grid_spec=pltpu.PrefetchScalarGridSpec(
+            num_scalar_prefetch=1,
+            grid=(heads,),
+            in_specs=[own_spec] * 3 + peer_specs,
+            out_specs=[prob_spec, pl.BlockSpec((HEAD_DIM, 2 * SPAN), lambda h, info: (h, 0))],
+        ),
+        out_shape=[
+            jax.ShapeDtypeStruct((heads, 2 * BLOCK, 2 * SPAN), f32),
+            jax.ShapeDtypeStruct((half, 2 * SPAN), b16),
+        ],
+        cost_estimate=pl.CostEstimate(
+            flops=heads * 2**25, bytes_accessed=5 * 2**20, transcendentals=heads * 2**16
+        ),
+    )(info, *own, peer, peer, peer)
+
+    near = [context] + [exchange(context, "dp", 2 * k) for k in range(1, 4)]
+    near_x = [exchange(c, "dp", 1) for c in near]
+    far = [exchange(c, "span", 1) for c in near]
+    far_x = [exchange(c, "span", 1) for c in near_x[:2]] + [exchange(c, "dp", 1) for c in far[2:]]
+
+    cg_own = pl.BlockSpec((tokens, HEAD_DIM), lambda h, info: (0, info[0] * heads + h))
+    cg_peer = pl.BlockSpec((tokens, HEAD_DIM), lambda h, info: (0, h))
+    out_spec = pl.BlockSpec((3, rows, HEAD_DIM), lambda h, info: (0, 0, h))
+    kept, sent = pl.pallas_call(
+        lambda *refs: backward_kernel(scale, *refs),
+        grid_spec=pltpu.PrefetchScalarGridSpec(
+            num_scalar_prefetch=1,
+            grid=(heads,),
+            in_specs=[own_spec] * 3 + peer_specs + [prob_spec, cg_own, cg_peer],
+            out_specs=[out_spec, out_spec],
+        ),
+        out_shape=[jax.ShapeDtypeStruct((3, rows, half), b16)] * 2,
+        cost_estimate=pl.CostEstimate(
+            flops=heads * 2**26, bytes_accessed=6 * 2**20, transcendentals=0
+        ),
+    )(info, *own, peer, peer, peer, prob, partial, partial_peer)
+    received = exchange(sent, "span", 1)
+    outs = [
+        jnp.where(
+            y == 0,
+            jnp.concatenate([kept[i], received[i]], axis=1),
+            jnp.concatenate([received[i], kept[i]], axis=1),
+        )[None]
+        for i in range(3)
+    ]
+
+    weight_grad = None
+    shape = (width, columns)
+    for row, left in ((y, near + near_x), (1 - y, far + far_x)):
+        for column, right in ((t, grads), (1 - t, grads_core)):
+            place = jnp.stack([row, column]).astype(jnp.int32)
+            weight_grad = weight_block(place, left, right, weight_grad, shape)
+    return (*outs, weight_grad)
+
+
 def shards(queries, key_states, value_states, out_grad, out_weight, align_ids, align_count):
+    two_spans = lax.axis_size("span") == 2 and queries.shape[1] == SPAN == key_states.shape[1]
+    if two_spans and lax.axis_size("dp") == 8 and lax.axis_size("tensor") == 2:
+        return paired(
+            queries, key_states, value_states, out_grad, out_weight, align_ids, align_count
+        )
     f32 = jnp.float32
     b16 = jnp.bfloat16
     scale = 1.0 / math.sqrt(HEAD_DIM)

time: 283 us -> 216 us (0.76)
  Pallas kernels: 0 us -> 49.2 us
  waiting for transfers between devices: 155 us -> 109 us
  matrix products: 40.4 us -> 6.08 us
  local copies, waits for them, and re-layouts: 32.3 us -> 9.95 us
  starting transfers between devices: 11.8 us -> 33.1 us
  other arithmetic: 23.3 us -> 6 us
  between operations: 16.4 us -> 1.43 us
    all_gather x2 -> x0, waiting for transfers between devices: 90.3 us -> none  [the longest x1 90.3 us: shards(): lax.all_gather(flat_context, ('dp', 'span'), axis=0, tiled=True)]
    pallas_call x0 -> x6, Pallas kernels: none -> 49.2 us  [the longest x4 32.7 us: weight_block(): pl.pallas_call(lambda *refs: weight_kernel(count, *refs), grid_spec=pltpu...]
    ppermute x4 -> x33, waiting for transfers between devices: 65 us -> 109 us  [exchange(): return lax.ppermute(value, axis, [(i, i ^ bits) for i in range(count)])]
    dot_general x8 -> x1, matrix products: 40.4 us -> 6.08 us  [dot(): return lax.dot_general(a, b, dims, preferred_element_type=jnp.float32)]
    ppermute x4 -> x33, starting transfers between devices: 11.7 us -> 33.1 us  [exchange(): return lax.ppermute(value, axis, [(i, i ^ bits) for i in range(count)])]
    another operation x6 -> x0, local copies, waits for them, and re-layouts: 11.1 us -> none  [the longest x2 7.44 us: shards(): jnp.stack([key_term, value_term])]
    another operation x2 -> x5, other arithmetic: 8.62 us -> 0.39 us  [the longest x4 0.3 us: paired(): place = jnp.stack([row, column]).astype(jnp.int32)]
    scatter-add x1 -> x0, other arithmetic: 8.2 us -> none  [shards(): jnp.zeros((2, 3 * block_number, BLOCK, local_width), f32).at[:, flat_ids]]
  transfers between devices with their start and end apart: 7 -> 33, of which waited for: 5 -> 11; matrix products, arithmetic and copies ran while one was open for 22% -> 8% of each run, Pallas kernels for 0% -> 16%
where the time goes in v2:
time: 216 us; the launch traced here: 214 us
  waiting for transfers between devices  109 us (50%)
  Pallas kernels  49.2 us (23%)
  starting transfers between devices  33.1 us (15%)
  local copies, waits for them, and re-layouts  9.95 us (5%)
  matrix products  6.08 us (3%)
  other arithmetic  6 us (3%)
    ppermute x33, waiting for transfers between devices, exchange(): return lax.ppermute(value, axis, [(i, i ^ bits) for i in range(count)])  109 us
    ppermute x33, starting transfers between devices, exchange(): return lax.ppermute(value, axis, [(i, i ^ bits) for i in range(count)])  33.1 us
    pallas_call x4, Pallas kernels, weight_block(): pl.pallas_call(lambda *refs: weight_kernel(count, *refs), grid_spec=pltpu...  32.7 us
    pallas_call x1, Pallas kernels, paired(): pl.pallas_call(lambda *refs: backward_kernel(scale, *refs), grid_spec=plt...  9.02 us
    pallas_call x1, Pallas kernels, paired(): pl.pallas_call(lambda *refs: forward_kernel(scale, *refs), grid_spec=pltp...  7.39 us
    dot_general x1, matrix products, dot(): return lax.dot_general(a, b, dims, preferred_element_type=jnp.float32)  6.08 us
    unnamed x16, local copies, waits for them, and re-layouts  4.5 us
  transfers between devices with their start and end apart: 33, of which 11 were waited for; matrix products, arithmetic and copies ran while one was open for 8% of the time, Pallas kernels for 16%

profile of v2, /device:TPU:8, one launch (start us, length us, event | category | flops | bytes accessed | tf_op | source)
XLA Modules:
  0.0 214.4 jit_solution(6690465588071090593)
XLA Ops:
  2.0 3.0 %collective-permute-start.19 = (bf16[256,1024]{1,0:T(8,128)(2,1)S(1)}, bf16[256,1024]{1,0:T(8,128)(2,1)}, u32[]{:S(2)}, u32[]{:S(2)}) collective-permute-start(bf16[256,1024]{1,0:T(8,128)(2,1)S(1)} %get-tuple-element.14.refs_9_), channel_id=1, source_target_pairs={{0,16},{4,20},{8,24},{12,28},{16,0},{20,4},{24,8},{28,12},{1,17},{... | collective-permute-start | bytes 1572872 | tf_op jit(solution)/shard_map/ppermute | solution.py:136
  8.5 1.6 collective-permute-start.1
  13.9 6.1 %convolution_convert_fusion.refs_8_ = bf16[256,2048]{1,0:T(8,128)(2,1)S(1)} fusion(bf16[2048,2048]{1,0:T(8,128)(2,1)} %param.11, bf16[1,256,2048]{2,1,0:T(8,128)(2,1)} %param.10), kind=kOutput, calls=%fused_computation | convolution fusion | flops 2148007936 | bytes 10485760 | tf_op jit(solution)/shard_map/dot_general | solution.py:41
  20.0 8.4 %collective-permute-done = s32[2,128]{0,1:T(8,128)S(1)} collective-permute-done((s32[2,128]{0,1:T(8,128)S(1)}, s32[2,128]{0,1:T(8,128)S(1)}, u32[]{:S(2)}, u32[]{:S(2)}) %collective-permute-start) | collective-permute-done | bytes 1056 | tf_op jit(solution)/shard_map/ppermute | solution.py:136
  28.4 1.5 collective-permute-start.23
  30.0 1.6 collective-permute-start.2
  31.5 8.3 %collective-permute-done.19.refs_11_ = bf16[256,1024]{1,0:T(8,128)(2,1)} collective-permute-done((bf16[256,1024]{1,0:T(8,128)(2,1)S(1)}, bf16[256,1024]{1,0:T(8,128)(2,1)}, u32[]{:S(2)}, u32[]{:S(2)}) %collective-permute-start.19) | collective-permute-done | bytes 524320 | tf_op jit(solution)/shard_map/ppermute | solution.py:136
  39.9 1.5 collective-permute-start.25
  41.3 9.3 %collective-permute-done.21.refs_12_ = bf16[256,1024]{1,0:T(8,128)(2,1)} collective-permute-done((bf16[256,1024]{1,0:T(8,128)(2,1)S(1)}, bf16[256,1024]{1,0:T(8,128)(2,1)}, u32[]{:S(2)}, u32[]{:S(2)}) %collective-permute-start.21) | collective-permute-done | bytes 524320 | tf_op jit(solution)/shard_map/ppermute | solution.py:136
  50.7 1.5 collective-permute-start.27
  55.0 10.9 %collective-permute-done.27.refs_15_ = bf16[256,1024]{1,0:T(8,128)(2,1)} collective-permute-done((bf16[256,1024]{1,0:T(8,128)(2,1)}, bf16[256,1024]{1,0:T(8,128)(2,1)}, u32[]{:S(2)}, u32[]{:S(2)}) %collective-permute-start.27) | collective-permute-done | bytes 524320 | tf_op jit(solution)/shard_map/ppermute | solution.py:136
  66.5 7.4 %shard_map.102 = (f32[8,256,256]{2,1,0:T(8,128)}, bf16[1024,256]{1,0:T(8,128)(2,1)}) custom-call(s32[5]{0:T(128)} %pad_add_fusion.refs_0_, bf16[128,2048]{1,0:T(8,128)(2,1)} %bitcast.29, bf16[128,2048]{1,0:T(8,128)(2,1)} %bitcast.31, bf16[128,2048]{1,0:T(8,128)(2,1)} %bitcast.33, bf16[3,128,1024]{2,1,0:T(8,128)(2,1)} %copy-done.5, ...), custom_call_target="tpu_custom_call" | custom-call | flops 268435456 | bytes 5242880 | tf_op jit(solution)/shard_map/pallas_call | solution.py:180
  74.7 2.1 collective-permute-start.5
  78.5 1.5 collective-permute-start.11
  80.0 9.0 %shard_map.103 = (bf16[3,128,1024]{2,1,0:T(8,128)(2,1)}, bf16[3,128,1024]{2,1,0:T(8,128)(2,1)}) custom-call(s32[5]{0:T(128)} %pad_add_fusion.refs_0_, bf16[128,2048]{1,0:T(8,128)(2,1)} %bitcast.30, bf16[128,2048]{1,0:T(8,128)(2,1)} %bitcast.32, bf16[128,2048]{1,0:T(8,128)(2,1)} %bitcast.34, bf16[3,128,1024]{2,1,0:T(8,128)(2,1)} %copy-done.5, ...), custom_call_target="tpu_custom_call" | custom-call | flops 536870912 | bytes 6291456 | tf_op jit(solution)/shard_map/pallas_call | solution.py:205
  89.0 1.6 collective-permute-start.3
  90.7 9.3 %collective-permute-done.5.refs_2_ = bf16[1024,256]{1,0:T(8,128)(2,1)} collective-permute-done((bf16[1024,256]{1,0:T(8,128)(2,1)}, bf16[1024,256]{1,0:T(8,128)(2,1)}, u32[]{:S(2)}, u32[]{:S(2)}) %collective-permute-start.5) | collective-permute-done | bytes 524320 | tf_op jit(solution)/shard_map/ppermute | solution.py:136
  100.0 1.5 collective-permute-start.4
  101.5 11.6 %collective-permute-done.7.refs_3_ = bf16[1024,256]{1,0:T(8,128)(2,1)} collective-permute-done((bf16[1024,256]{1,0:T(8,128)(2,1)}, bf16[1024,256]{1,0:T(8,128)(2,1)}, u32[]{:S(2)}, u32[]{:S(2)}) %collective-permute-start.7) | collective-permute-done | bytes 524320 | tf_op jit(solution)/shard_map/ppermute | solution.py:136
  113.1 11.8 %collective-permute-done.9.refs_4_ = bf16[1024,256]{1,0:T(8,128)(2,1)} collective-permute-done((bf16[1024,256]{1,0:T(8,128)(2,1)}, bf16[1024,256]{1,0:T(8,128)(2,1)}, u32[]{:S(2)}, u32[]{:S(2)}) %collective-permute-start.9) | collective-permute-done | bytes 524320 | tf_op jit(solution)/shard_map/ppermute | solution.py:136
  126.8 1.6 collective-permute-start.31
  128.3 1.5 collective-permute-start.8
  130.9 1.5 collective-permute-start.13
  134.7 28.6 %collective-permute-done.13.refs_6_ = bf16[1024,256]{1,0:T(8,128)(2,1)S(1)} collective-permute-done((bf16[1024,256]{1,0:T(8,128)(2,1)}, bf16[1024,256]{1,0:T(8,128)(2,1)S(1)}, u32[]{:S(2)}, u32[]{:S(2)}) %collective-permute-start.13) | collective-permute-done | bytes 524320 | tf_op jit(solution)/shard_map/ppermute | solution.py:136
  163.4 1.5 collective-permute-start.6
  165.4 1.5 collective-permute-start.14
  166.9 1.5 collective-permute-start.15
  172.1 8.8 %shard_map.104.refs_17_ = f32[2048,2048]{1,0:T(8,128)} custom-call(s32[2]{0:T(128)S(1)} %pad_add_fusion.4.refs_0_, bf16[1024,256]{1,0:T(8,128)(2,1)S(1)} %copy-done.4, bf16[1024,256]{1,0:T(8,128)(2,1)} %collective-permute-done.5.refs_2_, bf16[1024,256]{1,0:T(8,128)(2,1)} %collective-permute-done.7.refs_3_, bf16[1024,256]{1,0:T(8,128)(2,1)} %collective-permute-done.9.refs_4_, ...), custom_call_target="tpu_custom_call" | custom-call | flops 4294967296 | bytes 12582912 | tf_op jit(solution)/shard_map/pallas_call | solution.py:115
  180.8 8.6 %shard_map.105.refs_17_ = f32[2048,2048]{1,0:T(8,128)} custom-call(s32[2]{0:T(128)S(1)} %pad_add_fusion.1.refs_0_, bf16[1024,256]{1,0:T(8,128)(2,1)S(1)} %copy-done.4, bf16[1024,256]{1,0:T(8,128)(2,1)} %collective-permute-done.5.refs_2_, bf16[1024,256]{1,0:T(8,128)(2,1)} %collective-permute-done.7.refs_3_, ...), custom_call_target="tpu_custom_call", output_to_operand_aliasing={{}: (17, {})} | custom-call | flops 4294967296 | bytes 12582912 | tf_op jit(solution)/shard_map/pallas_call | solution.py:115
  189.7 9.3 %collective-permute-done.14.refs_6_ = bf16[1024,256]{1,0:T(8,128)(2,1)S(1)} collective-permute-done((bf16[1024,256]{1,0:T(8,128)(2,1)S(1)}, bf16[1024,256]{1,0:T(8,128)(2,1)S(1)}, u32[]{:S(2)}, u32[]{:S(2)}) %collective-permute-start.14) | collective-permute-done | bytes 524320 | tf_op jit(solution)/shard_map/ppermute | solution.py:136
  199.0 8.1 %shard_map.106.refs_17_ = f32[2048,2048]{1,0:T(8,128)} custom-call(s32[2]{0:T(128)S(1)} %pad_add_fusion.3.refs_0_, bf16[1024,256]{1,0:T(8,128)(2,1)S(1)} %collective-permute-done.4.refs_1_, bf16[1024,256]{1,0:T(8,128)(2,1)S(1)} %collective-permute-done.6.refs_2_, ...), custom_call_target="tpu_custom_call", output_to_operand_aliasing={{}: (17, {})} | custom-call | flops 4294967296 | bytes 12582912 | tf_op jit(solution)/shard_map/pallas_call | solution.py:115
  207.1 7.3 %shard_map.107 = f32[2048,2048]{1,0:T(8,128)} custom-call(s32[2]{0:T(128)S(1)} %pad_add_fusion.2.refs_0_, bf16[1024,256]{1,0:T(8,128)(2,1)S(1)} %collective-permute-done.4.refs_1_, bf16[1024,256]{1,0:T(8,128)(2,1)S(1)} %collective-permute-done.6.refs_2_, bf16[1024,256]{1,0:T(8,128)(2,1)S(1)} %collective-permute-done.8.refs_3_, ...), custom_call_target="tpu_custom_call", output_to_operand_aliasing={{}: (17, {})} | custom-call | flops 4294967296 | bytes 12582912 | tf_op jit(solution)/shard_map/pallas_call | solution.py:115
  (77 shorter events, 23.8 us)
Async XLA Ops:
  1.9 28.0 %collective-permute-start.17 = (bf16[256,1024]{1,0:T(8,128)(2,1)S(1)}, bf16[256,1024]{1,0:T(8,128)(2,1)}, u32[]{:S(2)}, u32[]{:S(2)}) collective-permute-start(bf16[256,1024]{1,0:T(8,128)(2,1)S(1)} %get-tuple-element.14.refs_9_), channel_id=1, source_target_pairs={{0,8},{4,12},{8,0},{12,4},{16,24},{20,28},{24,16},{28,20},{1,9},{5... | collective-permute-start | bytes 1572872 | tf_op jit(solution)/shard_map/ppermute | solution.py:136
  2.0 37.9 %collective-permute-start.19 = (bf16[256,1024]{1,0:T(8,128)(2,1)S(1)}, bf16[256,1024]{1,0:T(8,128)(2,1)}, u32[]{:S(2)}, u32[]{:S(2)}) collective-permute-start(bf16[256,1024]{1,0:T(8,128)(2,1)S(1)} %get-tuple-element.14.refs_9_), channel_id=1, source_target_pairs={{0,16},{4,20},{8,24},{12,28},{16,0},{20,4},{24,8},{28,12},{1,17},{... | collective-permute-start | bytes 1572872 | tf_op jit(solution)/shard_map/ppermute | solution.py:136
  5.0 45.7 %collective-permute-start.21 = (bf16[256,1024]{1,0:T(8,128)(2,1)S(1)}, bf16[256,1024]{1,0:T(8,128)(2,1)}, u32[]{:S(2)}, u32[]{:S(2)}) collective-permute-start(bf16[256,1024]{1,0:T(8,128)(2,1)S(1)} %get-tuple-element.14.refs_9_), channel_id=1, source_target_pairs={{0,24},{4,28},{8,16},{12,20},{16,8},{20,12},{24,0},{28,4},{1,25},{... | collective-permute-start | bytes 1572872 | tf_op jit(solution)/shard_map/ppermute | solution.py:136
  8.5 44.2 %collective-permute-start.1 = (bf16[3,128,1024]{2,1,0:T(8,128)(2,1)S(1)}, bf16[3,128,1024]{2,1,0:T(8,128)(2,1)S(1)}, u32[]{:S(2)}, u32[]{:S(2)}) collective-permute-start(bf16[3,128,1024]{2,1,0:T(8,128)(2,1)S(1)} %pad_maximum_fusion), channel_id=1, source_target_pairs={{0,2},{2,0},{1,3},{3,1},{4,6},{6,4},{5,7},{7,5},{8,10},{10,8},{9,1... | collective-permute-start | bytes 2359304 | tf_op jit(solution)/shard_map/ppermute | solution.py:136
  13.4 15.0 %collective-permute-start = (s32[2,128]{0,1:T(8,128)S(1)}, s32[2,128]{0,1:T(8,128)S(1)}, u32[]{:S(2)}, u32[]{:S(2)}) collective-permute-start(s32[2,128]{0,1:T(8,128)S(1)} %broadcast_in_dim.2), channel_id=1, source_target_pairs={{0,2},{2,0},{1,3},{3,1},{4,6},{6,4},{5,7},{7,5},{8,10},{10,8},{9,1... | collective-permute-start | bytes 3080 | tf_op jit(solution)/shard_map/ppermute | solution.py:136
  28.4 23.8 %collective-permute-start.23 = (bf16[256,1024]{1,0:T(8,128)(2,1)S(1)}, bf16[256,1024]{1,0:T(8,128)(2,1)S(1)}, u32[]{:S(2)}, u32[]{:S(2)}) collective-permute-start(bf16[256,1024]{1,0:T(8,128)(2,1)S(1)} %get-tuple-element.14.refs_9_), channel_id=1, source_target_pairs={{0,4},{4,0},{8,12},{12,8},{16,20},{20,16},{24,28},{28,24},{1,5},{5... | collective-permute-start | bytes 1572872 | tf_op jit(solution)/shard_map/ppermute | solution.py:136
  30.0 22.8 %collective-permute-start.2 = (bf16[256,1024]{1,0:T(8,128)(2,1)S(1)}, bf16[256,1024]{1,0:T(8,128)(2,1)S(1)}, u32[]{:S(2)}, u32[]{:S(2)}) collective-permute-start(bf16[256,1024]{1,0:T(8,128)(2,1)S(1)} %constant_dynamic-slice_fusion), channel_id=1, source_target_pairs={{0,2},{2,0},{1,3},{3,1},{4,6},{6,4},{5,7},{7,5},{8,10},{10,8},{9,1... | collective-permute-start | bytes 1572872 | tf_op jit(solution)/shard_map/ppermute | solution.py:136
  39.9 13.4 %collective-permute-start.25 = (bf16[256,1024]{1,0:T(8,128)(2,1)}, bf16[256,1024]{1,0:T(8,128)(2,1)S(1)}, u32[]{:S(2)}, u32[]{:S(2)}) collective-permute-start(bf16[256,1024]{1,0:T(8,128)(2,1)} %collective-permute-done.17.refs_10_), channel_id=1, source_target_pairs={{0,4},{4,0},{8,12},{12,8},{16,20},{20,16},{24,28},{28,24},{1,5},{5... | collective-permute-start | bytes 1572872 | tf_op jit(solution)/shard_map/ppermute | solution.py:136
  50.7 15.2 %collective-permute-start.27 = (bf16[256,1024]{1,0:T(8,128)(2,1)}, bf16[256,1024]{1,0:T(8,128)(2,1)}, u32[]{:S(2)}, u32[]{:S(2)}) collective-permute-start(bf16[256,1024]{1,0:T(8,128)(2,1)} %collective-permute-done.19.refs_11_), channel_id=1, source_target_pairs={{0,4},{4,0},{8,12},{12,8},{16,20},{20,16},{24,28},{28,24},{1,5},{5... | collective-permute-start | bytes 1572872 | tf_op jit(solution)/shard_map/ppermute | solution.py:136
  52.2 22.6 %collective-permute-start.29 = (bf16[256,1024]{1,0:T(8,128)(2,1)}, bf16[256,1024]{1,0:T(8,128)(2,1)}, u32[]{:S(2)}, u32[]{:S(2)}) collective-permute-start(bf16[256,1024]{1,0:T(8,128)(2,1)} %collective-permute-done.21.refs_12_), channel_id=1, source_target_pairs={{0,4},{4,0},{8,12},{12,8},{16,20},{20,16},{24,28},{28,24},{1,5},{5... | collective-permute-start | bytes 1572872 | tf_op jit(solution)/shard_map/ppermute | solution.py:136
  52.7 24.2 %collective-permute-start.18 = (bf16[256,1024]{1,0:T(8,128)(2,1)}, bf16[256,1024]{1,0:T(8,128)(2,1)S(1)}, u32[]{:S(2)}, u32[]{:S(2)}) collective-permute-start(bf16[256,1024]{1,0:T(8,128)(2,1)} %collective-permute-done.17.refs_10_), channel_id=1, source_target_pairs={{0,1},{1,0},{2,3},{3,2},{4,5},{5,4},{6,7},{7,6},{8,9},{9,8},{10,11... | collective-permute-start | bytes 1572872 | tf_op jit(solution)/shard_map/ppermute | solution.py:136
  52.7 25.2 %collective-permute-start.20 = (bf16[256,1024]{1,0:T(8,128)(2,1)}, bf16[256,1024]{1,0:T(8,128)(2,1)S(1)}, u32[]{:S(2)}, u32[]{:S(2)}) collective-permute-start(bf16[256,1024]{1,0:T(8,128)(2,1)} %collective-permute-done.19.refs_11_), channel_id=1, source_target_pairs={{0,1},{1,0},{2,3},{3,2},{4,5},{5,4},{6,7},{7,6},{8,9},{9,8},{10,11... | collective-permute-start | bytes 1572872 | tf_op jit(solution)/shard_map/ppermute | solution.py:136
  54.6 23.9 %collective-permute-start.22 = (bf16[256,1024]{1,0:T(8,128)(2,1)}, bf16[256,1024]{1,0:T(8,128)(2,1)S(1)}, u32[]{:S(2)}, u32[]{:S(2)}) collective-permute-start(bf16[256,1024]{1,0:T(8,128)(2,1)} %collective-permute-done.21.refs_12_), channel_id=1, source_target_pairs={{0,1},{1,0},{2,3},{3,2},{4,5},{5,4},{6,7},{7,6},{8,9},{9,8},{10,11... | collective-permute-start | bytes 1572872 | tf_op jit(solution)/shard_map/ppermute | solution.py:136
  65.9 23.2 %collective-permute-start.24 = (bf16[256,1024]{1,0:T(8,128)(2,1)}, bf16[256,1024]{1,0:T(8,128)(2,1)S(1)}, u32[]{:S(2)}, u32[]{:S(2)}) collective-permute-start(bf16[256,1024]{1,0:T(8,128)(2,1)} %copy-done), channel_id=1, source_target_pairs={{0,1},{1,0},{2,3},{3,2},{4,5},{5,4},{6,7},{7,6},{8,9},{9,8},{10,11... | collective-permute-start | bytes 1572872 | tf_op jit(solution)/shard_map/ppermute | solution.py:136
  74.7 25.2 %collective-permute-start.5 = (bf16[1024,256]{1,0:T(8,128)(2,1)}, bf16[1024,256]{1,0:T(8,128)(2,1)}, u32[]{:S(2)}, u32[]{:S(2)}) collective-permute-start(bf16[1024,256]{1,0:T(8,128)(2,1)} %get-tuple-element.11.refs_1_), channel_id=1, source_target_pairs={{0,8},{4,12},{8,0},{12,4},{16,24},{20,28},{24,16},{28,20},{1,9},{5... | collective-permute-start | bytes 1572872 | tf_op jit(solution)/shard_map/ppermute | solution.py:136
  76.9 36.2 %collective-permute-start.7 = (bf16[1024,256]{1,0:T(8,128)(2,1)}, bf16[1024,256]{1,0:T(8,128)(2,1)}, u32[]{:S(2)}, u32[]{:S(2)}) collective-permute-start(bf16[1024,256]{1,0:T(8,128)(2,1)} %get-tuple-element.11.refs_1_), channel_id=1, source_target_pairs={{0,16},{4,20},{8,24},{12,28},{16,0},{20,4},{24,8},{28,12},{1,17},{... | collective-permute-start | bytes 1572872 | tf_op jit(solution)/shard_map/ppermute | solution.py:136
  78.0 46.9 %collective-permute-start.9 = (bf16[1024,256]{1,0:T(8,128)(2,1)}, bf16[1024,256]{1,0:T(8,128)(2,1)}, u32[]{:S(2)}, u32[]{:S(2)}) collective-permute-start(bf16[1024,256]{1,0:T(8,128)(2,1)} %get-tuple-element.11.refs_1_), channel_id=1, source_target_pairs={{0,24},{4,28},{8,16},{12,20},{16,8},{20,12},{24,0},{28,4},{1,25},{... | collective-permute-start | bytes 1572872 | tf_op jit(solution)/shard_map/ppermute | solution.py:136
  78.5 46.3 %collective-permute-start.11 = (bf16[1024,256]{1,0:T(8,128)(2,1)}, bf16[1024,256]{1,0:T(8,128)(2,1)}, u32[]{:S(2)}, u32[]{:S(2)}) collective-permute-start(bf16[1024,256]{1,0:T(8,128)(2,1)} %get-tuple-element.11.refs_1_), channel_id=1, source_target_pairs={{0,4},{4,0},{8,12},{12,8},{16,20},{20,16},{24,28},{28,24},{1,5},{5... | collective-permute-start | bytes 1572872 | tf_op jit(solution)/shard_map/ppermute | solution.py:136
  89.0 41.9 %collective-permute-start.3 = (bf16[3,128,1024]{2,1,0:T(8,128)(2,1)}, bf16[3,128,1024]{2,1,0:T(8,128)(2,1)S(1)}, u32[]{:S(2)}, u32[]{:S(2)}) collective-permute-start(bf16[3,128,1024]{2,1,0:T(8,128)(2,1)} %get-tuple-element.10), channel_id=1, source_target_pairs={{0,2},{2,0},{1,3},{3,1},{4,6},{6,4},{5,7},{7,5},{8,10},{10,8},{9,1... | collective-permute-start | bytes 2359304 | tf_op jit(solution)/shard_map/ppermute | solution.py:136
  100.0 26.8 %collective-permute-start.4 = (bf16[1024,256]{1,0:T(8,128)(2,1)}, bf16[1024,256]{1,0:T(8,128)(2,1)S(1)}, u32[]{:S(2)}, u32[]{:S(2)}) collective-permute-start(bf16[1024,256]{1,0:T(8,128)(2,1)} %get-tuple-element.11.refs_1_), channel_id=1, source_target_pairs={{0,2},{2,0},{1,3},{3,1},{4,6},{6,4},{5,7},{7,5},{8,10},{10,8},{9,1... | collective-permute-start | bytes 1572872 | tf_op jit(solution)/shard_map/ppermute | solution.py:136
  113.0 15.3 %collective-permute-start.26 = (bf16[256,1024]{1,0:T(8,128)(2,1)}, bf16[256,1024]{1,0:T(8,128)(2,1)S(1)}, u32[]{:S(2)}, u32[]{:S(2)}) collective-permute-start(bf16[256,1024]{1,0:T(8,128)(2,1)} %copy-done.2), channel_id=1, source_target_pairs={{0,1},{1,0},{2,3},{3,2},{4,5},{5,4},{6,7},{7,6},{8,9},{9,8},{10,11... | collective-permute-start | bytes 1572872 | tf_op jit(solution)/shard_map/ppermute | solution.py:136
  124.9 5.5 %collective-permute-start.30 = (bf16[256,1024]{1,0:T(8,128)(2,1)}, bf16[256,1024]{1,0:T(8,128)(2,1)S(1)}, u32[]{:S(2)}, u32[]{:S(2)}) collective-permute-start(bf16[256,1024]{1,0:T(8,128)(2,1)} %collective-permute-done.29.refs_16_), channel_id=1, source_target_pairs={{0,1},{1,0},{2,3},{3,2},{4,5},{5,4},{6,7},{7,6},{8,9},{9,8},{10,11... | collective-permute-start | bytes 1572872 | tf_op jit(solution)/shard_map/ppermute | solution.py:136
  126.8 38.1 %collective-permute-start.31 = (bf16[1024,256]{1,0:T(8,128)(2,1)}, bf16[1024,256]{1,0:T(8,128)(2,1)S(1)}, u32[]{:S(2)}, u32[]{:S(2)}) collective-permute-start(bf16[1024,256]{1,0:T(8,128)(2,1)} %collective-permute-done.7.refs_3_), channel_id=1, source_target_pairs={{0,4},{4,0},{8,12},{12,8},{16,20},{20,16},{24,28},{28,24},{1,5},{5... | collective-permute-start | bytes 1572872 | tf_op jit(solution)/shard_map/ppermute | solution.py:136
  128.3 38.6 %collective-permute-start.8 = (bf16[1024,256]{1,0:T(8,128)(2,1)}, bf16[1024,256]{1,0:T(8,128)(2,1)S(1)}, u32[]{:S(2)}, u32[]{:S(2)}) collective-permute-start(bf16[1024,256]{1,0:T(8,128)(2,1)} %collective-permute-done.7.refs_3_), channel_id=1, source_target_pairs={{0,2},{2,0},{1,3},{3,1},{4,6},{6,4},{5,7},{7,5},{8,10},{10,8},{9,1... | collective-permute-start | bytes 1572872 | tf_op jit(solution)/shard_map/ppermute | solution.py:136
  129.9 35.6 %collective-permute-start.32 = (bf16[1024,256]{1,0:T(8,128)(2,1)}, bf16[1024,256]{1,0:T(8,128)(2,1)S(1)}, u32[]{:S(2)}, u32[]{:S(2)}) collective-permute-start(bf16[1024,256]{1,0:T(8,128)(2,1)} %collective-permute-done.9.refs_4_), channel_id=1, source_target_pairs={{0,4},{4,0},{8,12},{12,8},{16,20},{20,16},{24,28},{28,24},{1,5},{5... | collective-permute-start | bytes 1572872 | tf_op jit(solution)/shard_map/ppermute | solution.py:136
  130.4 38.0 %collective-permute-start.10 = (bf16[1024,256]{1,0:T(8,128)(2,1)}, bf16[1024,256]{1,0:T(8,128)(2,1)S(1)}, u32[]{:S(2)}, u32[]{:S(2)}) collective-permute-start(bf16[1024,256]{1,0:T(8,128)(2,1)} %collective-permute-done.9.refs_4_), channel_id=1, source_target_pairs={{0,2},{2,0},{1,3},{3,1},{4,6},{6,4},{5,7},{7,5},{8,10},{10,8},{9,1... | collective-permute-start | bytes 1572872 | tf_op jit(solution)/shard_map/ppermute | solution.py:136
  130.9 32.4 %collective-permute-start.13 = (bf16[1024,256]{1,0:T(8,128)(2,1)}, bf16[1024,256]{1,0:T(8,128)(2,1)S(1)}, u32[]{:S(2)}, u32[]{:S(2)}) collective-permute-start(bf16[1024,256]{1,0:T(8,128)(2,1)} %collective-permute-done.5.refs_2_), channel_id=1, source_target_pairs={{0,4},{4,0},{8,12},{12,8},{16,20},{20,16},{24,28},{28,24},{1,5},{5... | collective-permute-start | bytes 1572872 | tf_op jit(solution)/shard_map/ppermute | solution.py:136
  163.4 26.1 %collective-permute-start.6 = (bf16[1024,256]{1,0:T(8,128)(2,1)}, bf16[1024,256]{1,0:T(8,128)(2,1)S(1)}, u32[]{:S(2)}, u32[]{:S(2)}) collective-permute-start(bf16[1024,256]{1,0:T(8,128)(2,1)} %collective-permute-done.5.refs_2_), channel_id=1, source_target_pairs={{0,2},{2,0},{1,3},{3,1},{4,6},{6,4},{5,7},{7,5},{8,10},{10,8},{9,1... | collective-permute-start | bytes 1572872 | tf_op jit(solution)/shard_map/ppermute | solution.py:136
  164.9 24.8 %collective-permute-start.12 = (bf16[1024,256]{1,0:T(8,128)(2,1)}, bf16[1024,256]{1,0:T(8,128)(2,1)S(1)}, u32[]{:S(2)}, u32[]{:S(2)}) collective-permute-start(bf16[1024,256]{1,0:T(8,128)(2,1)} %collective-permute-done.11.refs_5_), channel_id=1, source_target_pairs={{0,2},{2,0},{1,3},{3,1},{4,6},{6,4},{5,7},{7,5},{8,10},{10,8},{9,1... | collective-permute-start | bytes 1572872 | tf_op jit(solution)/shard_map/ppermute | solution.py:136
  165.4 33.6 %collective-permute-start.14 = (bf16[1024,256]{1,0:T(8,128)(2,1)S(1)}, bf16[1024,256]{1,0:T(8,128)(2,1)S(1)}, u32[]{:S(2)}, u32[]{:S(2)}) collective-permute-start(bf16[1024,256]{1,0:T(8,128)(2,1)S(1)} %collective-permute-done.13.refs_6_), channel_id=1, source_target_pairs={{0,2},{2,0},{1,3},{3,1},{4,6},{6,4},{5,7},{7,5},{8,10},{10,8},{9,1... | collective-permute-start | bytes 1572872 | tf_op jit(solution)/shard_map/ppermute | solution.py:136
  166.9 32.1 %collective-permute-start.15 = (bf16[1024,256]{1,0:T(8,128)(2,1)S(1)}, bf16[1024,256]{1,0:T(8,128)(2,1)S(1)}, u32[]{:S(2)}, u32[]{:S(2)}) collective-permute-start(bf16[1024,256]{1,0:T(8,128)(2,1)S(1)} %collective-permute-done.8.refs_3_), channel_id=1, source_target_pairs={{0,4},{4,0},{8,12},{12,8},{16,20},{20,16},{24,28},{28,24},{1,5},{5... | collective-permute-start | bytes 1572872 | tf_op jit(solution)/shard_map/ppermute | solution.py:136
  168.4 30.6 %collective-permute-start.16 = (bf16[1024,256]{1,0:T(8,128)(2,1)S(1)}, bf16[1024,256]{1,0:T(8,128)(2,1)S(1)}, u32[]{:S(2)}, u32[]{:S(2)}) collective-permute-start(bf16[1024,256]{1,0:T(8,128)(2,1)S(1)} %collective-permute-done.10.refs_4_), channel_id=1, source_target_pairs={{0,4},{4,0},{8,12},{12,8},{16,20},{20,16},{24,28},{28,24},{1,5},{5... | collective-permute-start | bytes 1572872 | tf_op jit(solution)/shard_map/ppermute | solution.py:136
  (9 other events, 45.1 us)

commit v3 on v1

--- a/solution.py
+++ b/solution.py
@@ -3,6 +3,8 @@
 import jax
 import jax.numpy as jnp
 from jax import lax
+from jax.experimental import pallas as pl
+from jax.experimental.pallas import tpu as pltpu
 from jax.sharding import PartitionSpec as P
 
 HEAD_DIM = 128
@@ -30,7 +32,450 @@
     return lax.ppermute(value, axis, [(source, source + steps) for source in range(initial, last)])
 
 
+NT = (((1,), (1,)), ((), ()))
+TN = (((0,), (0,)), ((), ()))
+NN = (((1,), (0,)), ((), ()))
+MIB = 2**20
+FLAG_ROWS = 16
+
+
+def dot(a, b, dims):
+    return lax.dot_general(a, b, dims, preferred_element_type=jnp.float32)
+
+
+def ordered(first, own, peer, axis):
+    return jnp.where(
+        first, jnp.concatenate([own, peer], axis=axis), jnp.concatenate([peer, own], axis=axis)
+    )
+
+
+def call(kernel, place, grid, inputs, outputs, cost, aliases=None, scratch=(), vmem=60):
+    flops, moved, exps = cost
+    return pl.pallas_call(
+        kernel,
+        grid_spec=pltpu.PrefetchScalarGridSpec(
+            num_scalar_prefetch=1,
+            grid=grid,
+            in_specs=[spec for _, spec in inputs],
+            out_specs=[spec for _, _, spec in outputs],
+            scratch_shapes=list(scratch),
+        ),
+        out_shape=[jax.ShapeDtypeStruct(shape, dtype) for shape, dtype, _ in outputs],
+        input_output_aliases=aliases or {},
+        compiler_params=pltpu.CompilerParams(vmem_limit_bytes=vmem * MIB),
+        cost_estimate=pl.CostEstimate(flops=flops, bytes_accessed=moved, transcendentals=exps),
+    )(place, *[array for array, _ in inputs])
+
+
+def live_flags(ids, count, shape):
+    row = lax.broadcasted_iota(jnp.int32, shape, 0)
+    found = jnp.zeros(shape, jnp.float32)
+    for slot in range(ALIGN):
+        alive = slot < count[0, 0]
+        found += jnp.where((row == ids[0, 0, slot]) & alive, 1.0, 0.0)
+    return found
+
+
+def prepare_kernel(place, q, k, v, ids, count, packed):
+    rows = q.shape[1]
+    for i, ref in enumerate((q, k, v)):
+        packed[i * rows : (i + 1) * rows] = ref[0]
+    packed[3 * rows :] = live_flags(ids, count, (FLAG_ROWS, q.shape[2])).astype(jnp.bfloat16)
+
+
+def head_of(first, own, packed, h):
+    at = slice(h * HEAD_DIM, (h + 1) * HEAD_DIM)
+    rows = own[0].shape[1]
+    return at, [
+        ordered(first, ref[0, :, at], packed[i * rows : (i + 1) * rows, at], 0)
+        for i, ref in enumerate(own)
+    ]
+
+
+def block_bias(first, packed, ids, count):
+    flags = packed.shape[0] - FLAG_ROWS
+    live = live_flags(ids, count, (FLAG_ROWS, SPAN))
+    live_peer = packed[flags:, :SPAN].astype(jnp.float32)
+    return jnp.where(ordered(first, live, live_peer, 1) > 0.5, 0.0, -1e30)
+
+
+def probabilities(scale, queries, keys, bias):
+    scores = dot(keys, queries, NT) * scale
+    scores = jnp.concatenate([scores[:BLOCK] + bias[0:1], scores[BLOCK:] + bias[1:2]], axis=0)
+    weights = jnp.exp(scores - jnp.max(scores, axis=0, keepdims=True))
+    return weights * (1.0 / jnp.sum(weights, axis=0, keepdims=True))
+
+
+def forward_kernel(scale, heads, place, q, k, v, packed, ids, count, context_out):
+    first = place[0] == 0
+    bias = block_bias(first, packed, ids, count)
+    for h in range(heads):
+        at, (queries, keys, values) = head_of(first, (q, k, v), packed, h)
+        prob = probabilities(scale, queries, keys, bias)
+        context_out[at, :] = dot(values, prob.astype(jnp.bfloat16), TN).astype(jnp.bfloat16)
+
+
+def backward_kernel(
+    scale, heads, place, q, k, v, packed, ids, count, cg_own, cg_peer, q_out, k_out, v_out, sent
+):
+    b16 = jnp.bfloat16
+    first = place[0] == 0
+    bias = block_bias(first, packed, ids, count)
+    for h in range(heads):
+        at, (queries, keys, values) = head_of(first, (q, k, v), packed, h)
+        cg = (cg_own[at, :].astype(jnp.float32) + cg_peer[at, :].astype(jnp.float32)).astype(b16)
+        prob = probabilities(scale, queries, keys, bias)
+        dprob = dot(values, cg, NN)
+        delta = jnp.sum(prob * dprob, axis=0, keepdims=True)
+        dscore = (prob * (dprob - delta)).astype(b16)
+        grads = (
+            (dot(dscore, keys, TN) * scale).astype(b16),
+            (dot(dscore, queries, NN) * scale).astype(b16),
+            dot(prob.astype(b16), cg, NT).astype(b16),
+        )
+        for i, (grad, out) in enumerate(zip(grads, (q_out, k_out, v_out))):
+            out[0, :, at] = jnp.where(first, grad[:SPAN], grad[SPAN:])
+            sent[i, :, at] = jnp.where(first, grad[SPAN:], grad[:SPAN])
+
+
+def place_kernel(place, received, q_in, k_in, v_in, q_out, k_out, v_out):
+    for i, out in enumerate((q_out, k_out, v_out)):
+        out[0] = received[i]
+
+
+def projection_kernel(half_tiles, place, grads, weight, sent, kept):
+    value = dot(weight[...], grads[0], NT).astype(jnp.bfloat16)
+
+    @pl.when(pl.program_id(0) < half_tiles)
+    def _():
+        sent[...] = value
+
+    @pl.when(pl.program_id(0) >= half_tiles)
+    def _():
+        kept[...] = value
+
+
+def weight_kernel(left_at, straight_at, crossed_at, place, *refs):
+    left, refs = refs[: len(left_at)], refs[len(left_at) :]
+    straight, refs = refs[: len(straight_at)], refs[len(straight_at) :]
+    crossed, refs = refs[: len(crossed_at)], refs[len(crossed_at) :]
+    out, panel, right, left_done, right_done = refs[-5:]
+    j = pl.program_id(0)
+    depth, tile = left[0].shape[1], out.shape[1]
+    per_half = crossed[1].shape[1] // tile
+
+    def fetch(step, start):
+        slot = lax.rem(step, 2)
+        for half, (source, source_at) in enumerate(((straight, straight_at), (crossed, crossed_at))):
+
+            @pl.when(step // per_half == half)
+            def _():
+                for i, (ref, at) in enumerate(zip(source, source_at)):
+                    column = lax.rem(step, per_half) * tile
+                    if i == 0:
+                        column += place[1 + half] * per_half * tile
+                    ref = ref if at is None else ref.at[at]
+                    copy = pltpu.make_async_copy(
+                        ref.at[:, pl.ds(pl.multiple_of(column, tile), tile)],
+                        right.at[slot, pl.ds(i * depth, depth)],
+                        right_done.at[slot, i],
+                    )
+                    copy.start() if start else copy.wait()
+
+    def gather_left(start):
+        for n, (ref, at) in enumerate(zip(left, left_at)):
+            i = n // 2
+
+            @pl.when(place[3] == n % 2)
+            def _():
+                copy = pltpu.make_async_copy(
+                    ref if at is None else ref.at[at],
+                    panel.at[:, pl.ds(i * depth, depth)],
+                    left_done.at[i],
+                )
+                copy.start() if start else copy.wait()
+
+    @pl.when(j == 0)
+    def _():
+        fetch(j, True)
+        gather_left(True)
+
+    @pl.when(j + 1 < pl.num_programs(0))
+    def _():
+        fetch(j + 1, True)
+
+    fetch(j, False)
+
+    @pl.when(j == 0)
+    def _():
+        gather_left(False)
+
+    out[...] = dot(panel[...], right[lax.rem(j, 2)], NN)
+
+
+def weight_rows(place, left, straight, crossed, held, shape):
+    def split(entries):
+        entries = [entry if isinstance(entry, tuple) else (entry, None) for entry in entries]
+        return [array for array, _ in entries], [at for _, at in entries]
+
+    count = len(left)
+    left, left_at = split([entry for pair in left for entry in pair])
+    straight, straight_at = split(straight)
+    crossed, crossed_at = split(crossed)
+    straight[0], crossed[0] = straight[0][0], crossed[0][0]
+    rows, depth = left[0].shape
+    columns = shape[1]
+    tile = 512
+    per_half = columns // 2 // tile
+    hbm = pl.BlockSpec(memory_space=pl.ANY)
+    inputs = [(array, hbm) for array in (*left, *straight, *crossed)]
+    aliases = {}
+    if held is not None:
+        inputs.append((held, hbm))
+        aliases = {len(inputs): 0}
+
+    def to(j, p):
+        return p[0], lax.rem(j, per_half) + jnp.where(j < per_half, p[1], p[2]) * per_half
+
+    return call(
+        lambda *refs: weight_kernel(left_at, straight_at, crossed_at, *refs),
+        place,
+        (2 * per_half,),
+        inputs,
+        [(shape, jnp.float32, pl.BlockSpec((rows, tile), to))],
+        (
+            2 * rows * depth * count * columns,
+            4 * rows * columns + 2 * count * depth * (rows + columns),
+            0,
+        ),
+        aliases,
+        [
+            pltpu.VMEM((rows, count * depth), jnp.bfloat16),
+            pltpu.VMEM((2, count * depth, tile), jnp.bfloat16),
+            pltpu.SemaphoreType.DMA((count,)),
+            pltpu.SemaphoreType.DMA((2, count)),
+        ],
+    )[0]
+
+
+def queue(axis, pairs, ordered_queue=True):
+    arrived = []
+
+    def send(value):
+        if arrived and ordered_queue:
+            value = lax.optimization_barrier((value, arrived[-1]))[0]
+        arrived.append(lax.ppermute(value, axis, pairs))
+        return arrived[-1]
+
+    return send
+
+
+def flipped(axis, bits, ordered_queue=True):
+    return queue(axis, [(i, i ^ bits) for i in range(lax.axis_size(axis))], ordered_queue)
+
+
+def middle_pairs():
+    pairs = []
+    for d in range(8):
+        for core in range(2):
+            other = (d ^ 6, core) if d // 2 in (1, 2) else (d, 1 - core)
+            pairs.append((2 * d + core, 2 * other[0] + other[1]))
+    return pairs
+
+
+def pick_kernel(place, *refs):
+    ends, middles, out, done = refs[:2], refs[2:4], refs[4], refs[5]
+    for i in range(2):
+        for chosen, source in ((0, ends[i]), (1, middles[i])):
+
+            @pl.when(place[0] == chosen)
+            def _():
+                pltpu.make_async_copy(source, out.at[i], done.at[i]).start()
+
+    for i in range(2):
+        pltpu.make_async_copy(ends[i], out.at[i], done.at[i]).wait()
+
+
+def paired(queries, key_states, value_states, out_grad, out_weight, align_ids, align_count):
+    b16 = jnp.bfloat16
+    i32 = jnp.int32
+    scale = 1.0 / math.sqrt(HEAD_DIM)
+    width = queries.shape[2]
+    half = width // 2
+    heads = half // HEAD_DIM
+    rows = queries.shape[1]
+    tokens, columns = out_grad.shape[1:]
+    y = lax.axis_index("span").astype(i32)
+    t = lax.axis_index("tensor").astype(i32)
+    z = lax.axis_index("dp").astype(i32) // 2
+    middle = (z == 1) | (z == 2)
+    place = y[None]
+    is_middle = middle.astype(i32)
+    send_x, send_y, send_core = flipped("dp", 1), flipped("span", 1), flipped("tensor", 1, False)
+    send_edge, send_middle = flipped("dp", 2), queue(("dp", "tensor"), middle_pairs())
+
+    def whole(shape):
+        return pl.BlockSpec(shape, lambda j, p: (0,) * len(shape))
+
+    def half_of(which):
+        return pl.BlockSpec((1, rows, half), lambda j, p: (0, 0, which(p[0])))
+
+    def after(value, *others):
+        return lax.optimization_barrier((value, *others))[0]
+
+    own_half, peer_half = half_of(lambda y: y), half_of(lambda y: 1 - y)
+    own = (queries, key_states, value_states)
+    smem = pl.BlockSpec(memory_space=pltpu.SMEM)
+    hbm = pl.BlockSpec(memory_space=pl.ANY)
+    packed_shape = (3 * rows + FLAG_ROWS, half)
+    (packed,) = call(
+        prepare_kernel,
+        place,
+        (1,),
+        [(v, peer_half) for v in own] + [(align_ids, smem), (align_count, smem)],
+        [(packed_shape, b16, whole(packed_shape))],
+        (0, 12 * rows * half, 0),
+    )
+    packed_sent = packed
+    packed = send_y(packed)
+
+    grad_half = lax.dynamic_slice_in_dim(out_grad[0], t * (columns // 2), columns // 2, axis=1)
+    grad_half = after(grad_half, packed_sent)
+    grad_x = send_x(grad_half)
+    grad_1 = send_edge(grad_half)
+    grad_2m = send_middle(grad_half)
+    tile = 512
+    half_tiles = half // tile
+    whole_grad = pl.BlockSpec((1, tokens, columns), lambda j, p: (0, 0, 0))
+    cg_sent, cg_own = call(
+        lambda *refs: projection_kernel(half_tiles, *refs),
+        place,
+        (2 * half_tiles,),
+        [
+            (out_grad, whole_grad),
+            (
+                out_weight,
+                pl.BlockSpec(
+                    (tile, columns),
+                    lambda j, p: (lax.rem(j + (1 - p[0]) * half_tiles, 2 * half_tiles), 0),
+                ),
+            ),
+        ],
+        [
+            (
+                (half, tokens),
+                b16,
+                pl.BlockSpec((tile, tokens), lambda j, p: (jnp.minimum(j, half_tiles - 1), 0)),
+            ),
+            (
+                (half, tokens),
+                b16,
+                pl.BlockSpec((tile, tokens), lambda j, p: (jnp.maximum(j - half_tiles, 0), 0)),
+            ),
+        ],
+        (2 * tokens * columns * width, 2 * columns * (tokens + width), 0),
+    )
+
+    own_in = [(v, own_half) for v in own]
+    cg_peer = send_y(cg_sent)
+    grad_1, grad_2m = lax.optimization_barrier((grad_1, grad_2m, cg_sent))[:2]
+    grad_2e = send_edge(grad_2m)
+    grad_3m = send_middle(grad_1)
+    grad_1x = send_x(grad_1)
+    packed_in = (after(packed, cg_sent), whole(packed_shape))
+    (context,) = call(
+        lambda *refs: forward_kernel(scale, heads, *refs),
+        place,
+        (1,),
+        own_in + [packed_in, (align_ids, smem), (align_count, smem)],
+        [((half, tokens), b16, whole((half, tokens)))],
+        (heads * 2**25, 3 * MIB, heads * 2**16),
+    )
+
+    context_x = send_x(context)
+    context_y = send_y(context)
+    near_1 = send_edge(context)
+    near_2m = send_middle(context)
+    grad_3e = send_edge(grad_3m)
+    near_2e = send_edge(near_2m)
+    near_3m = send_middle(near_1)
+    near_3e = send_edge(near_3m)
+    def pick(ends, middles):
+        shape = ends[0].shape
+        return call(
+            pick_kernel,
+            is_middle[None],
+            (1,),
+            [(array, hbm) for array in (*ends, *middles)],
+            [((2, *shape), b16, whole((2, *shape)))],
+            (0, 8 * shape[0] * shape[1], 0),
+            scratch=[pltpu.SemaphoreType.DMA((2,))],
+        )[0]
+
+    grad_p = pick((grad_2e, grad_3e), (grad_2m, grad_3m))
+    near_p = pick((near_2e, near_3e), (near_2m, near_3m))
+    grad_px = send_x(grad_p)
+    diagonal = send_y(context_x)
+    diagonal_1 = send_edge(diagonal)
+    diagonal_2m = send_middle(diagonal)
+    diagonal_2e = send_edge(diagonal_2m)
+    diagonal_3m = send_middle(diagonal_1)
+    diagonal_3e = send_edge(diagonal_3m)
+    near_1x, near_1y = send_x(near_1), send_y(near_1)
+    near_px, near_py = send_x(near_p), send_y(near_p)
+    grad_1c = send_core(grad_1)
+    grad_pc = send_core(grad_p)
+    grad_xc = send_core(grad_x)
+    grad_1xc = send_core(grad_1x)
+    grad_pxc = send_core(grad_px)
+
+    cg_shape = (half, tokens)
+    full = (1, rows, width)
+    sent_shape = (3, rows, half)
+    *outs, sent = call(
+        lambda *refs: backward_kernel(scale, heads, *refs),
+        place,
+        (1,),
+        own_in
+        + [packed_in, (align_ids, smem), (align_count, smem)]
+        + [(cg_own, whole(cg_shape)), (cg_peer, whole(cg_shape))],
+        [(full, b16, own_half)] * 3 + [(sent_shape, b16, whole(sent_shape))],
+        (heads * 2**26, 5 * MIB, heads * 2**16),
+    )
+    received = send_y(sent)
+    outs = call(
+        place_kernel,
+        place,
+        (1,),
+        [(received, whole(sent_shape))] + [(out, hbm) for out in outs],
+        [(full, b16, peer_half)] * 3,
+        (0, 12 * rows * half, 0),
+        {2 + i: i for i in range(3)},
+    )
+
+    shape = (width, columns)
+    def parts(first, second, pair, first_x, second_x, pair_x):
+        return [first, second, (pair, 0), (pair, 1), first_x, second_x, (pair_x, 0), (pair_x, 1)]
+
+    straight = parts(out_grad, grad_1, grad_p, grad_x, grad_1x, grad_px)
+    crossed = parts(out_grad, grad_1c, grad_pc, grad_xc, grad_1xc, grad_pxc)
+    near = [(c, c) for c in parts(context, near_1, near_p, context_x, near_1x, near_px)]
+    far = [(c, c) for c in (context_y, near_1y, (near_py, 0), (near_py, 1), diagonal, diagonal_1)]
+    far += [(diagonal_2e, diagonal_2m), (diagonal_3e, diagonal_3m)]
+    near_place = jnp.stack([y, t, 1 - t, is_middle])
+    far_place = jnp.stack([1 - y, t, 1 - t, is_middle])
+    grad = weight_rows(near_place, near, straight, crossed, None, shape)
+    *outs, grad = lax.optimization_barrier((*outs, grad))
+    grad = weight_rows(far_place, far, straight, crossed, grad, shape)
+    return (*outs, grad)
+
+
 def shards(queries, key_states, value_states, out_grad, out_weight, align_ids, align_count):
+    two_spans = lax.axis_size("span") == 2 and queries.shape[1] == SPAN == key_states.shape[1]
+    if two_spans and lax.axis_size("dp") == 8 and lax.axis_size("tensor") == 2:
+        return paired(
+            queries, key_states, value_states, out_grad, out_weight, align_ids, align_count
+        )
     f32 = jnp.float32
     b16 = jnp.bfloat16
     scale = 1.0 / math.sqrt(HEAD_DIM)

time: 283 us -> 160 us (0.57)
  waiting for transfers between devices: 155 us -> 52.8 us
  Pallas kernels: 0 us -> 56.1 us
  matrix products: 40.4 us -> 0 us
  starting transfers between devices: 11.8 us -> 42.2 us
  local copies, waits for them, and re-layouts: 32.3 us -> 3.62 us
  other arithmetic: 23.3 us -> 1.34 us
  between operations: 16.4 us -> 1.4 us
    all_gather x2 -> x0, waiting for transfers between devices: 90.3 us -> none  [the longest x1 90.3 us: shards(): lax.all_gather(flat_context, ('dp', 'span'), axis=0, tiled=True)]
    pallas_call x0 -> x9, Pallas kernels: none -> 56.1 us  [call(): pl.pallas_call(kernel, grid_spec=pltpu.PrefetchScalarGridSpec(num_scalar_...]
    dot_general x8 -> x0, matrix products: 40.4 us -> none  [the longest x1 24.3 us: shards(): lax.dot_general(all_context, all_grad, (((0,), (0,)), ((), ())), preferre...]
    ppermute x4 -> x33, starting transfers between devices: 11.7 us -> 42.2 us  [send(): arrived.append(lax.ppermute(value, axis, pairs))]
    ppermute x4 -> x33, waiting for transfers between devices: 65 us -> 52.8 us  [send(): arrived.append(lax.ppermute(value, axis, pairs))]
    another operation x6 -> x0, local copies, waits for them, and re-layouts: 11.1 us -> none  [the longest x2 7.44 us: shards(): jnp.stack([key_term, value_term])]
    scatter-add x1 -> x0, other arithmetic: 8.2 us -> none  [shards(): jnp.zeros((2, 3 * block_number, BLOCK, local_width), f32).at[:, flat_ids]]
    another operation x2, other arithmetic: 8.62 us -> 1.34 us  [the longest x1 0.78 us: paired(): near_place = jnp.stack([y, t, 1 - t, is_middle])]
  transfers between devices with their start and end apart: 7 -> 33, of which waited for: 5 -> 18; matrix products, arithmetic and copies ran while one was open for 22% -> 1% of each run, Pallas kernels for 0% -> 25%
where the time goes in v3:
time: 160 us; the launch traced here: 158 us
  Pallas kernels  56.1 us (35%)
  waiting for transfers between devices  52.8 us (33%)
  starting transfers between devices  42.2 us (26%)
  local copies, waits for them, and re-layouts  3.62 us (2%)
    pallas_call x9, Pallas kernels, call(): pl.pallas_call(kernel, grid_spec=pltpu.PrefetchScalarGridSpec(num_scalar_...  56.1 us
    ppermute x33, waiting for transfers between devices, send(): arrived.append(lax.ppermute(value, axis, pairs))  52.8 us
    ppermute x33, starting transfers between devices, send(): arrived.append(lax.ppermute(value, axis, pairs))  42.2 us
  transfers between devices with their start and end apart: 33, of which 18 were waited for; matrix products, arithmetic and copies ran while one was open for 1% of the time, Pallas kernels for 25%

profile of v3, /device:TPU:8, one launch (start us, length us, event | category | flops | bytes accessed | tf_op | source)
XLA Modules:
  0.0 157.5 jit_solution(4096096103569593734)
XLA Ops:
  2.4 2.1 %shard_map.102 = bf16[400,1024]{1,0:T(8,128)(2,1)} custom-call(s32[1]{0:T(128)} %bitcast.place.refs_0_, bf16[1,128,2048]{2,1,0:T(8,128)(2,1)} %refs_1_.5, bf16[1,128,2048]{2,1,0:T(8,128)(2,1)} %refs_2_.5, bf16[1,128,2048]{2,1,0:T(8,128)(2,1)} %refs_3_.3, s32[1,1,2]{2,1,0:T(1,128)} %refs_5_.3, s32[1,1]{1,0:T(1,128)S(6)} %copy.19.count.refs_6_), custom_call_target="tpu_custom_call" | custom-call | bytes 1572864 | tf_op jit(solution)/shard_map/pallas_call | solution.py:54
  4.4 1.6 %collective-permute-start.3 = (bf16[256,1024]{1,0:T(8,128)(2,1)S(1)}, bf16[256,1024]{1,0:T(8,128)(2,1)S(1)}, u32[]{:S(2)}, u32[]{:S(2)}) collective-permute-start(bf16[256,1024]{1,0:T(8,128)(2,1)S(1)} %dynamic-slice_bitcast_fusion), channel_id=1, source_target_pairs={{0,1},{1,0},{4,5},{5,4},{8,16},{9,17},{12,20},{13,21},{16,8},{17,9... | collective-permute-start | bytes 1572872 | tf_op jit(solution)/shard_map/ppermute | solution.py:267
  6.0 1.5 collective-permute-start
  7.5 6.8 %shard_map.103 = (bf16[1024,256]{1,0:T(8,128)(2,1)}, bf16[1024,256]{1,0:T(8,128)(2,1)}) custom-call(s32[1]{0:T(128)} %bitcast.place.refs_0_, bf16[1,256,2048]{2,1,0:T(8,128)(2,1)} %refs_1_.3, bf16[2048,2048]{1,0:T(8,128)(2,1)} %refs_2_.3), custom_call_target="tpu_custom_call" | custom-call | flops 2147483648 | bytes 9437184 | tf_op jit(solution)/shard_map/pallas_call | solution.py:54
  14.3 3.8 %collective-permute-done.3.refs_2_ = bf16[256,1024]{1,0:T(8,128)(2,1)S(1)} collective-permute-done((bf16[256,1024]{1,0:T(8,128)(2,1)S(1)}, bf16[256,1024]{1,0:T(8,128)(2,1)S(1)}, u32[]{:S(2)}, u32[]{:S(2)}) %collective-permute-start.3) | collective-permute-done | bytes 524320 | tf_op jit(solution)/shard_map/ppermute | solution.py:267
  21.2 2.2 %collective-permute-start.4 = (bf16[256,1024]{1,0:T(8,128)(2,1)S(1)}, bf16[256,1024]{1,0:T(8,128)(2,1)}, u32[]{:S(2)}, u32[]{:S(2)}) collective-permute-start(bf16[256,1024]{1,0:T(8,128)(2,1)S(1)} %collective-permute-done.2.refs_18_), channel_id=1, source_target_pairs={{0,1},{1,0},{4,5},{5,4},{8,16},{9,17},{12,20},{13,21},{16,8},{17,9... | collective-permute-start | bytes 1572872 | tf_op jit(solution)/shard_map/ppermute | solution.py:267
  23.4 2.5 %collective-permute-done.refs_4_ = bf16[400,1024]{1,0:T(8,128)(2,1)S(1)} collective-permute-done((bf16[400,1024]{1,0:T(8,128)(2,1)}, bf16[400,1024]{1,0:T(8,128)(2,1)S(1)}, u32[]{:S(2)}, u32[]{:S(2)}) %collective-permute-start) | collective-permute-done | bytes 819232 | tf_op jit(solution)/shard_map/ppermute | solution.py:267
  26.8 5.0 %shard_map.105.refs_1_.refs_2_ = bf16[1024,256]{1,0:T(8,128)(2,1)} custom-call(s32[1]{0:T(128)} %bitcast.place.refs_0_, bf16[1,128,2048]{2,1,0:T(8,128)(2,1)} %refs_1_.5, bf16[1,128,2048]{2,1,0:T(8,128)(2,1)} %refs_2_.5, bf16[1,128,2048]{2,1,0:T(8,128)(2,1)} %refs_3_.3, bf16[400,1024]{1,0:T(8,128)(2,1)} %copy-done.3, s32[1,1,2]{2,1,0:T(1,128)} %refs_5_.3, ...), custom_call_target="tpu_custom_call" | custom-call | flops 268435456 | bytes 3145728 | tf_op jit(solution)/shard_map/pallas_call | solution.py:54
  32.0 1.6 %collective-permute-start.7 = (bf16[1024,256]{1,0:T(8,128)(2,1)}, bf16[1024,256]{1,0:T(8,128)(2,1)S(1)}, u32[]{:S(2)}, u32[]{:S(2)}) collective-permute-start(bf16[1024,256]{1,0:T(8,128)(2,1)} %shard_map.105.refs_1_.refs_2_), channel_id=1, source_target_pairs={{0,8},{4,12},{8,0},{12,4},{16,24},{20,28},{24,16},{28,20},{1,9},{5... | collective-permute-start | bytes 1572872 | tf_op jit(solution)/shard_map/ppermute | solution.py:267
  35.1 1.5 collective-permute-start.1
  36.6 2.0 %collective-permute-start.5 = (bf16[1024,256]{1,0:T(8,128)(2,1)}, bf16[1024,256]{1,0:T(8,128)(2,1)S(1)}, u32[]{:S(2)}, u32[]{:S(2)}) collective-permute-start(bf16[1024,256]{1,0:T(8,128)(2,1)} %shard_map.105.refs_1_.refs_2_), channel_id=1, source_target_pairs={{0,1},{1,0},{4,5},{5,4},{8,16},{9,17},{12,20},{13,21},{16,8},{17,9... | collective-permute-start | bytes 1572872 | tf_op jit(solution)/shard_map/ppermute | solution.py:267
  38.6 6.0 %collective-permute-done.7.refs_3_.refs_4_ = bf16[1024,256]{1,0:T(8,128)(2,1)S(1)} collective-permute-done((bf16[1024,256]{1,0:T(8,128)(2,1)}, bf16[1024,256]{1,0:T(8,128)(2,1)S(1)}, u32[]{:S(2)}, u32[]{:S(2)}) %collective-permute-start.7) | collective-permute-done | bytes 524320 | tf_op jit(solution)/shard_map/ppermute | solution.py:267
  49.9 2.4 %collective-permute-start.10 = (bf16[1024,256]{1,0:T(8,128)(2,1)S(1)}, bf16[1024,256]{1,0:T(8,128)(2,1)}, u32[]{:S(2)}, u32[]{:S(2)}) collective-permute-start(bf16[1024,256]{1,0:T(8,128)(2,1)S(1)} %collective-permute-done.7.refs_3_.refs_4_), channel_id=1, source_target_pairs={{0,1},{1,0},{4,5},{5,4},{8,16},{9,17},{12,20},{13,21},{16,8},{17,9... | collective-permute-start | bytes 1572872 | tf_op jit(solution)/shard_map/ppermute | solution.py:267
  52.3 4.7 %collective-permute-done.8.refs_1_ = bf16[256,1024]{1,0:T(8,128)(2,1)} collective-permute-done((bf16[256,1024]{1,0:T(8,128)(2,1)}, bf16[256,1024]{1,0:T(8,128)(2,1)}, u32[]{:S(2)}, u32[]{:S(2)}) %collective-permute-start.8) | collective-permute-done | bytes 524320 | tf_op jit(solution)/shard_map/ppermute | solution.py:267
  58.4 2.2 %collective-permute-done.15.refs_1_.refs_2_ = bf16[1024,256]{1,0:T(8,128)(2,1)S(1)} collective-permute-done((bf16[1024,256]{1,0:T(8,128)(2,1)}, bf16[1024,256]{1,0:T(8,128)(2,1)S(1)}, u32[]{:S(2)}, u32[]{:S(2)}) %collective-permute-start.15) | collective-permute-done | bytes 524320 | tf_op jit(solution)/shard_map/ppermute | solution.py:267
  62.1 2.2 %shard_map.108.refs_19_.refs_20_ = bf16[2,256,1024]{2,1,0:T(8,128)(2,1)} custom-call(s32[1]{0:T(128)} %bitcast.1.place, bf16[256,1024]{1,0:T(8,128)(2,1)} %collective-permute-done.6.refs_0_, bf16[256,1024]{1,0:T(8,128)(2,1)} %collective-permute-done.8.refs_1_, bf16[256,1024]{1,0:T(8,128)(2,1)} %copy-done.12, bf16[256,1024]{1,0:T(8,128)(2,1)} %collective-permute-done.4.refs_3_), custom_call_target="tpu_custom_call" | custom-call | bytes 2097152 | tf_op jit(solution)/shard_map/pallas_call | solution.py:54
  64.8 4.0 %collective-permute-done.9.refs_0_ = bf16[1024,256]{1,0:T(8,128)(2,1)} collective-permute-done((bf16[1024,256]{1,0:T(8,128)(2,1)S(1)}, bf16[1024,256]{1,0:T(8,128)(2,1)}, u32[]{:S(2)}, u32[]{:S(2)}) %collective-permute-start.9) | collective-permute-done | bytes 524320 | tf_op jit(solution)/shard_map/ppermute | solution.py:267
  70.3 2.3 %collective-permute-done.16.refs_9_.refs_10_ = bf16[1024,256]{1,0:T(8,128)(2,1)S(1)} collective-permute-done((bf16[1024,256]{1,0:T(8,128)(2,1)S(1)}, bf16[1024,256]{1,0:T(8,128)(2,1)S(1)}, u32[]{:S(2)}, u32[]{:S(2)}) %collective-permute-start.16) | collective-permute-done | bytes 524320 | tf_op jit(solution)/shard_map/ppermute | solution.py:267
  74.1 2.4 %collective-permute-start.29 = (bf16[1024,256]{1,0:T(8,128)(2,1)S(1)}, bf16[1024,256]{1,0:T(8,128)(2,1)}, u32[]{:S(2)}, u32[]{:S(2)}) collective-permute-start(bf16[1024,256]{1,0:T(8,128)(2,1)S(1)} %collective-permute-done.16.refs_9_.refs_10_), channel_id=1, source_target_pairs={{0,1},{1,0},{4,5},{5,4},{8,16},{9,17},{12,20},{13,21},{16,8},{17,9... | collective-permute-start | bytes 1572872 | tf_op jit(solution)/shard_map/ppermute | solution.py:267
  76.5 4.7 %collective-permute-done.11.refs_1_ = bf16[1024,256]{1,0:T(8,128)(2,1)S(1)} collective-permute-done((bf16[1024,256]{1,0:T(8,128)(2,1)}, bf16[1024,256]{1,0:T(8,128)(2,1)S(1)}, u32[]{:S(2)}, u32[]{:S(2)}) %collective-permute-start.11) | collective-permute-done | bytes 524320 | tf_op jit(solution)/shard_map/ppermute | solution.py:267
  82.6 2.0 %collective-permute-done.20.refs_23_.refs_24_ = bf16[2,256,1024]{2,1,0:T(8,128)(2,1)S(1)} collective-permute-done((bf16[2,256,1024]{2,1,0:T(8,128)(2,1)}, bf16[2,256,1024]{2,1,0:T(8,128)(2,1)S(1)}, u32[]{:S(2)}, u32[]{:S(2)}) %collective-permute-start.20) | collective-permute-done | bytes 1048608 | tf_op jit(solution)/shard_map/ppermute | solution.py:267
  85.2 2.2 %shard_map.106.refs_5_.refs_6_.refs_7_.refs_8_ = bf16[2,1024,256]{2,1,0:T(8,128)(2,1)} custom-call(s32[1]{0:T(128)} %bitcast.1.place, bf16[1024,256]{1,0:T(8,128)(2,1)} %collective-permute-done.9.refs_0_, bf16[1024,256]{1,0:T(8,128)(2,1)} %copy-done.14, bf16[1024,256]{1,0:T(8,128)(2,1)} %copy-done.13, bf16[1024,256]{1,0:T(8,128)(2,1)} %collective-permute-done.10.refs_3_), custom_call_target="tpu_custom_call" | custom-call | bytes 2097152 | tf_op jit(solution)/shard_map/pallas_call | solution.py:54
  88.6 1.9 %collective-permute-done.28.refs_11_.refs_12_ = bf16[1024,256]{1,0:T(8,128)(2,1)} collective-permute-done((bf16[1024,256]{1,0:T(8,128)(2,1)S(1)}, bf16[1024,256]{1,0:T(8,128)(2,1)}, u32[]{:S(2)}, u32[]{:S(2)}) %collective-permute-start.28) | collective-permute-done | bytes 524320 | tf_op jit(solution)/shard_map/ppermute | solution.py:267
  90.4 1.9 %collective-permute-start.30 = (bf16[1024,256]{1,0:T(8,128)(2,1)}, bf16[1024,256]{1,0:T(8,128)(2,1)S(1)}, u32[]{:S(2)}, u32[]{:S(2)}) collective-permute-start(bf16[1024,256]{1,0:T(8,128)(2,1)} %collective-permute-done.29.refs_14_), channel_id=1, source_target_pairs={{0,8},{4,12},{8,0},{12,4},{16,24},{20,28},{24,16},{28,20},{1,9},{5... | collective-permute-start | bytes 1572872 | tf_op jit(solution)/shard_map/ppermute | solution.py:267
  92.3 4.0 %collective-permute-start.31 = (bf16[1024,256]{1,0:T(8,128)(2,1)}, bf16[1024,256]{1,0:T(8,128)(2,1)}, u32[]{:S(2)}, u32[]{:S(2)}) collective-permute-start(bf16[1024,256]{1,0:T(8,128)(2,1)} %collective-permute-done.28.refs_11_.refs_12_), channel_id=1, source_target_pairs={{0,1},{1,0},{4,5},{5,4},{8,16},{9,17},{12,20},{13,21},{16,8},{17,9... | collective-permute-start | bytes 1572872 | tf_op jit(solution)/shard_map/ppermute | solution.py:267
  97.5 4.4 %collective-permute-done.30.refs_13_ = bf16[1024,256]{1,0:T(8,128)(2,1)S(1)} collective-permute-done((bf16[1024,256]{1,0:T(8,128)(2,1)}, bf16[1024,256]{1,0:T(8,128)(2,1)S(1)}, u32[]{:S(2)}, u32[]{:S(2)}) %collective-permute-start.30) | collective-permute-done | bytes 524320 | tf_op jit(solution)/shard_map/ppermute | solution.py:267
  104.0 7.9 %collective-permute-done.18.refs_5_.refs_6_.refs_7_.refs_8_ = bf16[2,1024,256]{2,1,0:T(8,128)(2,1)S(1)} collective-permute-done((bf16[2,1024,256]{2,1,0:T(8,128)(2,1)}, bf16[2,1024,256]{2,1,0:T(8,128)(2,1)S(1)}, u32[]{:S(2)}, u32[]{:S(2)}) %collective-permute-start.18) | collective-permute-done | bytes 1048608 | tf_op jit(solution)/shard_map/ppermute | solution.py:267
  113.3 6.2 %shard_map.104 = (bf16[1,128,2048]{2,1,0:T(8,128)(2,1)}, bf16[1,128,2048]{2,1,0:T(8,128)(2,1)}, bf16[1,128,2048]{2,1,0:T(8,128)(2,1)}, bf16[3,128,1024]{2,1,0:T(8,128)(2,1)}) custom-call(s32[1]{0:T(128)} %bitcast.place.refs_0_, bf16[1,128,2048]{2,1,0:T(8,128)(2,1)} %refs_1_.5, bf16[1,128,2048]{2,1,0:T(8,128)(2,1)} %refs_2_.5, bf16[1,128,2048]{2,1,0:T(8,128)(2,1)} %refs_3_.3, ...), custom_call_target="tpu_custom_call" | custom-call | flops 536870912 | bytes 5242880 | tf_op jit(solution)/shard_map/pallas_call | solution.py:54
  121.6 2.2 %collective-permute-done.22.refs_13_.refs_14_.refs_15_.refs_16_ = bf16[2,1024,256]{2,1,0:T(8,128)(2,1)} collective-permute-done((bf16[2,1024,256]{2,1,0:T(8,128)(2,1)}, bf16[2,1024,256]{2,1,0:T(8,128)(2,1)}, u32[]{:S(2)}, u32[]{:S(2)}) %collective-permute-start.22) | collective-permute-done | bytes 1048608 | tf_op jit(solution)/shard_map/ppermute | solution.py:267
  123.9 14.8 %shard_map.109.refs_33_ = f32[2048,2048]{1,0:T(8,128)} custom-call(s32[4]{0:T(128)} %add_add_fusion.refs_0_, bf16[1024,256]{1,0:T(8,128)(2,1)} %shard_map.105.refs_1_.refs_2_, bf16[1024,256]{1,0:T(8,128)(2,1)} %shard_map.105.refs_1_.refs_2_, bf16[1024,256]{1,0:T(8,128)(2,1)} %copy-done.6, bf16[1024,256]{1,0:T(8,128)(2,1)} %copy-done.6, ...), custom_call_target="tpu_custom_call" | custom-call | flops 8589934592 | bytes 20971520 | tf_op jit(solution)/shard_map/pallas_call | solution.py:54
  140.0 2.0 %shard_map.107 = (bf16[1,128,2048]{2,1,0:T(8,128)(2,1)}, bf16[1,128,2048]{2,1,0:T(8,128)(2,1)}, bf16[1,128,2048]{2,1,0:T(8,128)(2,1)}) custom-call(s32[1]{0:T(128)} %bitcast.place.refs_0_, bf16[3,128,1024]{2,1,0:T(8,128)(2,1)} %collective-permute-done.19.received, ...), custom_call_target="tpu_custom_call", output_to_operand_aliasing={{0}: (2, {}), {1}: (3, {}), {2}: (4, {})} | custom-call | bytes 1572864 | tf_op jit(solution)/shard_map/pallas_call | solution.py:54
  142.8 14.8 %shard_map.110 = f32[2048,2048]{1,0:T(8,128)} custom-call(s32[4]{0:T(128)} %add_add_fusion.1.refs_0_, bf16[1024,256]{1,0:T(8,128)(2,1)} %copy-done.7, bf16[1024,256]{1,0:T(8,128)(2,1)} %copy-done.7, bf16[1024,256]{1,0:T(8,128)(2,1)} %collective-permute-done.17.refs_3_.refs_4_, ...), custom_call_target="tpu_custom_call", output_to_operand_aliasing={{}: (33, {})} | custom-call | flops 8589934592 | bytes 20971520 | tf_op jit(solution)/shard_map/pallas_call | solution.py:54
  (76 shorter events, 30.5 us)
Async XLA Ops:
  4.4 13.7 %collective-permute-start.3 = (bf16[256,1024]{1,0:T(8,128)(2,1)S(1)}, bf16[256,1024]{1,0:T(8,128)(2,1)S(1)}, u32[]{:S(2)}, u32[]{:S(2)}) collective-permute-start(bf16[256,1024]{1,0:T(8,128)(2,1)S(1)} %dynamic-slice_bitcast_fusion), channel_id=1, source_target_pairs={{0,1},{1,0},{4,5},{5,4},{8,16},{9,17},{12,20},{13,21},{16,8},{17,9... | collective-permute-start | bytes 1572872 | tf_op jit(solution)/shard_map/ppermute | solution.py:267
  6.0 13.4 %collective-permute-start.2 = (bf16[256,1024]{1,0:T(8,128)(2,1)S(1)}, bf16[256,1024]{1,0:T(8,128)(2,1)S(1)}, u32[]{:S(2)}, u32[]{:S(2)}) collective-permute-start(bf16[256,1024]{1,0:T(8,128)(2,1)S(1)} %dynamic-slice_bitcast_fusion), channel_id=1, source_target_pairs={{0,8},{4,12},{8,0},{12,4},{16,24},{20,28},{24,16},{28,20},{1,9},{5... | collective-permute-start | bytes 1572872 | tf_op jit(solution)/shard_map/ppermute | solution.py:267
  6.0 19.9 %collective-permute-start = (bf16[400,1024]{1,0:T(8,128)(2,1)}, bf16[400,1024]{1,0:T(8,128)(2,1)S(1)}, u32[]{:S(2)}, u32[]{:S(2)}) collective-permute-start(bf16[400,1024]{1,0:T(8,128)(2,1)} %shard_map.102), channel_id=1, source_target_pairs={{0,2},{2,0},{1,3},{3,1},{4,6},{6,4},{5,7},{7,5},{8,10},{10,8},{9,1... | collective-permute-start | bytes 2457608 | tf_op jit(solution)/shard_map/ppermute | solution.py:267
  19.4 12.6 %collective-permute-start.6 = (bf16[256,1024]{1,0:T(8,128)(2,1)S(1)}, bf16[256,1024]{1,0:T(8,128)(2,1)}, u32[]{:S(2)}, u32[]{:S(2)}) collective-permute-start(bf16[256,1024]{1,0:T(8,128)(2,1)S(1)} %collective-permute-done.3.refs_2_), channel_id=1, source_target_pairs={{0,8},{4,12},{8,0},{12,4},{16,24},{20,28},{24,16},{28,20},{1,9},{5... | collective-permute-start | bytes 1572872 | tf_op jit(solution)/shard_map/ppermute | solution.py:267
  19.7 13.9 %collective-permute-start.12 = (bf16[256,1024]{1,0:T(8,128)(2,1)S(1)}, bf16[256,1024]{1,0:T(8,128)(2,1)}, u32[]{:S(2)}, u32[]{:S(2)}) collective-permute-start(bf16[256,1024]{1,0:T(8,128)(2,1)S(1)} %dynamic-slice_bitcast_fusion), channel_id=1, source_target_pairs={{0,4},{4,0},{8,12},{12,8},{16,20},{20,16},{24,28},{28,24},{1,5},{5... | collective-permute-start | bytes 1572872 | tf_op jit(solution)/shard_map/ppermute | solution.py:267
  21.2 15.4 %collective-permute-start.4 = (bf16[256,1024]{1,0:T(8,128)(2,1)S(1)}, bf16[256,1024]{1,0:T(8,128)(2,1)}, u32[]{:S(2)}, u32[]{:S(2)}) collective-permute-start(bf16[256,1024]{1,0:T(8,128)(2,1)S(1)} %collective-permute-done.2.refs_18_), channel_id=1, source_target_pairs={{0,1},{1,0},{4,5},{5,4},{8,16},{9,17},{12,20},{13,21},{16,8},{17,9... | collective-permute-start | bytes 1572872 | tf_op jit(solution)/shard_map/ppermute | solution.py:267
  32.0 12.7 %collective-permute-start.7 = (bf16[1024,256]{1,0:T(8,128)(2,1)}, bf16[1024,256]{1,0:T(8,128)(2,1)S(1)}, u32[]{:S(2)}, u32[]{:S(2)}) collective-permute-start(bf16[1024,256]{1,0:T(8,128)(2,1)} %shard_map.105.refs_1_.refs_2_), channel_id=1, source_target_pairs={{0,8},{4,12},{8,0},{12,4},{16,24},{20,28},{24,16},{28,20},{1,9},{5... | collective-permute-start | bytes 1572872 | tf_op jit(solution)/shard_map/ppermute | solution.py:267
  33.6 12.5 %collective-permute-start.13 = (bf16[256,1024]{1,0:T(8,128)(2,1)S(1)}, bf16[256,1024]{1,0:T(8,128)(2,1)S(1)}, u32[]{:S(2)}, u32[]{:S(2)}) collective-permute-start(bf16[256,1024]{1,0:T(8,128)(2,1)S(1)} %collective-permute-done.2.refs_18_), channel_id=1, source_target_pairs={{0,4},{4,0},{8,12},{12,8},{16,20},{20,16},{24,28},{28,24},{1,5},{5... | collective-permute-start | bytes 1572872 | tf_op jit(solution)/shard_map/ppermute | solution.py:267
  35.1 13.3 %collective-permute-start.1 = (bf16[1024,256]{1,0:T(8,128)(2,1)}, bf16[1024,256]{1,0:T(8,128)(2,1)}, u32[]{:S(2)}, u32[]{:S(2)}) collective-permute-start(bf16[1024,256]{1,0:T(8,128)(2,1)} %get-tuple-element.48), channel_id=1, source_target_pairs={{0,2},{2,0},{1,3},{3,1},{4,6},{6,4},{5,7},{7,5},{8,10},{10,8},{9,1... | collective-permute-start | bytes 1572872 | tf_op jit(solution)/shard_map/ppermute | solution.py:267
  36.6 13.3 %collective-permute-start.5 = (bf16[1024,256]{1,0:T(8,128)(2,1)}, bf16[1024,256]{1,0:T(8,128)(2,1)S(1)}, u32[]{:S(2)}, u32[]{:S(2)}) collective-permute-start(bf16[1024,256]{1,0:T(8,128)(2,1)} %shard_map.105.refs_1_.refs_2_), channel_id=1, source_target_pairs={{0,1},{1,0},{4,5},{5,4},{8,16},{9,17},{12,20},{13,21},{16,8},{17,9... | collective-permute-start | bytes 1572872 | tf_op jit(solution)/shard_map/ppermute | solution.py:267
  44.6 12.3 %collective-permute-start.8 = (bf16[256,1024]{1,0:T(8,128)(2,1)}, bf16[256,1024]{1,0:T(8,128)(2,1)}, u32[]{:S(2)}, u32[]{:S(2)}) collective-permute-start(bf16[256,1024]{1,0:T(8,128)(2,1)} %collective-permute-done.4.refs_3_), channel_id=1, source_target_pairs={{0,8},{4,12},{8,0},{12,4},{16,24},{20,28},{24,16},{28,20},{1,9},{5... | collective-permute-start | bytes 1572872 | tf_op jit(solution)/shard_map/ppermute | solution.py:267
  46.9 11.5 %collective-permute-start.14 = (bf16[1024,256]{1,0:T(8,128)(2,1)}, bf16[1024,256]{1,0:T(8,128)(2,1)S(1)}, u32[]{:S(2)}, u32[]{:S(2)}) collective-permute-start(bf16[1024,256]{1,0:T(8,128)(2,1)} %shard_map.105.refs_1_.refs_2_), channel_id=1, source_target_pairs={{0,4},{4,0},{8,12},{12,8},{16,20},{20,16},{24,28},{28,24},{1,5},{5... | collective-permute-start | bytes 1572872 | tf_op jit(solution)/shard_map/ppermute | solution.py:267
  48.4 12.2 %collective-permute-start.15 = (bf16[1024,256]{1,0:T(8,128)(2,1)}, bf16[1024,256]{1,0:T(8,128)(2,1)S(1)}, u32[]{:S(2)}, u32[]{:S(2)}) collective-permute-start(bf16[1024,256]{1,0:T(8,128)(2,1)} %shard_map.105.refs_1_.refs_2_), channel_id=1, source_target_pairs={{0,2},{2,0},{1,3},{3,1},{4,6},{6,4},{5,7},{7,5},{8,10},{10,8},{9,1... | collective-permute-start | bytes 1572872 | tf_op jit(solution)/shard_map/ppermute | solution.py:267
  49.9 14.9 %collective-permute-start.10 = (bf16[1024,256]{1,0:T(8,128)(2,1)S(1)}, bf16[1024,256]{1,0:T(8,128)(2,1)}, u32[]{:S(2)}, u32[]{:S(2)}) collective-permute-start(bf16[1024,256]{1,0:T(8,128)(2,1)S(1)} %collective-permute-done.7.refs_3_.refs_4_), channel_id=1, source_target_pairs={{0,1},{1,0},{4,5},{5,4},{8,16},{9,17},{12,20},{13,21},{16,8},{17,9... | collective-permute-start | bytes 1572872 | tf_op jit(solution)/shard_map/ppermute | solution.py:267
  56.9 11.9 %collective-permute-start.9 = (bf16[1024,256]{1,0:T(8,128)(2,1)S(1)}, bf16[1024,256]{1,0:T(8,128)(2,1)}, u32[]{:S(2)}, u32[]{:S(2)}) collective-permute-start(bf16[1024,256]{1,0:T(8,128)(2,1)S(1)} %collective-permute-done.5.refs_2_), channel_id=1, source_target_pairs={{0,8},{4,12},{8,0},{12,4},{16,24},{20,28},{24,16},{28,20},{1,9},{5... | collective-permute-start | bytes 1572872 | tf_op jit(solution)/shard_map/ppermute | solution.py:267
  60.6 12.0 %collective-permute-start.16 = (bf16[1024,256]{1,0:T(8,128)(2,1)S(1)}, bf16[1024,256]{1,0:T(8,128)(2,1)S(1)}, u32[]{:S(2)}, u32[]{:S(2)}) collective-permute-start(bf16[1024,256]{1,0:T(8,128)(2,1)S(1)} %collective-permute-done.14.refs_9_.refs_10_), channel_id=1, source_target_pairs={{0,2},{2,0},{1,3},{3,1},{4,6},{6,4},{5,7},{7,5},{8,10},{10,8},{9,1... | collective-permute-start | bytes 1572872 | tf_op jit(solution)/shard_map/ppermute | solution.py:267
  64.3 20.2 %collective-permute-start.20 = (bf16[2,256,1024]{2,1,0:T(8,128)(2,1)}, bf16[2,256,1024]{2,1,0:T(8,128)(2,1)S(1)}, u32[]{:S(2)}, u32[]{:S(2)}) collective-permute-start(bf16[2,256,1024]{2,1,0:T(8,128)(2,1)} %shard_map.108.refs_19_.refs_20_), channel_id=1, source_target_pairs={{0,4},{4,0},{8,12},{12,8},{16,20},{20,16},{24,28},{28,24},{1,5},{5... | collective-permute-start | bytes 3145736 | tf_op jit(solution)/shard_map/ppermute | solution.py:267
  68.8 12.3 %collective-permute-start.11 = (bf16[1024,256]{1,0:T(8,128)(2,1)}, bf16[1024,256]{1,0:T(8,128)(2,1)S(1)}, u32[]{:S(2)}, u32[]{:S(2)}) collective-permute-start(bf16[1024,256]{1,0:T(8,128)(2,1)} %collective-permute-done.10.refs_3_), channel_id=1, source_target_pairs={{0,8},{4,12},{8,0},{12,4},{16,24},{20,28},{24,16},{28,20},{1,9},{5... | collective-permute-start | bytes 1572872 | tf_op jit(solution)/shard_map/ppermute | solution.py:267
  72.6 14.9 %collective-permute-start.17 = (bf16[1024,256]{1,0:T(8,128)(2,1)S(1)}, bf16[1024,256]{1,0:T(8,128)(2,1)}, u32[]{:S(2)}, u32[]{:S(2)}) collective-permute-start(bf16[1024,256]{1,0:T(8,128)(2,1)S(1)} %collective-permute-done.7.refs_3_.refs_4_), channel_id=1, source_target_pairs={{0,2},{2,0},{1,3},{3,1},{4,6},{6,4},{5,7},{7,5},{8,10},{10,8},{9,1... | collective-permute-start | bytes 1572872 | tf_op jit(solution)/shard_map/ppermute | solution.py:267
  74.1 14.5 %collective-permute-start.29 = (bf16[1024,256]{1,0:T(8,128)(2,1)S(1)}, bf16[1024,256]{1,0:T(8,128)(2,1)}, u32[]{:S(2)}, u32[]{:S(2)}) collective-permute-start(bf16[1024,256]{1,0:T(8,128)(2,1)S(1)} %collective-permute-done.16.refs_9_.refs_10_), channel_id=1, source_target_pairs={{0,1},{1,0},{4,5},{5,4},{8,16},{9,17},{12,20},{13,21},{16,8},{17,9... | collective-permute-start | bytes 1572872 | tf_op jit(solution)/shard_map/ppermute | solution.py:267
  81.1 9.3 %collective-permute-start.28 = (bf16[1024,256]{1,0:T(8,128)(2,1)S(1)}, bf16[1024,256]{1,0:T(8,128)(2,1)}, u32[]{:S(2)}, u32[]{:S(2)}) collective-permute-start(bf16[1024,256]{1,0:T(8,128)(2,1)S(1)} %collective-permute-done.16.refs_9_.refs_10_), channel_id=1, source_target_pairs={{0,8},{4,12},{8,0},{12,4},{16,24},{20,28},{24,16},{28,20},{1,9},{5... | collective-permute-start | bytes 1572872 | tf_op jit(solution)/shard_map/ppermute | solution.py:267
  82.6 14.5 %collective-permute-start.25 = (bf16[256,1024]{1,0:T(8,128)(2,1)}, bf16[256,1024]{1,0:T(8,128)(2,1)}, u32[]{:S(2)}, u32[]{:S(2)}) collective-permute-start(bf16[256,1024]{1,0:T(8,128)(2,1)} %collective-permute-done.12.refs_21_), channel_id=1, source_target_pairs={{0,1},{1,0},{2,3},{3,2},{4,5},{5,4},{6,7},{7,6},{8,9},{9,8},{10,11... | collective-permute-start | bytes 1572872 | tf_op jit(solution)/shard_map/ppermute | solution.py:267
  84.6 12.4 %collective-permute-start.21 = (bf16[1024,256]{1,0:T(8,128)(2,1)S(1)}, bf16[1024,256]{1,0:T(8,128)(2,1)}, u32[]{:S(2)}, u32[]{:S(2)}) collective-permute-start(bf16[1024,256]{1,0:T(8,128)(2,1)S(1)} %collective-permute-done.7.refs_3_.refs_4_), channel_id=1, source_target_pairs={{0,4},{4,0},{8,12},{12,8},{16,20},{20,16},{24,28},{28,24},{1,5},{5... | collective-permute-start | bytes 1572872 | tf_op jit(solution)/shard_map/ppermute | solution.py:267
  87.4 24.4 %collective-permute-start.18 = (bf16[2,1024,256]{2,1,0:T(8,128)(2,1)}, bf16[2,1024,256]{2,1,0:T(8,128)(2,1)S(1)}, u32[]{:S(2)}, u32[]{:S(2)}) collective-permute-start(bf16[2,1024,256]{2,1,0:T(8,128)(2,1)} %shard_map.106.refs_5_.refs_6_.refs_7_.refs_8_), channel_id=1, source_target_pairs={{0,2},{2,0},{1,3},{3,1},{4,6},{6,4},{5,7},{7,5},{8,10},{10,8},{9,1... | collective-permute-start | bytes 3145736 | tf_op jit(solution)/shard_map/ppermute | solution.py:267
  90.4 11.5 %collective-permute-start.30 = (bf16[1024,256]{1,0:T(8,128)(2,1)}, bf16[1024,256]{1,0:T(8,128)(2,1)S(1)}, u32[]{:S(2)}, u32[]{:S(2)}) collective-permute-start(bf16[1024,256]{1,0:T(8,128)(2,1)} %collective-permute-done.29.refs_14_), channel_id=1, source_target_pairs={{0,8},{4,12},{8,0},{12,4},{16,24},{20,28},{24,16},{28,20},{1,9},{5... | collective-permute-start | bytes 1572872 | tf_op jit(solution)/shard_map/ppermute | solution.py:267
  92.3 11.7 %collective-permute-start.31 = (bf16[1024,256]{1,0:T(8,128)(2,1)}, bf16[1024,256]{1,0:T(8,128)(2,1)}, u32[]{:S(2)}, u32[]{:S(2)}) collective-permute-start(bf16[1024,256]{1,0:T(8,128)(2,1)} %collective-permute-done.28.refs_11_.refs_12_), channel_id=1, source_target_pairs={{0,1},{1,0},{4,5},{5,4},{8,16},{9,17},{12,20},{13,21},{16,8},{17,9... | collective-permute-start | bytes 1572872 | tf_op jit(solution)/shard_map/ppermute | solution.py:267
  97.0 24.6 %collective-permute-start.24 = (bf16[2,256,1024]{2,1,0:T(8,128)(2,1)}, bf16[2,256,1024]{2,1,0:T(8,128)(2,1)S(1)}, u32[]{:S(2)}, u32[]{:S(2)}) collective-permute-start(bf16[2,256,1024]{2,1,0:T(8,128)(2,1)} %shard_map.108.refs_19_.refs_20_), channel_id=1, source_target_pairs={{0,1},{1,0},{2,3},{3,2},{4,5},{5,4},{6,7},{7,6},{8,9},{9,8},{10,11... | collective-permute-start | bytes 3145736 | tf_op jit(solution)/shard_map/ppermute | solution.py:267
  97.0 24.6 %collective-permute-start.27 = (bf16[2,256,1024]{2,1,0:T(8,128)(2,1)S(1)}, bf16[2,256,1024]{2,1,0:T(8,128)(2,1)}, u32[]{:S(2)}, u32[]{:S(2)}) collective-permute-start(bf16[2,256,1024]{2,1,0:T(8,128)(2,1)S(1)} %collective-permute-done.20.refs_23_.refs_24_), channel_id=1, source_target_pairs={{0,1},{1,0},{2,3},{3,2},{4,5},{5,4},{6,7},{7,6},{8,9},{9,8},{10,11... | collective-permute-start | bytes 3145736 | tf_op jit(solution)/shard_map/ppermute | solution.py:267
  101.9 22.0 %collective-permute-start.22 = (bf16[2,1024,256]{2,1,0:T(8,128)(2,1)}, bf16[2,1024,256]{2,1,0:T(8,128)(2,1)}, u32[]{:S(2)}, u32[]{:S(2)}) collective-permute-start(bf16[2,1024,256]{2,1,0:T(8,128)(2,1)} %shard_map.106.refs_5_.refs_6_.refs_7_.refs_8_), channel_id=1, source_target_pairs={{0,4},{4,0},{8,12},{12,8},{16,20},{20,16},{24,28},{28,24},{1,5},{5... | collective-permute-start | bytes 3145736 | tf_op jit(solution)/shard_map/ppermute | solution.py:267
  104.0 15.5 %collective-permute-start.23 = (bf16[256,1024]{1,0:T(8,128)(2,1)}, bf16[256,1024]{1,0:T(8,128)(2,1)}, u32[]{:S(2)}, u32[]{:S(2)}) collective-permute-start(bf16[256,1024]{1,0:T(8,128)(2,1)} %copy-done.4), channel_id=1, source_target_pairs={{0,1},{1,0},{2,3},{3,2},{4,5},{5,4},{6,7},{7,6},{8,9},{9,8},{10,11... | collective-permute-start | bytes 1572872 | tf_op jit(solution)/shard_map/ppermute | solution.py:267
  119.5 22.5 %collective-permute-start.32 = (bf16[1024,256]{1,0:T(8,128)(2,1)}, bf16[1024,256]{1,0:T(8,128)(2,1)S(1)}, u32[]{:S(2)}, u32[]{:S(2)}) collective-permute-start(bf16[1024,256]{1,0:T(8,128)(2,1)} %collective-permute-done.31.refs_16_), channel_id=1, source_target_pairs={{0,8},{4,12},{8,0},{12,4},{16,24},{20,28},{24,16},{28,20},{1,9},{5... | collective-permute-start | bytes 1572872 | tf_op jit(solution)/shard_map/ppermute | solution.py:267
  120.1 19.8 %collective-permute-start.19 = (bf16[3,128,1024]{2,1,0:T(8,128)(2,1)}, bf16[3,128,1024]{2,1,0:T(8,128)(2,1)}, u32[]{:S(2)}, u32[]{:S(2)}) collective-permute-start(bf16[3,128,1024]{2,1,0:T(8,128)(2,1)} %get-tuple-element.67), channel_id=1, source_target_pairs={{0,2},{2,0},{1,3},{3,1},{4,6},{6,4},{5,7},{7,5},{8,10},{10,8},{9,1... | collective-permute-start | bytes 2359304 | tf_op jit(solution)/shard_map/ppermute | solution.py:267
  (16 other events, 336.7 us)

commit v4 on v3

--- a/solution.py
+++ b/solution.py
@@ -155,14 +155,13 @@
         kept[...] = value
 
 
-def weight_kernel(left_at, straight_at, crossed_at, place, *refs):
+def weight_kernel(left_at, straight_at, crossed_at, per_half, add, place, *refs):
     left, refs = refs[: len(left_at)], refs[len(left_at) :]
     straight, refs = refs[: len(straight_at)], refs[len(straight_at) :]
     crossed, refs = refs[: len(crossed_at)], refs[len(crossed_at) :]
     out, panel, right, left_done, right_done = refs[-5:]
     j = pl.program_id(0)
-    depth, tile = left[0].shape[1], out.shape[1]
-    per_half = crossed[1].shape[1] // tile
+    depth, tile = panel.shape[1] // len(straight), out.shape[1]
 
     def fetch(step, start):
         slot = lax.rem(step, 2)
@@ -172,9 +171,9 @@
             def _():
                 for i, (ref, at) in enumerate(zip(source, source_at)):
                     column = lax.rem(step, per_half) * tile
-                    if i == 0:
+                    ref = ref if at is None else ref.at[at]
+                    if ref.shape[1] > per_half * tile:
                         column += place[1 + half] * per_half * tile
-                    ref = ref if at is None else ref.at[at]
                     copy = pltpu.make_async_copy(
                         ref.at[:, pl.ds(pl.multiple_of(column, tile), tile)],
                         right.at[slot, pl.ds(i * depth, depth)],
@@ -204,16 +203,18 @@
     def _():
         fetch(j + 1, True)
 
-    fetch(j, False)
-
     @pl.when(j == 0)
     def _():
         gather_left(False)
 
-    out[...] = dot(panel[...], right[lax.rem(j, 2)], NN)
-
-
-def weight_rows(place, left, straight, crossed, held, shape):
+    fetch(j, False)
+    value = dot(panel[...], right[lax.rem(j, 2)], NN)
+    if add:
+        value += refs[0][...].astype(jnp.float32)
+    out[...] = value.astype(out.dtype)
+
+
+def weight_rows(place, left, straight, crossed, part, held, shape):
     def split(entries):
         entries = [entry if isinstance(entry, tuple) else (entry, None) for entry in entries]
         return [array for array, _ in entries], [at for _, at in entries]
@@ -222,27 +223,36 @@
     left, left_at = split([entry for pair in left for entry in pair])
     straight, straight_at = split(straight)
     crossed, crossed_at = split(crossed)
-    straight[0], crossed[0] = straight[0][0], crossed[0][0]
-    rows, depth = left[0].shape
-    columns = shape[1]
+    rows, depth = left[0].shape[-2:]
     tile = 512
-    per_half = columns // 2 // tile
+    per_half = crossed[-1].shape[-1] // tile
+    columns = 2 * per_half * tile
     hbm = pl.BlockSpec(memory_space=pl.ANY)
     inputs = [(array, hbm) for array in (*left, *straight, *crossed)]
+
+    def column(j, p):
+        return lax.rem(j, per_half) + jnp.where(j < per_half, p[1], p[2]) * per_half
+
+    alone = pl.BlockSpec((rows, tile), lambda j, p: (0, column(j, p)))
+    block = pl.BlockSpec((rows, tile), lambda j, p: (p[0], column(j, p)))
+    if part is not None:
+        inputs.append((part, alone))
     aliases = {}
     if held is not None:
         inputs.append((held, hbm))
         aliases = {len(inputs): 0}
-
-    def to(j, p):
-        return p[0], lax.rem(j, per_half) + jnp.where(j < per_half, p[1], p[2]) * per_half
-
+    if shape is None:
+        output = ((rows, columns), jnp.bfloat16, alone)
+    else:
+        output = (shape, jnp.float32, block)
     return call(
-        lambda *refs: weight_kernel(left_at, straight_at, crossed_at, *refs),
+        lambda *refs: weight_kernel(
+            left_at, straight_at, crossed_at, per_half, part is not None, *refs
+        ),
         place,
         (2 * per_half,),
         inputs,
-        [(shape, jnp.float32, pl.BlockSpec((rows, tile), to))],
+        [output],
         (
             2 * rows * depth * count * columns,
             4 * rows * columns + 2 * count * depth * (rows + columns),
@@ -258,20 +268,24 @@
     )[0]
 
 
-def queue(axis, pairs, ordered_queue=True):
+def after(value, others):
+    return lax.optimization_barrier((value, *others))[0] if others else value
+
+
+def queue(axis, pairs, in_order=True):
     arrived = []
 
-    def send(value):
-        if arrived and ordered_queue:
-            value = lax.optimization_barrier((value, arrived[-1]))[0]
-        arrived.append(lax.ppermute(value, axis, pairs))
+    def send(value, *others):
+        if in_order:
+            others += tuple(arrived[-1:])
+        arrived.append(lax.ppermute(after(value, others), axis, pairs))
         return arrived[-1]
 
     return send
 
 
-def flipped(axis, bits, ordered_queue=True):
-    return queue(axis, [(i, i ^ bits) for i in range(lax.axis_size(axis))], ordered_queue)
+def flipped(axis, bits, in_order=True):
+    return queue(axis, [(i, i ^ bits) for i in range(lax.axis_size(axis))], in_order)
 
 
 def middle_pairs():
@@ -317,11 +331,8 @@
     def whole(shape):
         return pl.BlockSpec(shape, lambda j, p: (0,) * len(shape))
 
-    def half_of(which):
-        return pl.BlockSpec((1, rows, half), lambda j, p: (0, 0, which(p[0])))
-
-    def after(value, *others):
-        return lax.optimization_barrier((value, *others))[0]
+    def half_of(which, parts=1):
+        return pl.BlockSpec((1, rows, half // parts), lambda j, p: (0, 0, which(p[0]) * parts + j))
 
     own_half, peer_half = half_of(lambda y: y), half_of(lambda y: 1 - y)
     own = (queries, key_states, value_states)
@@ -340,7 +351,7 @@
     packed = send_y(packed)
 
     grad_half = lax.dynamic_slice_in_dim(out_grad[0], t * (columns // 2), columns // 2, axis=1)
-    grad_half = after(grad_half, packed_sent)
+    grad_half = after(grad_half, [packed_sent])
     grad_x = send_x(grad_half)
     grad_1 = send_edge(grad_half)
     grad_2m = send_middle(grad_half)
@@ -376,30 +387,26 @@
         (2 * tokens * columns * width, 2 * columns * (tokens + width), 0),
     )
 
-    own_in = [(v, own_half) for v in own]
+    groups = 2
+    heads //= groups
+    own_in = [(v, half_of(lambda y: y, groups)) for v in own]
+    grad_2e = send_edge(grad_2m, cg_sent, grad_x, packed)
+    grad_3m = send_middle(grad_1, cg_sent, grad_x, packed)
+    grad_1x = send_x(grad_1, packed)
     cg_peer = send_y(cg_sent)
-    grad_1, grad_2m = lax.optimization_barrier((grad_1, grad_2m, cg_sent))[:2]
-    grad_2e = send_edge(grad_2m)
-    grad_3m = send_middle(grad_1)
-    grad_1x = send_x(grad_1)
-    packed_in = (after(packed, cg_sent), whole(packed_shape))
+    group = half // groups
+    packed_block = pl.BlockSpec((packed_shape[0], group), lambda j, p: (0, j))
+    packed_in = (after(packed, [cg_sent]), packed_block)
+    feature_block = pl.BlockSpec((group, tokens), lambda j, p: (j, 0))
     (context,) = call(
         lambda *refs: forward_kernel(scale, heads, *refs),
         place,
-        (1,),
+        (groups,),
         own_in + [packed_in, (align_ids, smem), (align_count, smem)],
-        [((half, tokens), b16, whole((half, tokens)))],
-        (heads * 2**25, 3 * MIB, heads * 2**16),
-    )
-
-    context_x = send_x(context)
-    context_y = send_y(context)
-    near_1 = send_edge(context)
-    near_2m = send_middle(context)
-    grad_3e = send_edge(grad_3m)
-    near_2e = send_edge(near_2m)
-    near_3m = send_middle(near_1)
-    near_3e = send_edge(near_3m)
+        [((half, tokens), b16, feature_block)],
+        (groups * heads * 2**25, 3 * MIB, groups * heads * 2**16),
+    )
+
     def pick(ends, middles):
         shape = ends[0].shape
         return call(
@@ -412,37 +419,46 @@
             scratch=[pltpu.SemaphoreType.DMA((2,))],
         )[0]
 
+    context_x = send_x(context)
+    context_y = send_y(context)
+    near_1 = send_edge(context, grad_1x, cg_peer)
+    near_2m = send_middle(context, cg_peer)
+    grad_3e = send_edge(grad_3m, context_x)
+    near_3m = send_middle(near_1)
+    diagonal = send_y(context_x)
+    near_1x = send_x(near_1)
+    full = (1, rows, width)
+    sent_shape = (3, rows, half)
+    *outs, sent = call(
+        lambda *refs: backward_kernel(scale, heads, *refs),
+        place,
+        (groups,),
+        own_in
+        + [packed_in, (align_ids, smem), (align_count, smem)]
+        + [(cg_own, feature_block), (cg_peer, feature_block)],
+        [(full, b16, half_of(lambda y: y, groups))] * 3
+        + [(sent_shape, b16, pl.BlockSpec((3, rows, group), lambda j, p: (0, 0, j)))],
+        (groups * heads * 2**26, 5 * MIB, groups * heads * 2**16),
+    )
+    near_2e = send_edge(near_2m, near_1x, diagonal, sent)
     grad_p = pick((grad_2e, grad_3e), (grad_2m, grad_3m))
+    grad_px = send_x(grad_p)
+    near_1y = send_y(near_1)
+    near_3e = send_edge(near_3m, near_1y)
     near_p = pick((near_2e, near_3e), (near_2m, near_3m))
-    grad_px = send_x(grad_p)
-    diagonal = send_y(context_x)
-    diagonal_1 = send_edge(diagonal)
+    near_px = send_x(near_p)
+    near_py = send_y(near_p)
+    received = send_y(sent)
+    diagonal_1 = send_edge(diagonal, grad_px)
     diagonal_2m = send_middle(diagonal)
     diagonal_2e = send_edge(diagonal_2m)
     diagonal_3m = send_middle(diagonal_1)
-    diagonal_3e = send_edge(diagonal_3m)
-    near_1x, near_1y = send_x(near_1), send_y(near_1)
-    near_px, near_py = send_x(near_p), send_y(near_p)
     grad_1c = send_core(grad_1)
     grad_pc = send_core(grad_p)
     grad_xc = send_core(grad_x)
     grad_1xc = send_core(grad_1x)
     grad_pxc = send_core(grad_px)
 
-    cg_shape = (half, tokens)
-    full = (1, rows, width)
-    sent_shape = (3, rows, half)
-    *outs, sent = call(
-        lambda *refs: backward_kernel(scale, heads, *refs),
-        place,
-        (1,),
-        own_in
-        + [packed_in, (align_ids, smem), (align_count, smem)]
-        + [(cg_own, whole(cg_shape)), (cg_peer, whole(cg_shape))],
-        [(full, b16, own_half)] * 3 + [(sent_shape, b16, whole(sent_shape))],
-        (heads * 2**26, 5 * MIB, heads * 2**16),
-    )
-    received = send_y(sent)
     outs = call(
         place_kernel,
         place,
@@ -457,16 +473,22 @@
     def parts(first, second, pair, first_x, second_x, pair_x):
         return [first, second, (pair, 0), (pair, 1), first_x, second_x, (pair_x, 0), (pair_x, 1)]
 
-    straight = parts(out_grad, grad_1, grad_p, grad_x, grad_1x, grad_px)
-    crossed = parts(out_grad, grad_1c, grad_pc, grad_xc, grad_1xc, grad_pxc)
+    straight = parts((out_grad, 0), grad_1, grad_p, grad_x, grad_1x, grad_px)
+    crossed = parts((out_grad, 0), grad_1c, grad_pc, grad_xc, grad_1xc, grad_pxc)
     near = [(c, c) for c in parts(context, near_1, near_p, context_x, near_1x, near_px)]
+    near_place = jnp.stack([y, t, 1 - t, is_middle])
+    far_place = jnp.stack([1 - y, t, 1 - t, is_middle])
+    early = len(near) - 2
+    part = weight_rows(
+        near_place, near[:early], straight[:early], crossed[:early], None, None, None
+    )
+    diagonal_3e = send_edge(diagonal_3m, part)
     far = [(c, c) for c in (context_y, near_1y, (near_py, 0), (near_py, 1), diagonal, diagonal_1)]
     far += [(diagonal_2e, diagonal_2m), (diagonal_3e, diagonal_3m)]
-    near_place = jnp.stack([y, t, 1 - t, is_middle])
-    far_place = jnp.stack([1 - y, t, 1 - t, is_middle])
-    grad = weight_rows(near_place, near, straight, crossed, None, shape)
-    *outs, grad = lax.optimization_barrier((*outs, grad))
-    grad = weight_rows(far_place, far, straight, crossed, grad, shape)
+    grad = weight_rows(
+        near_place, near[early:], straight[early:], crossed[early:], part, None, shape
+    )
+    grad = weight_rows(far_place, far, straight, crossed, None, grad, shape)
     return (*outs, grad)
 
 

time: 160 us -> 150 us (0.938)
  waiting for transfers between devices: 52.8 us -> 39.4 us
  Pallas kernels: 56.1 us -> 62.4 us
  starting transfers between devices: 42.2 us -> 39 us
    ppermute x33, waiting for transfers between devices: 52.8 us -> 39.4 us  [send(): arrived.append(lax.ppermute(after(value, others), axis, pairs))]
    pallas_call x9 -> x10, Pallas kernels: 56.1 us -> 62.4 us  [call(): pl.pallas_call(kernel, grid_spec=pltpu.PrefetchScalarGridSpec(num_scalar_...]
    ppermute x33, starting transfers between devices: 42.2 us -> 39 us  [send(): arrived.append(lax.ppermute(after(value, others), axis, pairs))]
  transfers between devices with their start and end apart: 33 -> 33, of which waited for: 18 -> 17; matrix products, arithmetic and copies ran while one was open for 1% -> 2% of each run, Pallas kernels for 25% -> 40%
where the time goes in v4:
time: 150 us; the launch traced here: 147 us
  Pallas kernels  62.4 us (42%)
  waiting for transfers between devices  39.4 us (26%)
  starting transfers between devices  39 us (26%)
  local copies, waits for them, and re-layouts  3.6 us (2%)
    pallas_call x10, Pallas kernels, call(): pl.pallas_call(kernel, grid_spec=pltpu.PrefetchScalarGridSpec(num_scalar_...  62.4 us
    ppermute x33, waiting for transfers between devices, send(): arrived.append(lax.ppermute(after(value, others), axis, pairs))  39.4 us
    ppermute x33, starting transfers between devices, send(): arrived.append(lax.ppermute(after(value, others), axis, pairs))  39 us
  transfers between devices with their start and end apart: 33, of which 17 were waited for; matrix products, arithmetic and copies ran while one was open for 2% of the time, Pallas kernels for 40%

profile of v4, /device:TPU:8, one launch (start us, length us, event | category | flops | bytes accessed | tf_op | source)
XLA Modules:
  0.0 147.1 jit_solution(10209038991717562936)
XLA Ops:
  1.3 2.1 %shard_map.102 = bf16[400,1024]{1,0:T(8,128)(2,1)} custom-call(s32[1]{0:T(128)} %bitcast.place.refs_0_, bf16[1,128,2048]{2,1,0:T(8,128)(2,1)} %refs_1_.5, bf16[1,128,2048]{2,1,0:T(8,128)(2,1)} %refs_2_.5, bf16[1,128,2048]{2,1,0:T(8,128)(2,1)} %refs_3_.3, s32[1,1,2]{2,1,0:T(1,128)} %refs_5_.3, s32[1,1]{1,0:T(1,128)S(6)} %copy.19.count.refs_6_), custom_call_target="tpu_custom_call" | custom-call | bytes 1572864 | tf_op jit(solution)/shard_map/pallas_call | solution.py:54
  3.3 1.5 %collective-permute-start = (bf16[400,1024]{1,0:T(8,128)(2,1)}, bf16[400,1024]{1,0:T(8,128)(2,1)S(1)}, u32[]{:S(2)}, u32[]{:S(2)}) collective-permute-start(bf16[400,1024]{1,0:T(8,128)(2,1)} %shard_map.102), channel_id=1, source_target_pairs={{0,2},{2,0},{1,3},{3,1},{4,6},{6,4},{5,7},{7,5},{8,10},{10,8},{9,1... | collective-permute-start | bytes 2457608 | tf_op jit(solution)/shard_map/ppermute | solution.py:281
  5.9 1.6 %collective-permute-start.3 = (bf16[256,1024]{1,0:T(8,128)(2,1)S(1)}, bf16[256,1024]{1,0:T(8,128)(2,1)S(1)}, u32[]{:S(2)}, u32[]{:S(2)}) collective-permute-start(bf16[256,1024]{1,0:T(8,128)(2,1)S(1)} %dynamic-slice_bitcast_fusion), channel_id=1, source_target_pairs={{0,4},{4,0},{8,12},{12,8},{16,20},{20,16},{24,28},{28,24},{1,5},{5... | collective-permute-start | bytes 1572872 | tf_op jit(solution)/shard_map/ppermute | solution.py:281
  8.0 2.7 %collective-permute-start.4 = (bf16[256,1024]{1,0:T(8,128)(2,1)S(1)}, bf16[256,1024]{1,0:T(8,128)(2,1)S(1)}, u32[]{:S(2)}, u32[]{:S(2)}) collective-permute-start(bf16[256,1024]{1,0:T(8,128)(2,1)S(1)} %dynamic-slice_bitcast_fusion), channel_id=1, source_target_pairs={{0,1},{1,0},{4,5},{5,4},{8,16},{9,17},{12,20},{13,21},{16,8},{17,9... | collective-permute-start | bytes 1572872 | tf_op jit(solution)/shard_map/ppermute | solution.py:281
  10.7 6.8 %shard_map.103 = (bf16[1024,256]{1,0:T(8,128)(2,1)}, bf16[1024,256]{1,0:T(8,128)(2,1)}) custom-call(s32[1]{0:T(128)} %bitcast.place.refs_0_, bf16[1,256,2048]{2,1,0:T(8,128)(2,1)} %refs_25_.1, bf16[2048,2048]{1,0:T(8,128)(2,1)} %refs_2_.3), custom_call_target="tpu_custom_call" | custom-call | flops 2147483648 | bytes 9437184 | tf_op jit(solution)/shard_map/pallas_call | solution.py:54
  17.4 1.9 %collective-permute-done.3.refs_17_.refs_21_ = bf16[256,1024]{1,0:T(8,128)(2,1)S(1)} collective-permute-done((bf16[256,1024]{1,0:T(8,128)(2,1)S(1)}, bf16[256,1024]{1,0:T(8,128)(2,1)S(1)}, u32[]{:S(2)}, u32[]{:S(2)}) %collective-permute-start.3) | collective-permute-done | bytes 524320 | tf_op jit(solution)/shard_map/ppermute | solution.py:281
  20.6 2.9 %collective-permute-done.refs_4_ = bf16[400,1024]{1,0:T(8,128)(2,1)S(1)} collective-permute-done((bf16[400,1024]{1,0:T(8,128)(2,1)}, bf16[400,1024]{1,0:T(8,128)(2,1)S(1)}, u32[]{:S(2)}, u32[]{:S(2)}) %collective-permute-start) | collective-permute-done | bytes 819232 | tf_op jit(solution)/shard_map/ppermute | solution.py:281
  25.0 1.5 %collective-permute-start.1 = (bf16[1024,256]{1,0:T(8,128)(2,1)}, bf16[1024,256]{1,0:T(8,128)(2,1)}, u32[]{:S(2)}, u32[]{:S(2)}) collective-permute-start(bf16[1024,256]{1,0:T(8,128)(2,1)} %get-tuple-element.42), channel_id=1, source_target_pairs={{0,2},{2,0},{1,3},{3,1},{4,6},{6,4},{5,7},{7,5},{8,10},{10,8},{9,1... | collective-permute-start | bytes 1572872 | tf_op jit(solution)/shard_map/ppermute | solution.py:281
  27.0 2.7 %collective-permute-start.5 = (bf16[256,1024]{1,0:T(8,128)(2,1)S(1)}, bf16[256,1024]{1,0:T(8,128)(2,1)}, u32[]{:S(2)}, u32[]{:S(2)}) collective-permute-start(bf16[256,1024]{1,0:T(8,128)(2,1)S(1)} %collective-permute-done.2.refs_14_.refs_18_), channel_id=1, source_target_pairs={{0,1},{1,0},{4,5},{5,4},{8,16},{9,17},{12,20},{13,21},{16,8},{17,9... | collective-permute-start | bytes 1572872 | tf_op jit(solution)/shard_map/ppermute | solution.py:281
  29.7 4.9 %shard_map.105.refs_1_.refs_2_ = bf16[1024,256]{1,0:T(8,128)(2,1)} custom-call(s32[1]{0:T(128)} %bitcast.place.refs_0_, bf16[1,128,2048]{2,1,0:T(8,128)(2,1)} %refs_1_.5, bf16[1,128,2048]{2,1,0:T(8,128)(2,1)} %refs_2_.5, bf16[1,128,2048]{2,1,0:T(8,128)(2,1)} %refs_3_.3, bf16[400,1024]{1,0:T(8,128)(2,1)} %copy-done.3, s32[1,1,2]{2,1,0:T(1,128)} %refs_5_.3, ...), custom_call_target="tpu_custom_call" | custom-call | flops 268435456 | bytes 3145728 | tf_op jit(solution)/shard_map/pallas_call | solution.py:54
  34.7 1.7 %collective-permute-done.7.refs_18_.refs_22_ = bf16[256,1024]{1,0:T(8,128)(2,1)S(1)} collective-permute-done((bf16[256,1024]{1,0:T(8,128)(2,1)S(1)}, bf16[256,1024]{1,0:T(8,128)(2,1)S(1)}, u32[]{:S(2)}, u32[]{:S(2)}) %collective-permute-start.7) | collective-permute-done | bytes 524320 | tf_op jit(solution)/shard_map/ppermute | solution.py:281
  40.0 2.5 %collective-permute-start.6 = (bf16[1024,256]{1,0:T(8,128)(2,1)}, bf16[1024,256]{1,0:T(8,128)(2,1)}, u32[]{:S(2)}, u32[]{:S(2)}) collective-permute-start(bf16[1024,256]{1,0:T(8,128)(2,1)} %shard_map.105.refs_1_.refs_2_), channel_id=1, source_target_pairs={{0,1},{1,0},{4,5},{5,4},{8,16},{9,17},{12,20},{13,21},{16,8},{17,9... | collective-permute-start | bytes 1572872 | tf_op jit(solution)/shard_map/ppermute | solution.py:281
  42.5 6.1 %collective-permute-done.10.refs_9_.refs_10_ = bf16[1024,256]{1,0:T(8,128)(2,1)} collective-permute-done((bf16[1024,256]{1,0:T(8,128)(2,1)}, bf16[1024,256]{1,0:T(8,128)(2,1)}, u32[]{:S(2)}, u32[]{:S(2)}) %collective-permute-start.10) | collective-permute-done | bytes 524320 | tf_op jit(solution)/shard_map/ppermute | solution.py:281
  50.0 1.5 %collective-permute-start.13 = (bf16[1024,256]{1,0:T(8,128)(2,1)}, bf16[1024,256]{1,0:T(8,128)(2,1)S(1)}, u32[]{:S(2)}, u32[]{:S(2)}) collective-permute-start(bf16[1024,256]{1,0:T(8,128)(2,1)} %collective-permute-done.10.refs_9_.refs_10_), channel_id=1, source_target_pairs={{0,2},{2,0},{1,3},{3,1},{4,6},{6,4},{5,7},{7,5},{8,10},{10,8},{9,1... | collective-permute-start | bytes 1572872 | tf_op jit(solution)/shard_map/ppermute | solution.py:281
  52.4 5.9 %shard_map.104 = (bf16[1,128,2048]{2,1,0:T(8,128)(2,1)}, bf16[1,128,2048]{2,1,0:T(8,128)(2,1)}, bf16[1,128,2048]{2,1,0:T(8,128)(2,1)}, bf16[3,128,1024]{2,1,0:T(8,128)(2,1)}) custom-call(s32[1]{0:T(128)} %bitcast.place.refs_0_, bf16[1,128,2048]{2,1,0:T(8,128)(2,1)} %refs_1_.5, bf16[1,128,2048]{2,1,0:T(8,128)(2,1)} %refs_2_.5, bf16[1,128,2048]{2,1,0:T(8,128)(2,1)} %refs_3_.3, ...), custom_call_target="tpu_custom_call" | custom-call | flops 536870912 | bytes 5242880 | tf_op jit(solution)/shard_map/pallas_call | solution.py:54
  58.3 2.8 %collective-permute-start.16 = (bf16[1024,256]{1,0:T(8,128)(2,1)}, bf16[1024,256]{1,0:T(8,128)(2,1)}, u32[]{:S(2)}, u32[]{:S(2)}) collective-permute-start(bf16[1024,256]{1,0:T(8,128)(2,1)} %collective-permute-done.9.refs_3_.refs_4_), channel_id=1, source_target_pairs={{0,1},{1,0},{4,5},{5,4},{8,16},{9,17},{12,20},{13,21},{16,8},{17,9... | collective-permute-start | bytes 1572872 | tf_op jit(solution)/shard_map/ppermute | solution.py:281
  61.9 1.5 %collective-permute-start.17 = (bf16[1024,256]{1,0:T(8,128)(2,1)}, bf16[1024,256]{1,0:T(8,128)(2,1)S(1)}, u32[]{:S(2)}, u32[]{:S(2)}) collective-permute-start(bf16[1024,256]{1,0:T(8,128)(2,1)} %collective-permute-done.9.refs_3_.refs_4_), channel_id=1, source_target_pairs={{0,2},{2,0},{1,3},{3,1},{4,6},{6,4},{5,7},{7,5},{8,10},{10,8},{9,1... | collective-permute-start | bytes 1572872 | tf_op jit(solution)/shard_map/ppermute | solution.py:281
  64.3 2.2 %shard_map.108.refs_15_.refs_16_.refs_19_.refs_20_ = bf16[2,256,1024]{2,1,0:T(8,128)(2,1)} custom-call(s32[1]{0:T(128)} %bitcast.1.place, bf16[256,1024]{1,0:T(8,128)(2,1)} %copy-done.12, bf16[256,1024]{1,0:T(8,128)(2,1)} %copy-done.13, bf16[256,1024]{1,0:T(8,128)(2,1)} %copy-done.11, bf16[256,1024]{1,0:T(8,128)(2,1)} %collective-permute-done.5.refs_3_), custom_call_target="tpu_custom_call" | custom-call | bytes 2097152 | tf_op jit(solution)/shard_map/pallas_call | solution.py:54
  67.1 2.5 %collective-permute-done.16.refs_3_ = bf16[1024,256]{1,0:T(8,128)(2,1)} collective-permute-done((bf16[1024,256]{1,0:T(8,128)(2,1)}, bf16[1024,256]{1,0:T(8,128)(2,1)}, u32[]{:S(2)}, u32[]{:S(2)}) %collective-permute-start.16) | collective-permute-done | bytes 524320 | tf_op jit(solution)/shard_map/ppermute | solution.py:281
  69.7 2.5 %collective-permute-done.17.refs_3_.refs_4_ = bf16[1024,256]{1,0:T(8,128)(2,1)S(1)} collective-permute-done((bf16[1024,256]{1,0:T(8,128)(2,1)}, bf16[1024,256]{1,0:T(8,128)(2,1)S(1)}, u32[]{:S(2)}, u32[]{:S(2)}) %collective-permute-start.17) | collective-permute-done | bytes 524320 | tf_op jit(solution)/shard_map/ppermute | solution.py:281
  72.2 1.6 %collective-permute-done.15.refs_0_ = bf16[1024,256]{1,0:T(8,128)(2,1)} collective-permute-done((bf16[1024,256]{1,0:T(8,128)(2,1)}, bf16[1024,256]{1,0:T(8,128)(2,1)}, u32[]{:S(2)}, u32[]{:S(2)}) %collective-permute-start.15) | collective-permute-done | bytes 524320 | tf_op jit(solution)/shard_map/ppermute | solution.py:281
  75.5 9.6 %collective-permute-done.18.refs_1_ = bf16[1024,256]{1,0:T(8,128)(2,1)S(1)} collective-permute-done((bf16[1024,256]{1,0:T(8,128)(2,1)}, bf16[1024,256]{1,0:T(8,128)(2,1)S(1)}, u32[]{:S(2)}, u32[]{:S(2)}) %collective-permute-start.18) | collective-permute-done | bytes 524320 | tf_op jit(solution)/shard_map/ppermute | solution.py:281
  86.5 1.6 %collective-permute-done.21.refs_5_.refs_6_.refs_23_.refs_24_ = bf16[2,256,1024]{2,1,0:T(8,128)(2,1)S(1)} collective-permute-done((bf16[2,256,1024]{2,1,0:T(8,128)(2,1)}, bf16[2,256,1024]{2,1,0:T(8,128)(2,1)S(1)}, u32[]{:S(2)}, u32[]{:S(2)}) %collective-permute-start.21) | collective-permute-done | bytes 1048608 | tf_op jit(solution)/shard_map/ppermute | solution.py:281
  89.9 2.2 %shard_map.106.refs_5_.refs_6_.refs_7_.refs_8_ = bf16[2,1024,256]{2,1,0:T(8,128)(2,1)} custom-call(s32[1]{0:T(128)} %bitcast.1.place, bf16[1024,256]{1,0:T(8,128)(2,1)} %collective-permute-done.15.refs_0_, bf16[1024,256]{1,0:T(8,128)(2,1)} %copy-done.14, bf16[1024,256]{1,0:T(8,128)(2,1)} %collective-permute-done.6.refs_2_, ...), custom_call_target="tpu_custom_call" | custom-call | bytes 2097152 | tf_op jit(solution)/shard_map/pallas_call | solution.py:54
  92.2 1.6 %collective-permute-start.19 = (bf16[2,1024,256]{2,1,0:T(8,128)(2,1)}, bf16[2,1024,256]{2,1,0:T(8,128)(2,1)S(1)}, u32[]{:S(2)}, u32[]{:S(2)}) collective-permute-start(bf16[2,1024,256]{2,1,0:T(8,128)(2,1)} %shard_map.106.refs_5_.refs_6_.refs_7_.refs_8_), channel_id=1, source_target_pairs={{0,2},{2,0},{1,3},{3,1},{4,6},{6,4},{5,7},{7,5},{8,10},{10,8},{9,1... | collective-permute-start | bytes 3145736 | tf_op jit(solution)/shard_map/ppermute | solution.py:281
  93.7 1.7 %collective-permute-done.23.refs_14_ = bf16[1024,256]{1,0:T(8,128)(2,1)} collective-permute-done((bf16[1024,256]{1,0:T(8,128)(2,1)S(1)}, bf16[1024,256]{1,0:T(8,128)(2,1)}, u32[]{:S(2)}, u32[]{:S(2)}) %collective-permute-start.23) | collective-permute-done | bytes 524320 | tf_op jit(solution)/shard_map/ppermute | solution.py:281
  95.4 2.9 %collective-permute-start.32 = (bf16[2,1024,256]{2,1,0:T(8,128)(2,1)}, bf16[2,1024,256]{2,1,0:T(8,128)(2,1)}, u32[]{:S(2)}, u32[]{:S(2)}) collective-permute-start(bf16[2,1024,256]{2,1,0:T(8,128)(2,1)} %shard_map.106.refs_5_.refs_6_.refs_7_.refs_8_), channel_id=1, source_target_pairs={{0,4},{4,0},{8,12},{12,8},{16,20},{20,16},{24,28},{28,24},{1,5},{5... | collective-permute-start | bytes 3145736 | tf_op jit(solution)/shard_map/ppermute | solution.py:281
  100.2 1.7 %collective-permute-start.24 = (bf16[1024,256]{1,0:T(8,128)(2,1)}, bf16[1024,256]{1,0:T(8,128)(2,1)}, u32[]{:S(2)}, u32[]{:S(2)}) collective-permute-start(bf16[1024,256]{1,0:T(8,128)(2,1)} %collective-permute-done.23.refs_14_), channel_id=1, source_target_pairs={{0,8},{4,12},{8,0},{12,4},{16,24},{20,28},{24,16},{28,20},{1,9},{5... | collective-permute-start | bytes 1572872 | tf_op jit(solution)/shard_map/ppermute | solution.py:281
  103.1 11.7 %shard_map.109.refs_9_ = bf16[1024,2048]{1,0:T(8,128)(2,1)} custom-call(s32[4]{0:T(128)} %add_add_fusion.1.refs_0_, bf16[1024,256]{1,0:T(8,128)(2,1)} %shard_map.105.refs_1_.refs_2_, bf16[1024,256]{1,0:T(8,128)(2,1)} %shard_map.105.refs_1_.refs_2_, bf16[1024,256]{1,0:T(8,128)(2,1)} %collective-permute-done.9.refs_3_.refs_4_, ...), custom_call_target="tpu_custom_call" | custom-call | flops 6442450944 | bytes 17825792 | tf_op jit(solution)/shard_map/pallas_call | solution.py:54
  120.5 9.7 %shard_map.110.refs_33_ = f32[2048,2048]{1,0:T(8,128)} custom-call(s32[4]{0:T(128)} %add_add_fusion.1.refs_0_, bf16[2,1024,256]{2,1,0:T(8,128)(2,1)} %collective-permute-done.32.refs_1_.refs_2_.refs_3_.refs_4_, bf16[2,1024,256]{2,1,0:T(8,128)(2,1)} %collective-permute-done.32.refs_1_.refs_2_.refs_3_.refs_4_, ...), custom_call_target="tpu_custom_call" | custom-call | flops 2147483648 | bytes 11534336 | tf_op jit(solution)/shard_map/pallas_call | solution.py:54
  130.2 14.8 %shard_map.111 = f32[2048,2048]{1,0:T(8,128)} custom-call(s32[4]{0:T(128)} %add_add_fusion.refs_0_, bf16[1024,256]{1,0:T(8,128)(2,1)} %collective-permute-done.12.refs_1_.refs_2_, bf16[1024,256]{1,0:T(8,128)(2,1)} %collective-permute-done.12.refs_1_.refs_2_, bf16[1024,256]{1,0:T(8,128)(2,1)} %copy-done.5, ...), custom_call_target="tpu_custom_call", output_to_operand_aliasing={{}: (33, {})} | custom-call | flops 8589934592 | bytes 20971520 | tf_op jit(solution)/shard_map/pallas_call | solution.py:54
  145.1 2.0 %shard_map.107 = (bf16[1,128,2048]{2,1,0:T(8,128)(2,1)}, bf16[1,128,2048]{2,1,0:T(8,128)(2,1)}, bf16[1,128,2048]{2,1,0:T(8,128)(2,1)}) custom-call(s32[1]{0:T(128)} %bitcast.place.refs_0_, bf16[3,128,1024]{2,1,0:T(8,128)(2,1)} %collective-permute-done.20.received, ...), custom_call_target="tpu_custom_call", output_to_operand_aliasing={{0}: (2, {}), {1}: (3, {}), {2}: (4, {})} | custom-call | bytes 1572864 | tf_op jit(solution)/shard_map/pallas_call | solution.py:54
  (77 shorter events, 26.5 us)
Async XLA Ops:
  3.3 20.2 %collective-permute-start = (bf16[400,1024]{1,0:T(8,128)(2,1)}, bf16[400,1024]{1,0:T(8,128)(2,1)S(1)}, u32[]{:S(2)}, u32[]{:S(2)}) collective-permute-start(bf16[400,1024]{1,0:T(8,128)(2,1)} %shard_map.102), channel_id=1, source_target_pairs={{0,2},{2,0},{1,3},{3,1},{4,6},{6,4},{5,7},{7,5},{8,10},{10,8},{9,1... | collective-permute-start | bytes 2457608 | tf_op jit(solution)/shard_map/ppermute | solution.py:281
  5.9 13.4 %collective-permute-start.3 = (bf16[256,1024]{1,0:T(8,128)(2,1)S(1)}, bf16[256,1024]{1,0:T(8,128)(2,1)S(1)}, u32[]{:S(2)}, u32[]{:S(2)}) collective-permute-start(bf16[256,1024]{1,0:T(8,128)(2,1)S(1)} %dynamic-slice_bitcast_fusion), channel_id=1, source_target_pairs={{0,4},{4,0},{8,12},{12,8},{16,20},{20,16},{24,28},{28,24},{1,5},{5... | collective-permute-start | bytes 1572872 | tf_op jit(solution)/shard_map/ppermute | solution.py:281
  7.5 13.1 %collective-permute-start.2 = (bf16[256,1024]{1,0:T(8,128)(2,1)S(1)}, bf16[256,1024]{1,0:T(8,128)(2,1)S(1)}, u32[]{:S(2)}, u32[]{:S(2)}) collective-permute-start(bf16[256,1024]{1,0:T(8,128)(2,1)S(1)} %dynamic-slice_bitcast_fusion), channel_id=1, source_target_pairs={{0,8},{4,12},{8,0},{12,4},{16,24},{20,28},{24,16},{28,20},{1,9},{5... | collective-permute-start | bytes 1572872 | tf_op jit(solution)/shard_map/ppermute | solution.py:281
  8.0 18.6 %collective-permute-start.4 = (bf16[256,1024]{1,0:T(8,128)(2,1)S(1)}, bf16[256,1024]{1,0:T(8,128)(2,1)S(1)}, u32[]{:S(2)}, u32[]{:S(2)}) collective-permute-start(bf16[256,1024]{1,0:T(8,128)(2,1)S(1)} %dynamic-slice_bitcast_fusion), channel_id=1, source_target_pairs={{0,1},{1,0},{4,5},{5,4},{8,16},{9,17},{12,20},{13,21},{16,8},{17,9... | collective-permute-start | bytes 1572872 | tf_op jit(solution)/shard_map/ppermute | solution.py:281
  23.5 12.8 %collective-permute-start.7 = (bf16[256,1024]{1,0:T(8,128)(2,1)S(1)}, bf16[256,1024]{1,0:T(8,128)(2,1)S(1)}, u32[]{:S(2)}, u32[]{:S(2)}) collective-permute-start(bf16[256,1024]{1,0:T(8,128)(2,1)S(1)} %collective-permute-done.2.refs_14_.refs_18_), channel_id=1, source_target_pairs={{0,4},{4,0},{8,12},{12,8},{16,20},{20,16},{24,28},{28,24},{1,5},{5... | collective-permute-start | bytes 1572872 | tf_op jit(solution)/shard_map/ppermute | solution.py:281
  25.0 12.8 %collective-permute-start.1 = (bf16[1024,256]{1,0:T(8,128)(2,1)}, bf16[1024,256]{1,0:T(8,128)(2,1)}, u32[]{:S(2)}, u32[]{:S(2)}) collective-permute-start(bf16[1024,256]{1,0:T(8,128)(2,1)} %get-tuple-element.42), channel_id=1, source_target_pairs={{0,2},{2,0},{1,3},{3,1},{4,6},{6,4},{5,7},{7,5},{8,10},{10,8},{9,1... | collective-permute-start | bytes 1572872 | tf_op jit(solution)/shard_map/ppermute | solution.py:281
  26.6 12.8 %collective-permute-start.8 = (bf16[256,1024]{1,0:T(8,128)(2,1)S(1)}, bf16[256,1024]{1,0:T(8,128)(2,1)S(1)}, u32[]{:S(2)}, u32[]{:S(2)}) collective-permute-start(bf16[256,1024]{1,0:T(8,128)(2,1)S(1)} %collective-permute-done.4.refs_2_), channel_id=1, source_target_pairs={{0,8},{4,12},{8,0},{12,4},{16,24},{20,28},{24,16},{28,20},{1,9},{5... | collective-permute-start | bytes 1572872 | tf_op jit(solution)/shard_map/ppermute | solution.py:281
  27.0 13.0 %collective-permute-start.5 = (bf16[256,1024]{1,0:T(8,128)(2,1)S(1)}, bf16[256,1024]{1,0:T(8,128)(2,1)}, u32[]{:S(2)}, u32[]{:S(2)}) collective-permute-start(bf16[256,1024]{1,0:T(8,128)(2,1)S(1)} %collective-permute-done.2.refs_14_.refs_18_), channel_id=1, source_target_pairs={{0,1},{1,0},{4,5},{5,4},{8,16},{9,17},{12,20},{13,21},{16,8},{17,9... | collective-permute-start | bytes 1572872 | tf_op jit(solution)/shard_map/ppermute | solution.py:281
  36.3 12.3 %collective-permute-start.10 = (bf16[1024,256]{1,0:T(8,128)(2,1)}, bf16[1024,256]{1,0:T(8,128)(2,1)}, u32[]{:S(2)}, u32[]{:S(2)}) collective-permute-start(bf16[1024,256]{1,0:T(8,128)(2,1)} %shard_map.105.refs_1_.refs_2_), channel_id=1, source_target_pairs={{0,4},{4,0},{8,12},{12,8},{16,20},{20,16},{24,28},{28,24},{1,5},{5... | collective-permute-start | bytes 1572872 | tf_op jit(solution)/shard_map/ppermute | solution.py:281
  37.9 12.1 %collective-permute-start.12 = (bf16[1024,256]{1,0:T(8,128)(2,1)}, bf16[1024,256]{1,0:T(8,128)(2,1)}, u32[]{:S(2)}, u32[]{:S(2)}) collective-permute-start(bf16[1024,256]{1,0:T(8,128)(2,1)} %shard_map.105.refs_1_.refs_2_), channel_id=1, source_target_pairs={{0,2},{2,0},{1,3},{3,1},{4,6},{6,4},{5,7},{7,5},{8,10},{10,8},{9,1... | collective-permute-start | bytes 1572872 | tf_op jit(solution)/shard_map/ppermute | solution.py:281
  39.4 12.1 %collective-permute-start.9 = (bf16[1024,256]{1,0:T(8,128)(2,1)}, bf16[1024,256]{1,0:T(8,128)(2,1)}, u32[]{:S(2)}, u32[]{:S(2)}) collective-permute-start(bf16[1024,256]{1,0:T(8,128)(2,1)} %shard_map.105.refs_1_.refs_2_), channel_id=1, source_target_pairs={{0,8},{4,12},{8,0},{12,4},{16,24},{20,28},{24,16},{28,20},{1,9},{5... | collective-permute-start | bytes 1572872 | tf_op jit(solution)/shard_map/ppermute | solution.py:281
  40.0 18.3 %collective-permute-start.6 = (bf16[1024,256]{1,0:T(8,128)(2,1)}, bf16[1024,256]{1,0:T(8,128)(2,1)}, u32[]{:S(2)}, u32[]{:S(2)}) collective-permute-start(bf16[1024,256]{1,0:T(8,128)(2,1)} %shard_map.105.refs_1_.refs_2_), channel_id=1, source_target_pairs={{0,1},{1,0},{4,5},{5,4},{8,16},{9,17},{12,20},{13,21},{16,8},{17,9... | collective-permute-start | bytes 1572872 | tf_op jit(solution)/shard_map/ppermute | solution.py:281
  50.0 12.0 %collective-permute-start.13 = (bf16[1024,256]{1,0:T(8,128)(2,1)}, bf16[1024,256]{1,0:T(8,128)(2,1)S(1)}, u32[]{:S(2)}, u32[]{:S(2)}) collective-permute-start(bf16[1024,256]{1,0:T(8,128)(2,1)} %collective-permute-done.10.refs_9_.refs_10_), channel_id=1, source_target_pairs={{0,2},{2,0},{1,3},{3,1},{4,6},{6,4},{5,7},{7,5},{8,10},{10,8},{9,1... | collective-permute-start | bytes 1572872 | tf_op jit(solution)/shard_map/ppermute | solution.py:281
  51.5 12.0 %collective-permute-start.11 = (bf16[1024,256]{1,0:T(8,128)(2,1)}, bf16[1024,256]{1,0:T(8,128)(2,1)}, u32[]{:S(2)}, u32[]{:S(2)}) collective-permute-start(bf16[1024,256]{1,0:T(8,128)(2,1)} %collective-permute-done.9.refs_3_.refs_4_), channel_id=1, source_target_pairs={{0,4},{4,0},{8,12},{12,8},{16,20},{20,16},{24,28},{28,24},{1,5},{5... | collective-permute-start | bytes 1572872 | tf_op jit(solution)/shard_map/ppermute | solution.py:281
  51.9 11.6 %collective-permute-start.14 = (bf16[256,1024]{1,0:T(8,128)(2,1)}, bf16[256,1024]{1,0:T(8,128)(2,1)S(1)}, u32[]{:S(2)}, u32[]{:S(2)}) collective-permute-start(bf16[256,1024]{1,0:T(8,128)(2,1)} %collective-permute-done.5.refs_3_), channel_id=1, source_target_pairs={{0,8},{4,12},{8,0},{12,4},{16,24},{20,28},{24,16},{28,20},{1,9},{5... | collective-permute-start | bytes 1572872 | tf_op jit(solution)/shard_map/ppermute | solution.py:281
  58.3 11.4 %collective-permute-start.16 = (bf16[1024,256]{1,0:T(8,128)(2,1)}, bf16[1024,256]{1,0:T(8,128)(2,1)}, u32[]{:S(2)}, u32[]{:S(2)}) collective-permute-start(bf16[1024,256]{1,0:T(8,128)(2,1)} %collective-permute-done.9.refs_3_.refs_4_), channel_id=1, source_target_pairs={{0,1},{1,0},{4,5},{5,4},{8,16},{9,17},{12,20},{13,21},{16,8},{17,9... | collective-permute-start | bytes 1572872 | tf_op jit(solution)/shard_map/ppermute | solution.py:281
  61.9 10.3 %collective-permute-start.17 = (bf16[1024,256]{1,0:T(8,128)(2,1)}, bf16[1024,256]{1,0:T(8,128)(2,1)S(1)}, u32[]{:S(2)}, u32[]{:S(2)}) collective-permute-start(bf16[1024,256]{1,0:T(8,128)(2,1)} %collective-permute-done.9.refs_3_.refs_4_), channel_id=1, source_target_pairs={{0,2},{2,0},{1,3},{3,1},{4,6},{6,4},{5,7},{7,5},{8,10},{10,8},{9,1... | collective-permute-start | bytes 1572872 | tf_op jit(solution)/shard_map/ppermute | solution.py:281
  63.5 10.3 %collective-permute-start.15 = (bf16[1024,256]{1,0:T(8,128)(2,1)}, bf16[1024,256]{1,0:T(8,128)(2,1)}, u32[]{:S(2)}, u32[]{:S(2)}) collective-permute-start(bf16[1024,256]{1,0:T(8,128)(2,1)} %collective-permute-done.6.refs_2_), channel_id=1, source_target_pairs={{0,8},{4,12},{8,0},{12,4},{16,24},{20,28},{24,16},{28,20},{1,9},{5... | collective-permute-start | bytes 1572872 | tf_op jit(solution)/shard_map/ppermute | solution.py:281
  66.5 21.6 %collective-permute-start.21 = (bf16[2,256,1024]{2,1,0:T(8,128)(2,1)}, bf16[2,256,1024]{2,1,0:T(8,128)(2,1)S(1)}, u32[]{:S(2)}, u32[]{:S(2)}) collective-permute-start(bf16[2,256,1024]{2,1,0:T(8,128)(2,1)} %shard_map.108.refs_15_.refs_16_.refs_19_.refs_20_), channel_id=1, source_target_pairs={{0,4},{4,0},{8,12},{12,8},{16,20},{20,16},{24,28},{28,24},{1,5},{5... | collective-permute-start | bytes 3145736 | tf_op jit(solution)/shard_map/ppermute | solution.py:281
  73.8 11.3 %collective-permute-start.18 = (bf16[1024,256]{1,0:T(8,128)(2,1)}, bf16[1024,256]{1,0:T(8,128)(2,1)S(1)}, u32[]{:S(2)}, u32[]{:S(2)}) collective-permute-start(bf16[1024,256]{1,0:T(8,128)(2,1)} %collective-permute-done.16.refs_3_), channel_id=1, source_target_pairs={{0,8},{4,12},{8,0},{12,4},{16,24},{20,28},{24,16},{28,20},{1,9},{5... | collective-permute-start | bytes 1572872 | tf_op jit(solution)/shard_map/ppermute | solution.py:281
  75.0 14.1 %collective-permute-start.28 = (bf16[256,1024]{1,0:T(8,128)(2,1)S(1)}, bf16[256,1024]{1,0:T(8,128)(2,1)S(1)}, u32[]{:S(2)}, u32[]{:S(2)}) collective-permute-start(bf16[256,1024]{1,0:T(8,128)(2,1)S(1)} %collective-permute-done.3.refs_17_.refs_21_), channel_id=1, source_target_pairs={{0,1},{1,0},{2,3},{3,2},{4,5},{5,4},{6,7},{7,6},{8,9},{9,8},{10,11... | collective-permute-start | bytes 1572872 | tf_op jit(solution)/shard_map/ppermute | solution.py:281
  75.0 27.0 %collective-permute-start.27 = (bf16[2,256,1024]{2,1,0:T(8,128)(2,1)}, bf16[2,256,1024]{2,1,0:T(8,128)(2,1)}, u32[]{:S(2)}, u32[]{:S(2)}) collective-permute-start(bf16[2,256,1024]{2,1,0:T(8,128)(2,1)} %shard_map.108.refs_15_.refs_16_.refs_19_.refs_20_), channel_id=1, source_target_pairs={{0,1},{1,0},{2,3},{3,2},{4,5},{5,4},{6,7},{7,6},{8,9},{9,8},{10,11... | collective-permute-start | bytes 3145736 | tf_op jit(solution)/shard_map/ppermute | solution.py:281
  75.5 16.7 %collective-permute-start.26 = (bf16[256,1024]{1,0:T(8,128)(2,1)S(1)}, bf16[256,1024]{1,0:T(8,128)(2,1)S(1)}, u32[]{:S(2)}, u32[]{:S(2)}) collective-permute-start(bf16[256,1024]{1,0:T(8,128)(2,1)S(1)} %collective-permute-done.2.refs_14_.refs_18_), channel_id=1, source_target_pairs={{0,1},{1,0},{2,3},{3,2},{4,5},{5,4},{6,7},{7,6},{8,9},{9,8},{10,11... | collective-permute-start | bytes 1572872 | tf_op jit(solution)/shard_map/ppermute | solution.py:281
  85.1 10.3 %collective-permute-start.23 = (bf16[1024,256]{1,0:T(8,128)(2,1)S(1)}, bf16[1024,256]{1,0:T(8,128)(2,1)}, u32[]{:S(2)}, u32[]{:S(2)}) collective-permute-start(bf16[1024,256]{1,0:T(8,128)(2,1)S(1)} %collective-permute-done.13.refs_9_.refs_10_), channel_id=1, source_target_pairs={{0,1},{1,0},{4,5},{5,4},{8,16},{9,17},{12,20},{13,21},{16,8},{17,9... | collective-permute-start | bytes 1572872 | tf_op jit(solution)/shard_map/ppermute | solution.py:281
  88.1 11.5 %collective-permute-start.22 = (bf16[1024,256]{1,0:T(8,128)(2,1)S(1)}, bf16[1024,256]{1,0:T(8,128)(2,1)}, u32[]{:S(2)}, u32[]{:S(2)}) collective-permute-start(bf16[1024,256]{1,0:T(8,128)(2,1)S(1)} %collective-permute-done.13.refs_9_.refs_10_), channel_id=1, source_target_pairs={{0,8},{4,12},{8,0},{12,4},{16,24},{20,28},{24,16},{28,20},{1,9},{5... | collective-permute-start | bytes 1572872 | tf_op jit(solution)/shard_map/ppermute | solution.py:281
  92.2 25.8 %collective-permute-start.19 = (bf16[2,1024,256]{2,1,0:T(8,128)(2,1)}, bf16[2,1024,256]{2,1,0:T(8,128)(2,1)S(1)}, u32[]{:S(2)}, u32[]{:S(2)}) collective-permute-start(bf16[2,1024,256]{2,1,0:T(8,128)(2,1)} %shard_map.106.refs_5_.refs_6_.refs_7_.refs_8_), channel_id=1, source_target_pairs={{0,2},{2,0},{1,3},{3,1},{4,6},{6,4},{5,7},{7,5},{8,10},{10,8},{9,1... | collective-permute-start | bytes 3145736 | tf_op jit(solution)/shard_map/ppermute | solution.py:281
  95.4 24.1 %collective-permute-start.32 = (bf16[2,1024,256]{2,1,0:T(8,128)(2,1)}, bf16[2,1024,256]{2,1,0:T(8,128)(2,1)}, u32[]{:S(2)}, u32[]{:S(2)}) collective-permute-start(bf16[2,1024,256]{2,1,0:T(8,128)(2,1)} %shard_map.106.refs_5_.refs_6_.refs_7_.refs_8_), channel_id=1, source_target_pairs={{0,4},{4,0},{8,12},{12,8},{16,20},{20,16},{24,28},{28,24},{1,5},{5... | collective-permute-start | bytes 3145736 | tf_op jit(solution)/shard_map/ppermute | solution.py:281
  99.6 20.0 %collective-permute-start.31 = (bf16[2,256,1024]{2,1,0:T(8,128)(2,1)S(1)}, bf16[2,256,1024]{2,1,0:T(8,128)(2,1)S(1)}, u32[]{:S(2)}, u32[]{:S(2)}) collective-permute-start(bf16[2,256,1024]{2,1,0:T(8,128)(2,1)S(1)} %collective-permute-done.21.refs_5_.refs_6_.refs_23_.refs_24_), channel_id=1, source_target_pairs={{0,1},{1,0},{2,3},{3,2},{4,5},{5,4},{6,7},{7,6},{8,9},{9,8},{10,11... | collective-permute-start | bytes 3145736 | tf_op jit(solution)/shard_map/ppermute | solution.py:281
  100.2 14.7 %collective-permute-start.24 = (bf16[1024,256]{1,0:T(8,128)(2,1)}, bf16[1024,256]{1,0:T(8,128)(2,1)}, u32[]{:S(2)}, u32[]{:S(2)}) collective-permute-start(bf16[1024,256]{1,0:T(8,128)(2,1)} %collective-permute-done.23.refs_14_), channel_id=1, source_target_pairs={{0,8},{4,12},{8,0},{12,4},{16,24},{20,28},{24,16},{28,20},{1,9},{5... | collective-permute-start | bytes 1572872 | tf_op jit(solution)/shard_map/ppermute | solution.py:281
  101.9 14.4 %collective-permute-start.25 = (bf16[1024,256]{1,0:T(8,128)(2,1)}, bf16[1024,256]{1,0:T(8,128)(2,1)}, u32[]{:S(2)}, u32[]{:S(2)}) collective-permute-start(bf16[1024,256]{1,0:T(8,128)(2,1)} %collective-permute-done.22.refs_11_.refs_12_), channel_id=1, source_target_pairs={{0,1},{1,0},{4,5},{5,4},{8,16},{9,17},{12,20},{13,21},{16,8},{17,9... | collective-permute-start | bytes 1572872 | tf_op jit(solution)/shard_map/ppermute | solution.py:281
  116.3 13.9 %collective-permute-start.30 = (bf16[1024,256]{1,0:T(8,128)(2,1)}, bf16[1024,256]{1,0:T(8,128)(2,1)}, u32[]{:S(2)}, u32[]{:S(2)}) collective-permute-start(bf16[1024,256]{1,0:T(8,128)(2,1)} %collective-permute-done.25.refs_16_), channel_id=1, source_target_pairs={{0,8},{4,12},{8,0},{12,4},{16,24},{20,28},{24,16},{28,20},{1,9},{5... | collective-permute-start | bytes 1572872 | tf_op jit(solution)/shard_map/ppermute | solution.py:281
  118.0 27.1 %collective-permute-start.20 = (bf16[3,128,1024]{2,1,0:T(8,128)(2,1)}, bf16[3,128,1024]{2,1,0:T(8,128)(2,1)}, u32[]{:S(2)}, u32[]{:S(2)}) collective-permute-start(bf16[3,128,1024]{2,1,0:T(8,128)(2,1)} %get-tuple-element.60), channel_id=1, source_target_pairs={{0,2},{2,0},{1,3},{3,1},{4,6},{6,4},{5,7},{7,5},{8,10},{10,8},{9,1... | collective-permute-start | bytes 2359304 | tf_op jit(solution)/shard_map/ppermute | solution.py:281
  (16 other events, 338.2 us)

commit v5 on v4

--- a/solution.py
+++ b/solution.py
@@ -390,8 +390,8 @@
     groups = 2
     heads //= groups
     own_in = [(v, half_of(lambda y: y, groups)) for v in own]
-    grad_2e = send_edge(grad_2m, cg_sent, grad_x, packed)
-    grad_3m = send_middle(grad_1, cg_sent, grad_x, packed)
+    grad_2e = send_edge(grad_2m, cg_sent, grad_x)
+    grad_3m = send_middle(grad_1, cg_sent, grad_x)
     grad_1x = send_x(grad_1, packed)
     cg_peer = send_y(cg_sent)
     group = half // groups
@@ -451,7 +451,7 @@
     received = send_y(sent)
     diagonal_1 = send_edge(diagonal, grad_px)
     diagonal_2m = send_middle(diagonal)
-    diagonal_2e = send_edge(diagonal_2m)
+    diagonal_2e = flipped("dp", 2)(diagonal_2m, near_3e)
     diagonal_3m = send_middle(diagonal_1)
     grad_1c = send_core(grad_1)
     grad_pc = send_core(grad_p)

time: 150 us -> 150 us (level)
  no operation moved by 1% of the time
where the time goes in v5:
time: 150 us; the launch traced here: 147 us
  Pallas kernels  62.4 us (42%)
  waiting for transfers between devices  39.6 us (26%)
  starting transfers between devices  38.8 us (26%)
  local copies, waits for them, and re-layouts  3.6 us (2%)
    pallas_call x10, Pallas kernels, call(): pl.pallas_call(kernel, grid_spec=pltpu.PrefetchScalarGridSpec(num_scalar_...  62.4 us
    ppermute x33, waiting for transfers between devices, send(): arrived.append(lax.ppermute(after(value, others), axis, pairs))  39.6 us
    ppermute x33, starting transfers between devices, send(): arrived.append(lax.ppermute(after(value, others), axis, pairs))  38.8 us
  transfers between devices with their start and end apart: 33, of which 17 were waited for; matrix products, arithmetic and copies ran while one was open for 2% of the time, Pallas kernels for 40%

profile of v5, /device:TPU:8, one launch (start us, length us, event | category | flops | bytes accessed | tf_op | source)
XLA Modules:
  0.0 147.1 jit_solution(507369398159753694)
XLA Ops:
  1.3 2.1 %shard_map.102 = bf16[400,1024]{1,0:T(8,128)(2,1)} custom-call(s32[1]{0:T(128)} %bitcast.place.refs_0_, bf16[1,128,2048]{2,1,0:T(8,128)(2,1)} %refs_1_.5, bf16[1,128,2048]{2,1,0:T(8,128)(2,1)} %refs_2_.5, bf16[1,128,2048]{2,1,0:T(8,128)(2,1)} %refs_3_.3, s32[1,1,2]{2,1,0:T(1,128)} %refs_5_.3, s32[1,1]{1,0:T(1,128)S(6)} %copy.19.count.refs_6_), custom_call_target="tpu_custom_call" | custom-call | bytes 1572864 | tf_op jit(solution)/shard_map/pallas_call | solution.py:54
  3.3 1.5 %collective-permute-start = (bf16[400,1024]{1,0:T(8,128)(2,1)}, bf16[400,1024]{1,0:T(8,128)(2,1)S(1)}, u32[]{:S(2)}, u32[]{:S(2)}) collective-permute-start(bf16[400,1024]{1,0:T(8,128)(2,1)} %shard_map.102), channel_id=1, source_target_pairs={{0,2},{2,0},{1,3},{3,1},{4,6},{6,4},{5,7},{7,5},{8,10},{10,8},{9,1... | collective-permute-start | bytes 2457608 | tf_op jit(solution)/shard_map/ppermute | solution.py:281
  5.9 1.6 %collective-permute-start.3 = (bf16[256,1024]{1,0:T(8,128)(2,1)S(1)}, bf16[256,1024]{1,0:T(8,128)(2,1)S(1)}, u32[]{:S(2)}, u32[]{:S(2)}) collective-permute-start(bf16[256,1024]{1,0:T(8,128)(2,1)S(1)} %dynamic-slice_bitcast_fusion), channel_id=1, source_target_pairs={{0,4},{4,0},{8,12},{12,8},{16,20},{20,16},{24,28},{28,24},{1,5},{5... | collective-permute-start | bytes 1572872 | tf_op jit(solution)/shard_map/ppermute | solution.py:281
  8.0 2.7 %collective-permute-start.4 = (bf16[256,1024]{1,0:T(8,128)(2,1)S(1)}, bf16[256,1024]{1,0:T(8,128)(2,1)S(1)}, u32[]{:S(2)}, u32[]{:S(2)}) collective-permute-start(bf16[256,1024]{1,0:T(8,128)(2,1)S(1)} %dynamic-slice_bitcast_fusion), channel_id=1, source_target_pairs={{0,1},{1,0},{4,5},{5,4},{8,16},{9,17},{12,20},{13,21},{16,8},{17,9... | collective-permute-start | bytes 1572872 | tf_op jit(solution)/shard_map/ppermute | solution.py:281
  10.7 6.8 %shard_map.103 = (bf16[1024,256]{1,0:T(8,128)(2,1)}, bf16[1024,256]{1,0:T(8,128)(2,1)}) custom-call(s32[1]{0:T(128)} %bitcast.place.refs_0_, bf16[1,256,2048]{2,1,0:T(8,128)(2,1)} %refs_25_.1, bf16[2048,2048]{1,0:T(8,128)(2,1)} %refs_2_.3), custom_call_target="tpu_custom_call" | custom-call | flops 2147483648 | bytes 9437184 | tf_op jit(solution)/shard_map/pallas_call | solution.py:54
  17.4 1.9 %collective-permute-done.3.refs_17_.refs_21_ = bf16[256,1024]{1,0:T(8,128)(2,1)S(1)} collective-permute-done((bf16[256,1024]{1,0:T(8,128)(2,1)S(1)}, bf16[256,1024]{1,0:T(8,128)(2,1)S(1)}, u32[]{:S(2)}, u32[]{:S(2)}) %collective-permute-start.3) | collective-permute-done | bytes 524320 | tf_op jit(solution)/shard_map/ppermute | solution.py:281
  20.6 2.9 %collective-permute-done.refs_4_ = bf16[400,1024]{1,0:T(8,128)(2,1)S(1)} collective-permute-done((bf16[400,1024]{1,0:T(8,128)(2,1)}, bf16[400,1024]{1,0:T(8,128)(2,1)S(1)}, u32[]{:S(2)}, u32[]{:S(2)}) %collective-permute-start) | collective-permute-done | bytes 819232 | tf_op jit(solution)/shard_map/ppermute | solution.py:281
  25.0 1.5 %collective-permute-start.1 = (bf16[1024,256]{1,0:T(8,128)(2,1)}, bf16[1024,256]{1,0:T(8,128)(2,1)}, u32[]{:S(2)}, u32[]{:S(2)}) collective-permute-start(bf16[1024,256]{1,0:T(8,128)(2,1)} %get-tuple-element.42), channel_id=1, source_target_pairs={{0,2},{2,0},{1,3},{3,1},{4,6},{6,4},{5,7},{7,5},{8,10},{10,8},{9,1... | collective-permute-start | bytes 1572872 | tf_op jit(solution)/shard_map/ppermute | solution.py:281
  27.0 2.7 %collective-permute-start.5 = (bf16[256,1024]{1,0:T(8,128)(2,1)S(1)}, bf16[256,1024]{1,0:T(8,128)(2,1)}, u32[]{:S(2)}, u32[]{:S(2)}) collective-permute-start(bf16[256,1024]{1,0:T(8,128)(2,1)S(1)} %collective-permute-done.2.refs_14_.refs_18_), channel_id=1, source_target_pairs={{0,1},{1,0},{4,5},{5,4},{8,16},{9,17},{12,20},{13,21},{16,8},{17,9... | collective-permute-start | bytes 1572872 | tf_op jit(solution)/shard_map/ppermute | solution.py:281
  29.7 4.9 %shard_map.105.refs_1_.refs_2_ = bf16[1024,256]{1,0:T(8,128)(2,1)} custom-call(s32[1]{0:T(128)} %bitcast.place.refs_0_, bf16[1,128,2048]{2,1,0:T(8,128)(2,1)} %refs_1_.5, bf16[1,128,2048]{2,1,0:T(8,128)(2,1)} %refs_2_.5, bf16[1,128,2048]{2,1,0:T(8,128)(2,1)} %refs_3_.3, bf16[400,1024]{1,0:T(8,128)(2,1)} %copy-done.3, s32[1,1,2]{2,1,0:T(1,128)} %refs_5_.3, ...), custom_call_target="tpu_custom_call" | custom-call | flops 268435456 | bytes 3145728 | tf_op jit(solution)/shard_map/pallas_call | solution.py:54
  34.7 1.7 %collective-permute-done.7.refs_18_.refs_22_ = bf16[256,1024]{1,0:T(8,128)(2,1)S(1)} collective-permute-done((bf16[256,1024]{1,0:T(8,128)(2,1)S(1)}, bf16[256,1024]{1,0:T(8,128)(2,1)S(1)}, u32[]{:S(2)}, u32[]{:S(2)}) %collective-permute-start.7) | collective-permute-done | bytes 524320 | tf_op jit(solution)/shard_map/ppermute | solution.py:281
  40.0 2.5 %collective-permute-start.6 = (bf16[1024,256]{1,0:T(8,128)(2,1)}, bf16[1024,256]{1,0:T(8,128)(2,1)}, u32[]{:S(2)}, u32[]{:S(2)}) collective-permute-start(bf16[1024,256]{1,0:T(8,128)(2,1)} %shard_map.105.refs_1_.refs_2_), channel_id=1, source_target_pairs={{0,1},{1,0},{4,5},{5,4},{8,16},{9,17},{12,20},{13,21},{16,8},{17,9... | collective-permute-start | bytes 1572872 | tf_op jit(solution)/shard_map/ppermute | solution.py:281
  42.5 6.1 %collective-permute-done.10.refs_9_.refs_10_ = bf16[1024,256]{1,0:T(8,128)(2,1)} collective-permute-done((bf16[1024,256]{1,0:T(8,128)(2,1)}, bf16[1024,256]{1,0:T(8,128)(2,1)}, u32[]{:S(2)}, u32[]{:S(2)}) %collective-permute-start.10) | collective-permute-done | bytes 524320 | tf_op jit(solution)/shard_map/ppermute | solution.py:281
  50.0 1.5 %collective-permute-start.13 = (bf16[1024,256]{1,0:T(8,128)(2,1)}, bf16[1024,256]{1,0:T(8,128)(2,1)S(1)}, u32[]{:S(2)}, u32[]{:S(2)}) collective-permute-start(bf16[1024,256]{1,0:T(8,128)(2,1)} %collective-permute-done.10.refs_9_.refs_10_), channel_id=1, source_target_pairs={{0,2},{2,0},{1,3},{3,1},{4,6},{6,4},{5,7},{7,5},{8,10},{10,8},{9,1... | collective-permute-start | bytes 1572872 | tf_op jit(solution)/shard_map/ppermute | solution.py:281
  52.4 5.9 %shard_map.104 = (bf16[1,128,2048]{2,1,0:T(8,128)(2,1)}, bf16[1,128,2048]{2,1,0:T(8,128)(2,1)}, bf16[1,128,2048]{2,1,0:T(8,128)(2,1)}, bf16[3,128,1024]{2,1,0:T(8,128)(2,1)}) custom-call(s32[1]{0:T(128)} %bitcast.place.refs_0_, bf16[1,128,2048]{2,1,0:T(8,128)(2,1)} %refs_1_.5, bf16[1,128,2048]{2,1,0:T(8,128)(2,1)} %refs_2_.5, bf16[1,128,2048]{2,1,0:T(8,128)(2,1)} %refs_3_.3, ...), custom_call_target="tpu_custom_call" | custom-call | flops 536870912 | bytes 5242880 | tf_op jit(solution)/shard_map/pallas_call | solution.py:54
  58.3 2.8 %collective-permute-start.16 = (bf16[1024,256]{1,0:T(8,128)(2,1)}, bf16[1024,256]{1,0:T(8,128)(2,1)}, u32[]{:S(2)}, u32[]{:S(2)}) collective-permute-start(bf16[1024,256]{1,0:T(8,128)(2,1)} %collective-permute-done.9.refs_3_.refs_4_), channel_id=1, source_target_pairs={{0,1},{1,0},{4,5},{5,4},{8,16},{9,17},{12,20},{13,21},{16,8},{17,9... | collective-permute-start | bytes 1572872 | tf_op jit(solution)/shard_map/ppermute | solution.py:281
  61.9 1.5 %collective-permute-start.17 = (bf16[1024,256]{1,0:T(8,128)(2,1)}, bf16[1024,256]{1,0:T(8,128)(2,1)S(1)}, u32[]{:S(2)}, u32[]{:S(2)}) collective-permute-start(bf16[1024,256]{1,0:T(8,128)(2,1)} %collective-permute-done.9.refs_3_.refs_4_), channel_id=1, source_target_pairs={{0,2},{2,0},{1,3},{3,1},{4,6},{6,4},{5,7},{7,5},{8,10},{10,8},{9,1... | collective-permute-start | bytes 1572872 | tf_op jit(solution)/shard_map/ppermute | solution.py:281
  64.3 2.2 %shard_map.108.refs_15_.refs_16_.refs_19_.refs_20_ = bf16[2,256,1024]{2,1,0:T(8,128)(2,1)} custom-call(s32[1]{0:T(128)} %bitcast.1.place, bf16[256,1024]{1,0:T(8,128)(2,1)} %copy-done.12, bf16[256,1024]{1,0:T(8,128)(2,1)} %copy-done.13, bf16[256,1024]{1,0:T(8,128)(2,1)} %copy-done.11, bf16[256,1024]{1,0:T(8,128)(2,1)} %collective-permute-done.5.refs_3_), custom_call_target="tpu_custom_call" | custom-call | bytes 2097152 | tf_op jit(solution)/shard_map/pallas_call | solution.py:54
  67.1 2.5 %collective-permute-done.16.refs_3_ = bf16[1024,256]{1,0:T(8,128)(2,1)} collective-permute-done((bf16[1024,256]{1,0:T(8,128)(2,1)}, bf16[1024,256]{1,0:T(8,128)(2,1)}, u32[]{:S(2)}, u32[]{:S(2)}) %collective-permute-start.16) | collective-permute-done | bytes 524320 | tf_op jit(solution)/shard_map/ppermute | solution.py:281
  69.7 2.5 %collective-permute-done.17.refs_3_.refs_4_ = bf16[1024,256]{1,0:T(8,128)(2,1)S(1)} collective-permute-done((bf16[1024,256]{1,0:T(8,128)(2,1)}, bf16[1024,256]{1,0:T(8,128)(2,1)S(1)}, u32[]{:S(2)}, u32[]{:S(2)}) %collective-permute-start.17) | collective-permute-done | bytes 524320 | tf_op jit(solution)/shard_map/ppermute | solution.py:281
  72.2 1.6 %collective-permute-done.15.refs_0_ = bf16[1024,256]{1,0:T(8,128)(2,1)} collective-permute-done((bf16[1024,256]{1,0:T(8,128)(2,1)}, bf16[1024,256]{1,0:T(8,128)(2,1)}, u32[]{:S(2)}, u32[]{:S(2)}) %collective-permute-start.15) | collective-permute-done | bytes 524320 | tf_op jit(solution)/shard_map/ppermute | solution.py:281
  75.5 9.6 %collective-permute-done.18.refs_1_ = bf16[1024,256]{1,0:T(8,128)(2,1)S(1)} collective-permute-done((bf16[1024,256]{1,0:T(8,128)(2,1)}, bf16[1024,256]{1,0:T(8,128)(2,1)S(1)}, u32[]{:S(2)}, u32[]{:S(2)}) %collective-permute-start.18) | collective-permute-done | bytes 524320 | tf_op jit(solution)/shard_map/ppermute | solution.py:281
  86.5 1.6 %collective-permute-done.21.refs_5_.refs_6_.refs_23_.refs_24_ = bf16[2,256,1024]{2,1,0:T(8,128)(2,1)S(1)} collective-permute-done((bf16[2,256,1024]{2,1,0:T(8,128)(2,1)}, bf16[2,256,1024]{2,1,0:T(8,128)(2,1)S(1)}, u32[]{:S(2)}, u32[]{:S(2)}) %collective-permute-start.21) | collective-permute-done | bytes 1048608 | tf_op jit(solution)/shard_map/ppermute | solution.py:281
  89.9 2.2 %shard_map.106.refs_5_.refs_6_.refs_7_.refs_8_ = bf16[2,1024,256]{2,1,0:T(8,128)(2,1)} custom-call(s32[1]{0:T(128)} %bitcast.1.place, bf16[1024,256]{1,0:T(8,128)(2,1)} %collective-permute-done.15.refs_0_, bf16[1024,256]{1,0:T(8,128)(2,1)} %copy-done.14, bf16[1024,256]{1,0:T(8,128)(2,1)} %collective-permute-done.6.refs_2_, ...), custom_call_target="tpu_custom_call" | custom-call | bytes 2097152 | tf_op jit(solution)/shard_map/pallas_call | solution.py:54
  92.2 1.6 %collective-permute-start.19 = (bf16[2,1024,256]{2,1,0:T(8,128)(2,1)}, bf16[2,1024,256]{2,1,0:T(8,128)(2,1)S(1)}, u32[]{:S(2)}, u32[]{:S(2)}) collective-permute-start(bf16[2,1024,256]{2,1,0:T(8,128)(2,1)} %shard_map.106.refs_5_.refs_6_.refs_7_.refs_8_), channel_id=1, source_target_pairs={{0,2},{2,0},{1,3},{3,1},{4,6},{6,4},{5,7},{7,5},{8,10},{10,8},{9,1... | collective-permute-start | bytes 3145736 | tf_op jit(solution)/shard_map/ppermute | solution.py:281
  93.7 1.7 %collective-permute-done.23.refs_14_ = bf16[1024,256]{1,0:T(8,128)(2,1)} collective-permute-done((bf16[1024,256]{1,0:T(8,128)(2,1)S(1)}, bf16[1024,256]{1,0:T(8,128)(2,1)}, u32[]{:S(2)}, u32[]{:S(2)}) %collective-permute-start.23) | collective-permute-done | bytes 524320 | tf_op jit(solution)/shard_map/ppermute | solution.py:281
  95.4 2.9 %collective-permute-start.32 = (bf16[2,1024,256]{2,1,0:T(8,128)(2,1)}, bf16[2,1024,256]{2,1,0:T(8,128)(2,1)}, u32[]{:S(2)}, u32[]{:S(2)}) collective-permute-start(bf16[2,1024,256]{2,1,0:T(8,128)(2,1)} %shard_map.106.refs_5_.refs_6_.refs_7_.refs_8_), channel_id=1, source_target_pairs={{0,4},{4,0},{8,12},{12,8},{16,20},{20,16},{24,28},{28,24},{1,5},{5... | collective-permute-start | bytes 3145736 | tf_op jit(solution)/shard_map/ppermute | solution.py:281
  100.2 1.7 %collective-permute-start.24 = (bf16[1024,256]{1,0:T(8,128)(2,1)}, bf16[1024,256]{1,0:T(8,128)(2,1)}, u32[]{:S(2)}, u32[]{:S(2)}) collective-permute-start(bf16[1024,256]{1,0:T(8,128)(2,1)} %collective-permute-done.23.refs_14_), channel_id=1, source_target_pairs={{0,8},{4,12},{8,0},{12,4},{16,24},{20,28},{24,16},{28,20},{1,9},{5... | collective-permute-start | bytes 1572872 | tf_op jit(solution)/shard_map/ppermute | solution.py:281
  103.1 11.7 %shard_map.109.refs_9_ = bf16[1024,2048]{1,0:T(8,128)(2,1)} custom-call(s32[4]{0:T(128)} %add_add_fusion.1.refs_0_, bf16[1024,256]{1,0:T(8,128)(2,1)} %shard_map.105.refs_1_.refs_2_, bf16[1024,256]{1,0:T(8,128)(2,1)} %shard_map.105.refs_1_.refs_2_, bf16[1024,256]{1,0:T(8,128)(2,1)} %collective-permute-done.9.refs_3_.refs_4_, ...), custom_call_target="tpu_custom_call" | custom-call | flops 6442450944 | bytes 17825792 | tf_op jit(solution)/shard_map/pallas_call | solution.py:54
  120.5 9.7 %shard_map.110.refs_33_ = f32[2048,2048]{1,0:T(8,128)} custom-call(s32[4]{0:T(128)} %add_add_fusion.1.refs_0_, bf16[2,1024,256]{2,1,0:T(8,128)(2,1)} %collective-permute-done.32.refs_1_.refs_2_.refs_3_.refs_4_, bf16[2,1024,256]{2,1,0:T(8,128)(2,1)} %collective-permute-done.32.refs_1_.refs_2_.refs_3_.refs_4_, ...), custom_call_target="tpu_custom_call" | custom-call | flops 2147483648 | bytes 11534336 | tf_op jit(solution)/shard_map/pallas_call | solution.py:54
  130.2 14.8 %shard_map.111 = f32[2048,2048]{1,0:T(8,128)} custom-call(s32[4]{0:T(128)} %add_add_fusion.refs_0_, bf16[1024,256]{1,0:T(8,128)(2,1)} %collective-permute-done.12.refs_1_.refs_2_, bf16[1024,256]{1,0:T(8,128)(2,1)} %collective-permute-done.12.refs_1_.refs_2_, bf16[1024,256]{1,0:T(8,128)(2,1)} %copy-done.5, ...), custom_call_target="tpu_custom_call", output_to_operand_aliasing={{}: (33, {})} | custom-call | flops 8589934592 | bytes 20971520 | tf_op jit(solution)/shard_map/pallas_call | solution.py:54
  145.1 2.0 %shard_map.107 = (bf16[1,128,2048]{2,1,0:T(8,128)(2,1)}, bf16[1,128,2048]{2,1,0:T(8,128)(2,1)}, bf16[1,128,2048]{2,1,0:T(8,128)(2,1)}) custom-call(s32[1]{0:T(128)} %bitcast.place.refs_0_, bf16[3,128,1024]{2,1,0:T(8,128)(2,1)} %collective-permute-done.20.received, ...), custom_call_target="tpu_custom_call", output_to_operand_aliasing={{0}: (2, {}), {1}: (3, {}), {2}: (4, {})} | custom-call | bytes 1572864 | tf_op jit(solution)/shard_map/pallas_call | solution.py:54
  (77 shorter events, 26.5 us)
Async XLA Ops:
  3.3 20.2 %collective-permute-start = (bf16[400,1024]{1,0:T(8,128)(2,1)}, bf16[400,1024]{1,0:T(8,128)(2,1)S(1)}, u32[]{:S(2)}, u32[]{:S(2)}) collective-permute-start(bf16[400,1024]{1,0:T(8,128)(2,1)} %shard_map.102), channel_id=1, source_target_pairs={{0,2},{2,0},{1,3},{3,1},{4,6},{6,4},{5,7},{7,5},{8,10},{10,8},{9,1... | collective-permute-start | bytes 2457608 | tf_op jit(solution)/shard_map/ppermute | solution.py:281
  5.9 13.4 %collective-permute-start.3 = (bf16[256,1024]{1,0:T(8,128)(2,1)S(1)}, bf16[256,1024]{1,0:T(8,128)(2,1)S(1)}, u32[]{:S(2)}, u32[]{:S(2)}) collective-permute-start(bf16[256,1024]{1,0:T(8,128)(2,1)S(1)} %dynamic-slice_bitcast_fusion), channel_id=1, source_target_pairs={{0,4},{4,0},{8,12},{12,8},{16,20},{20,16},{24,28},{28,24},{1,5},{5... | collective-permute-start | bytes 1572872 | tf_op jit(solution)/shard_map/ppermute | solution.py:281
  7.5 13.1 %collective-permute-start.2 = (bf16[256,1024]{1,0:T(8,128)(2,1)S(1)}, bf16[256,1024]{1,0:T(8,128)(2,1)S(1)}, u32[]{:S(2)}, u32[]{:S(2)}) collective-permute-start(bf16[256,1024]{1,0:T(8,128)(2,1)S(1)} %dynamic-slice_bitcast_fusion), channel_id=1, source_target_pairs={{0,8},{4,12},{8,0},{12,4},{16,24},{20,28},{24,16},{28,20},{1,9},{5... | collective-permute-start | bytes 1572872 | tf_op jit(solution)/shard_map/ppermute | solution.py:281
  8.0 18.6 %collective-permute-start.4 = (bf16[256,1024]{1,0:T(8,128)(2,1)S(1)}, bf16[256,1024]{1,0:T(8,128)(2,1)S(1)}, u32[]{:S(2)}, u32[]{:S(2)}) collective-permute-start(bf16[256,1024]{1,0:T(8,128)(2,1)S(1)} %dynamic-slice_bitcast_fusion), channel_id=1, source_target_pairs={{0,1},{1,0},{4,5},{5,4},{8,16},{9,17},{12,20},{13,21},{16,8},{17,9... | collective-permute-start | bytes 1572872 | tf_op jit(solution)/shard_map/ppermute | solution.py:281
  23.5 12.8 %collective-permute-start.7 = (bf16[256,1024]{1,0:T(8,128)(2,1)S(1)}, bf16[256,1024]{1,0:T(8,128)(2,1)S(1)}, u32[]{:S(2)}, u32[]{:S(2)}) collective-permute-start(bf16[256,1024]{1,0:T(8,128)(2,1)S(1)} %collective-permute-done.2.refs_14_.refs_18_), channel_id=1, source_target_pairs={{0,4},{4,0},{8,12},{12,8},{16,20},{20,16},{24,28},{28,24},{1,5},{5... | collective-permute-start | bytes 1572872 | tf_op jit(solution)/shard_map/ppermute | solution.py:281
  25.0 12.8 %collective-permute-start.1 = (bf16[1024,256]{1,0:T(8,128)(2,1)}, bf16[1024,256]{1,0:T(8,128)(2,1)}, u32[]{:S(2)}, u32[]{:S(2)}) collective-permute-start(bf16[1024,256]{1,0:T(8,128)(2,1)} %get-tuple-element.42), channel_id=1, source_target_pairs={{0,2},{2,0},{1,3},{3,1},{4,6},{6,4},{5,7},{7,5},{8,10},{10,8},{9,1... | collective-permute-start | bytes 1572872 | tf_op jit(solution)/shard_map/ppermute | solution.py:281
  26.6 12.8 %collective-permute-start.8 = (bf16[256,1024]{1,0:T(8,128)(2,1)S(1)}, bf16[256,1024]{1,0:T(8,128)(2,1)S(1)}, u32[]{:S(2)}, u32[]{:S(2)}) collective-permute-start(bf16[256,1024]{1,0:T(8,128)(2,1)S(1)} %collective-permute-done.4.refs_2_), channel_id=1, source_target_pairs={{0,8},{4,12},{8,0},{12,4},{16,24},{20,28},{24,16},{28,20},{1,9},{5... | collective-permute-start | bytes 1572872 | tf_op jit(solution)/shard_map/ppermute | solution.py:281
  27.0 13.0 %collective-permute-start.5 = (bf16[256,1024]{1,0:T(8,128)(2,1)S(1)}, bf16[256,1024]{1,0:T(8,128)(2,1)}, u32[]{:S(2)}, u32[]{:S(2)}) collective-permute-start(bf16[256,1024]{1,0:T(8,128)(2,1)S(1)} %collective-permute-done.2.refs_14_.refs_18_), channel_id=1, source_target_pairs={{0,1},{1,0},{4,5},{5,4},{8,16},{9,17},{12,20},{13,21},{16,8},{17,9... | collective-permute-start | bytes 1572872 | tf_op jit(solution)/shard_map/ppermute | solution.py:281
  36.3 12.3 %collective-permute-start.10 = (bf16[1024,256]{1,0:T(8,128)(2,1)}, bf16[1024,256]{1,0:T(8,128)(2,1)}, u32[]{:S(2)}, u32[]{:S(2)}) collective-permute-start(bf16[1024,256]{1,0:T(8,128)(2,1)} %shard_map.105.refs_1_.refs_2_), channel_id=1, source_target_pairs={{0,4},{4,0},{8,12},{12,8},{16,20},{20,16},{24,28},{28,24},{1,5},{5... | collective-permute-start | bytes 1572872 | tf_op jit(solution)/shard_map/ppermute | solution.py:281
  37.9 12.1 %collective-permute-start.12 = (bf16[1024,256]{1,0:T(8,128)(2,1)}, bf16[1024,256]{1,0:T(8,128)(2,1)}, u32[]{:S(2)}, u32[]{:S(2)}) collective-permute-start(bf16[1024,256]{1,0:T(8,128)(2,1)} %shard_map.105.refs_1_.refs_2_), channel_id=1, source_target_pairs={{0,2},{2,0},{1,3},{3,1},{4,6},{6,4},{5,7},{7,5},{8,10},{10,8},{9,1... | collective-permute-start | bytes 1572872 | tf_op jit(solution)/shard_map/ppermute | solution.py:281
  39.4 12.1 %collective-permute-start.9 = (bf16[1024,256]{1,0:T(8,128)(2,1)}, bf16[1024,256]{1,0:T(8,128)(2,1)}, u32[]{:S(2)}, u32[]{:S(2)}) collective-permute-start(bf16[1024,256]{1,0:T(8,128)(2,1)} %shard_map.105.refs_1_.refs_2_), channel_id=1, source_target_pairs={{0,8},{4,12},{8,0},{12,4},{16,24},{20,28},{24,16},{28,20},{1,9},{5... | collective-permute-start | bytes 1572872 | tf_op jit(solution)/shard_map/ppermute | solution.py:281
  40.0 18.3 %collective-permute-start.6 = (bf16[1024,256]{1,0:T(8,128)(2,1)}, bf16[1024,256]{1,0:T(8,128)(2,1)}, u32[]{:S(2)}, u32[]{:S(2)}) collective-permute-start(bf16[1024,256]{1,0:T(8,128)(2,1)} %shard_map.105.refs_1_.refs_2_), channel_id=1, source_target_pairs={{0,1},{1,0},{4,5},{5,4},{8,16},{9,17},{12,20},{13,21},{16,8},{17,9... | collective-permute-start | bytes 1572872 | tf_op jit(solution)/shard_map/ppermute | solution.py:281
  50.0 12.0 %collective-permute-start.13 = (bf16[1024,256]{1,0:T(8,128)(2,1)}, bf16[1024,256]{1,0:T(8,128)(2,1)S(1)}, u32[]{:S(2)}, u32[]{:S(2)}) collective-permute-start(bf16[1024,256]{1,0:T(8,128)(2,1)} %collective-permute-done.10.refs_9_.refs_10_), channel_id=1, source_target_pairs={{0,2},{2,0},{1,3},{3,1},{4,6},{6,4},{5,7},{7,5},{8,10},{10,8},{9,1... | collective-permute-start | bytes 1572872 | tf_op jit(solution)/shard_map/ppermute | solution.py:281
  51.5 12.0 %collective-permute-start.11 = (bf16[1024,256]{1,0:T(8,128)(2,1)}, bf16[1024,256]{1,0:T(8,128)(2,1)}, u32[]{:S(2)}, u32[]{:S(2)}) collective-permute-start(bf16[1024,256]{1,0:T(8,128)(2,1)} %collective-permute-done.9.refs_3_.refs_4_), channel_id=1, source_target_pairs={{0,4},{4,0},{8,12},{12,8},{16,20},{20,16},{24,28},{28,24},{1,5},{5... | collective-permute-start | bytes 1572872 | tf_op jit(solution)/shard_map/ppermute | solution.py:281
  51.9 11.6 %collective-permute-start.14 = (bf16[256,1024]{1,0:T(8,128)(2,1)}, bf16[256,1024]{1,0:T(8,128)(2,1)S(1)}, u32[]{:S(2)}, u32[]{:S(2)}) collective-permute-start(bf16[256,1024]{1,0:T(8,128)(2,1)} %collective-permute-done.5.refs_3_), channel_id=1, source_target_pairs={{0,8},{4,12},{8,0},{12,4},{16,24},{20,28},{24,16},{28,20},{1,9},{5... | collective-permute-start | bytes 1572872 | tf_op jit(solution)/shard_map/ppermute | solution.py:281
  58.3 11.4 %collective-permute-start.16 = (bf16[1024,256]{1,0:T(8,128)(2,1)}, bf16[1024,256]{1,0:T(8,128)(2,1)}, u32[]{:S(2)}, u32[]{:S(2)}) collective-permute-start(bf16[1024,256]{1,0:T(8,128)(2,1)} %collective-permute-done.9.refs_3_.refs_4_), channel_id=1, source_target_pairs={{0,1},{1,0},{4,5},{5,4},{8,16},{9,17},{12,20},{13,21},{16,8},{17,9... | collective-permute-start | bytes 1572872 | tf_op jit(solution)/shard_map/ppermute | solution.py:281
  61.9 10.3 %collective-permute-start.17 = (bf16[1024,256]{1,0:T(8,128)(2,1)}, bf16[1024,256]{1,0:T(8,128)(2,1)S(1)}, u32[]{:S(2)}, u32[]{:S(2)}) collective-permute-start(bf16[1024,256]{1,0:T(8,128)(2,1)} %collective-permute-done.9.refs_3_.refs_4_), channel_id=1, source_target_pairs={{0,2},{2,0},{1,3},{3,1},{4,6},{6,4},{5,7},{7,5},{8,10},{10,8},{9,1... | collective-permute-start | bytes 1572872 | tf_op jit(solution)/shard_map/ppermute | solution.py:281
  63.5 10.3 %collective-permute-start.15 = (bf16[1024,256]{1,0:T(8,128)(2,1)}, bf16[1024,256]{1,0:T(8,128)(2,1)}, u32[]{:S(2)}, u32[]{:S(2)}) collective-permute-start(bf16[1024,256]{1,0:T(8,128)(2,1)} %collective-permute-done.6.refs_2_), channel_id=1, source_target_pairs={{0,8},{4,12},{8,0},{12,4},{16,24},{20,28},{24,16},{28,20},{1,9},{5... | collective-permute-start | bytes 1572872 | tf_op jit(solution)/shard_map/ppermute | solution.py:281
  66.5 21.6 %collective-permute-start.21 = (bf16[2,256,1024]{2,1,0:T(8,128)(2,1)}, bf16[2,256,1024]{2,1,0:T(8,128)(2,1)S(1)}, u32[]{:S(2)}, u32[]{:S(2)}) collective-permute-start(bf16[2,256,1024]{2,1,0:T(8,128)(2,1)} %shard_map.108.refs_15_.refs_16_.refs_19_.refs_20_), channel_id=1, source_target_pairs={{0,4},{4,0},{8,12},{12,8},{16,20},{20,16},{24,28},{28,24},{1,5},{5... | collective-permute-start | bytes 3145736 | tf_op jit(solution)/shard_map/ppermute | solution.py:281
  73.8 11.3 %collective-permute-start.18 = (bf16[1024,256]{1,0:T(8,128)(2,1)}, bf16[1024,256]{1,0:T(8,128)(2,1)S(1)}, u32[]{:S(2)}, u32[]{:S(2)}) collective-permute-start(bf16[1024,256]{1,0:T(8,128)(2,1)} %collective-permute-done.16.refs_3_), channel_id=1, source_target_pairs={{0,8},{4,12},{8,0},{12,4},{16,24},{20,28},{24,16},{28,20},{1,9},{5... | collective-permute-start | bytes 1572872 | tf_op jit(solution)/shard_map/ppermute | solution.py:281
  75.0 14.1 %collective-permute-start.28 = (bf16[256,1024]{1,0:T(8,128)(2,1)S(1)}, bf16[256,1024]{1,0:T(8,128)(2,1)S(1)}, u32[]{:S(2)}, u32[]{:S(2)}) collective-permute-start(bf16[256,1024]{1,0:T(8,128)(2,1)S(1)} %collective-permute-done.3.refs_17_.refs_21_), channel_id=1, source_target_pairs={{0,1},{1,0},{2,3},{3,2},{4,5},{5,4},{6,7},{7,6},{8,9},{9,8},{10,11... | collective-permute-start | bytes 1572872 | tf_op jit(solution)/shard_map/ppermute | solution.py:281
  75.0 27.0 %collective-permute-start.27 = (bf16[2,256,1024]{2,1,0:T(8,128)(2,1)}, bf16[2,256,1024]{2,1,0:T(8,128)(2,1)}, u32[]{:S(2)}, u32[]{:S(2)}) collective-permute-start(bf16[2,256,1024]{2,1,0:T(8,128)(2,1)} %shard_map.108.refs_15_.refs_16_.refs_19_.refs_20_), channel_id=1, source_target_pairs={{0,1},{1,0},{2,3},{3,2},{4,5},{5,4},{6,7},{7,6},{8,9},{9,8},{10,11... | collective-permute-start | bytes 3145736 | tf_op jit(solution)/shard_map/ppermute | solution.py:281
  75.5 16.7 %collective-permute-start.26 = (bf16[256,1024]{1,0:T(8,128)(2,1)S(1)}, bf16[256,1024]{1,0:T(8,128)(2,1)S(1)}, u32[]{:S(2)}, u32[]{:S(2)}) collective-permute-start(bf16[256,1024]{1,0:T(8,128)(2,1)S(1)} %collective-permute-done.2.refs_14_.refs_18_), channel_id=1, source_target_pairs={{0,1},{1,0},{2,3},{3,2},{4,5},{5,4},{6,7},{7,6},{8,9},{9,8},{10,11... | collective-permute-start | bytes 1572872 | tf_op jit(solution)/shard_map/ppermute | solution.py:281
  85.1 10.3 %collective-permute-start.23 = (bf16[1024,256]{1,0:T(8,128)(2,1)S(1)}, bf16[1024,256]{1,0:T(8,128)(2,1)}, u32[]{:S(2)}, u32[]{:S(2)}) collective-permute-start(bf16[1024,256]{1,0:T(8,128)(2,1)S(1)} %collective-permute-done.13.refs_9_.refs_10_), channel_id=1, source_target_pairs={{0,1},{1,0},{4,5},{5,4},{8,16},{9,17},{12,20},{13,21},{16,8},{17,9... | collective-permute-start | bytes 1572872 | tf_op jit(solution)/shard_map/ppermute | solution.py:281
  88.1 11.5 %collective-permute-start.22 = (bf16[1024,256]{1,0:T(8,128)(2,1)S(1)}, bf16[1024,256]{1,0:T(8,128)(2,1)}, u32[]{:S(2)}, u32[]{:S(2)}) collective-permute-start(bf16[1024,256]{1,0:T(8,128)(2,1)S(1)} %collective-permute-done.13.refs_9_.refs_10_), channel_id=1, source_target_pairs={{0,8},{4,12},{8,0},{12,4},{16,24},{20,28},{24,16},{28,20},{1,9},{5... | collective-permute-start | bytes 1572872 | tf_op jit(solution)/shard_map/ppermute | solution.py:281
  92.2 25.8 %collective-permute-start.19 = (bf16[2,1024,256]{2,1,0:T(8,128)(2,1)}, bf16[2,1024,256]{2,1,0:T(8,128)(2,1)S(1)}, u32[]{:S(2)}, u32[]{:S(2)}) collective-permute-start(bf16[2,1024,256]{2,1,0:T(8,128)(2,1)} %shard_map.106.refs_5_.refs_6_.refs_7_.refs_8_), channel_id=1, source_target_pairs={{0,2},{2,0},{1,3},{3,1},{4,6},{6,4},{5,7},{7,5},{8,10},{10,8},{9,1... | collective-permute-start | bytes 3145736 | tf_op jit(solution)/shard_map/ppermute | solution.py:281
  95.4 24.1 %collective-permute-start.32 = (bf16[2,1024,256]{2,1,0:T(8,128)(2,1)}, bf16[2,1024,256]{2,1,0:T(8,128)(2,1)}, u32[]{:S(2)}, u32[]{:S(2)}) collective-permute-start(bf16[2,1024,256]{2,1,0:T(8,128)(2,1)} %shard_map.106.refs_5_.refs_6_.refs_7_.refs_8_), channel_id=1, source_target_pairs={{0,4},{4,0},{8,12},{12,8},{16,20},{20,16},{24,28},{28,24},{1,5},{5... | collective-permute-start | bytes 3145736 | tf_op jit(solution)/shard_map/ppermute | solution.py:281
  99.6 20.0 %collective-permute-start.31 = (bf16[2,256,1024]{2,1,0:T(8,128)(2,1)S(1)}, bf16[2,256,1024]{2,1,0:T(8,128)(2,1)S(1)}, u32[]{:S(2)}, u32[]{:S(2)}) collective-permute-start(bf16[2,256,1024]{2,1,0:T(8,128)(2,1)S(1)} %collective-permute-done.21.refs_5_.refs_6_.refs_23_.refs_24_), channel_id=1, source_target_pairs={{0,1},{1,0},{2,3},{3,2},{4,5},{5,4},{6,7},{7,6},{8,9},{9,8},{10,11... | collective-permute-start | bytes 3145736 | tf_op jit(solution)/shard_map/ppermute | solution.py:281
  100.2 30.0 %collective-permute-start.24 = (bf16[1024,256]{1,0:T(8,128)(2,1)}, bf16[1024,256]{1,0:T(8,128)(2,1)}, u32[]{:S(2)}, u32[]{:S(2)}) collective-permute-start(bf16[1024,256]{1,0:T(8,128)(2,1)} %collective-permute-done.23.refs_14_), channel_id=1, source_target_pairs={{0,8},{4,12},{8,0},{12,4},{16,24},{20,28},{24,16},{28,20},{1,9},{5... | collective-permute-start | bytes 1572872 | tf_op jit(solution)/shard_map/ppermute | solution.py:281
  101.9 14.4 %collective-permute-start.25 = (bf16[1024,256]{1,0:T(8,128)(2,1)}, bf16[1024,256]{1,0:T(8,128)(2,1)}, u32[]{:S(2)}, u32[]{:S(2)}) collective-permute-start(bf16[1024,256]{1,0:T(8,128)(2,1)} %collective-permute-done.22.refs_11_.refs_12_), channel_id=1, source_target_pairs={{0,1},{1,0},{4,5},{5,4},{8,16},{9,17},{12,20},{13,21},{16,8},{17,9... | collective-permute-start | bytes 1572872 | tf_op jit(solution)/shard_map/ppermute | solution.py:281
  116.3 13.9 %collective-permute-start.30 = (bf16[1024,256]{1,0:T(8,128)(2,1)}, bf16[1024,256]{1,0:T(8,128)(2,1)}, u32[]{:S(2)}, u32[]{:S(2)}) collective-permute-start(bf16[1024,256]{1,0:T(8,128)(2,1)} %collective-permute-done.25.refs_16_), channel_id=1, source_target_pairs={{0,8},{4,12},{8,0},{12,4},{16,24},{20,28},{24,16},{28,20},{1,9},{5... | collective-permute-start | bytes 1572872 | tf_op jit(solution)/shard_map/ppermute | solution.py:281
  118.0 27.1 %collective-permute-start.20 = (bf16[3,128,1024]{2,1,0:T(8,128)(2,1)}, bf16[3,128,1024]{2,1,0:T(8,128)(2,1)}, u32[]{:S(2)}, u32[]{:S(2)}) collective-permute-start(bf16[3,128,1024]{2,1,0:T(8,128)(2,1)} %get-tuple-element.60), channel_id=1, source_target_pairs={{0,2},{2,0},{1,3},{3,1},{4,6},{6,4},{5,7},{7,5},{8,10},{10,8},{9,1... | collective-permute-start | bytes 2359304 | tf_op jit(solution)/shard_map/ppermute | solution.py:281
  (16 other events, 338.2 us)
